TPU v7x, 1024 devices: a whole 4x8x16 slice. The times are simulated.
1024 devices in a mesh: seq: 128 (over x, z, core), head: 8 (over y).
Axes of the slice: x: 4, y: 8, z: 16, core: 2. Of those that a mesh axis runs over, the one named last changes fastest.
Arguments:
- query: bfloat16 [16384, 2048], P('seq', 'head'), may hold values from -6 to 6
- key: bfloat16 [16384, 2048], P('seq', 'head'), may hold values from -6 to 6
- value: bfloat16 [16384, 2048], P('seq', 'head'), may hold values from -6 to 6
- gain: float32 [2048], P('head'), may hold values from 0.1 to 1.9
- grad_out: bfloat16 [16384, 2048], P('seq', 'head'), may hold values from -48 to 48
Outputs:
- grad_query: float32 [16384, 2048], P('seq', 'head')
- grad_key: float32 [16384, 2048], P('seq', 'head')
- grad_value: float32 [16384, 2048], P('seq', 'head')
All inputs are finite; a program needn't handle non-finite values.
Results may differ from a plain program's by a relative error of at most 0.0003.
Values sent between devices are 32-bit elements; how exact they have to be, the bound alone decides.
No kernel may reach another device: no remote copies, remote signals or barrier semaphores. Data moves between devices by JAX's collectives and lax.ppermute only.
A program may use at most 128 MiB of HBM per device.

v0:
```python
import jax
import jax.numpy as jnp
from jax import lax
from jax.sharding import PartitionSpec as P

HD = 128


def prefix_2(value, axis, join, neutral, backward):
    count, mine = (lax.axis_size(axis), lax.axis_index(axis))
    pieces = lax.all_gather(value, axis)
    if backward:
        pieces = pieces[::-1]
        mine = count - 1 - mine
    so_far = jnp.full_like(value, 0) + jnp.asarray(neutral, value.dtype)

    def step(position, so_far):
        longer = join(so_far, pieces[position])
        return jnp.where(position < mine, longer, so_far)

    return lax.fori_loop(0, count - 1, step, so_far)


def feature(raw):
    wide = raw.astype(jnp.float32)
    return jnp.where(wide > 0, wide + 1.0, jnp.exp(jnp.minimum(wide, 0.0)))


def slope(raw):
    wide = raw.astype(jnp.float32)
    return jnp.where(wide > 0, 1.0, jnp.exp(jnp.minimum(wide, 0.0)))


def product(form, left, right):
    return jnp.einsum(
        form, left, right, precision=lax.Precision.HIGHEST, preferred_element_type=jnp.float32
    )


def norm_grad(output, gain_row, grad_norm):
    inverse = lax.rsqrt(jnp.mean(output * output, axis=-1, keepdims=True) + 1e-06)
    normed = output * inverse
    scaled = gain_row * grad_norm
    return inverse * (scaled - normed * jnp.mean(scaled * normed, axis=-1, keepdims=True))


def combine(earlier, later):
    return earlier + later


def body(query, key, value, gain, grad_out):
    tok_rows = query.shape[0]
    heads_here = query.shape[1] // HD

    def split(array):
        return array.reshape(tok_rows, heads_here, HD)

    def joined(array):
        return array.reshape(tok_rows, heads_here * HD)

    query_raw = split(query)
    key_raw = split(key)
    value_wide = split(value).astype(jnp.float32)
    grad_wide = split(grad_out).astype(jnp.float32)
    gain_row = gain.reshape(heads_here, HD)
    causal_mask = jnp.tril(jnp.ones((tok_rows, tok_rows), jnp.float32))
    zero_state = jnp.zeros((heads_here, HD, HD), jnp.float32)
    query_feat = feature(query_raw)
    key_feat = feature(key_raw)
    local_kv = product("shi,shj->hij", key_feat, value_wide)
    prefix = prefix_2(local_kv, "seq", combine, zero_state, False)
    scores = product("thi,shi->hts", query_feat, key_feat) * causal_mask
    output = product("hts,shj->thj", scores, value_wide) + product(
        "thi,hij->thj", query_feat, prefix
    )
    grad_o = norm_grad(output, gain_row, grad_wide)
    local_qg = product("thi,thj->hij", query_feat, grad_o)
    suffix = prefix_2(local_qg, "seq", combine, zero_state, True)
    grad_scores = product("thj,shj->hts", grad_o, value_wide) * causal_mask
    grad_q = slope(query_raw) * (
        product("hts,shi->thi", grad_scores, key_feat) + product("thj,hij->thi", grad_o, prefix)
    )
    grad_k = slope(key_raw) * (
        product("hts,thi->shi", grad_scores, query_feat)
        + product("shj,hij->shi", value_wide, suffix)
    )
    grad_v = product("hts,thj->shj", scores, grad_o) + product("shi,hij->shj", key_feat, suffix)
    return (joined(grad_q), joined(grad_k), joined(grad_v))


def solution(mesh):
    placed = (P("seq", "head"), P("seq", "head"), P("seq", "head"), P("head"), P("seq", "head"))
    return jax.shard_map(
        body,
        mesh=mesh,
        in_specs=placed,
        out_specs=(P("seq", "head"), P("seq", "head"), P("seq", "head")),
        check_vma=False,
    )
```

profile of v0, /device:TPU:1, one launch (start us, length us, event | category | flops | bytes accessed | tf_op | source)
XLA Modules:
  0.0 618.6 jit_solution(7573750882929308322)
XLA Ops:
  11.5 175.8 %all-gather.5.cloned.1.call-done = f32[256,128,128]{2,1,0:T(8,128)} async-done(((f32[2,128,128]{2,1,0:T(8,128)}), f32[256,128,128]{2,1,0:T(8,128)}) %all-gather.5.cloned.1.call-update) | async-done | bytes 16777232 | tf_op jit(solution)/shard_map/all_gather | solution.py:11
  187.3 123.6 %while.28 = (s32[]{:T(128)}, f32[2,128,128]{2,1,0:T(8,128)S(1)}, s32[]{:T(128)}, f32[128,2,128,128]{3,2,1,0:T(8,128)}, s32[]{:T(128)}, /*index=5*/s32[]{:T(128)}) while((s32[]{:T(128)}, f32[2,128,128]{2,1,0:T(8,128)S(1)}, s32[]{:T(128)}, f32[128,2,128,128]{3,2,1,0:T(8,128)}, s32[]{:T(128)}, /*index=5*/s32[]{:T(128)}) %tuple.79), condition=%wide.region_1.2_spmd.clone, body=%wide.region_0.1_spmd.clone.sunk | while | flops 98308 | bytes 393317 | solution.py:21
  188.2 0.9 add_select_fusion.4
  189.2 0.9 add_select_fusion.4
  190.2 0.9 add_select_fusion.4
  191.2 0.9 add_select_fusion.4
  192.1 0.9 add_select_fusion.4
  193.1 0.9 add_select_fusion.4
  194.1 0.9 add_select_fusion.4
  195.1 0.9 add_select_fusion.4
  196.0 0.9 add_select_fusion.4
  197.0 0.9 add_select_fusion.4
  198.0 0.9 add_select_fusion.4
  198.9 0.9 add_select_fusion.4
  199.9 0.9 add_select_fusion.4
  200.9 0.9 add_select_fusion.4
  201.9 0.9 add_select_fusion.4
  202.8 0.9 add_select_fusion.4
  203.8 0.9 add_select_fusion.4
  204.8 0.9 add_select_fusion.4
  205.8 0.9 add_select_fusion.4
  206.7 0.9 add_select_fusion.4
  207.7 0.9 add_select_fusion.4
  208.7 0.9 add_select_fusion.4
  209.7 0.9 add_select_fusion.4
  210.6 0.9 add_select_fusion.4
  211.6 0.9 add_select_fusion.4
  212.6 0.9 add_select_fusion.4
  213.5 0.9 add_select_fusion.4
  214.5 0.9 add_select_fusion.4
  215.5 0.9 add_select_fusion.4
  216.5 0.9 add_select_fusion.4
  217.4 0.9 add_select_fusion.4
  218.4 0.9 add_select_fusion.4
  219.4 0.9 add_select_fusion.4
  220.4 0.9 add_select_fusion.4
  221.3 0.9 add_select_fusion.4
  222.3 0.9 add_select_fusion.4
  223.3 0.9 add_select_fusion.4
  224.2 0.9 add_select_fusion.4
  225.2 0.9 add_select_fusion.4
  226.2 0.9 add_select_fusion.4
  227.2 0.9 add_select_fusion.4
  228.1 0.9 add_select_fusion.4
  229.1 0.9 add_select_fusion.4
  230.1 0.9 add_select_fusion.4
  231.1 0.9 add_select_fusion.4
  232.0 0.9 add_select_fusion.4
  233.0 0.9 add_select_fusion.4
  234.0 0.9 add_select_fusion.4
  235.0 0.9 add_select_fusion.4
  235.9 0.9 add_select_fusion.4
  236.9 0.9 add_select_fusion.4
  237.9 0.9 add_select_fusion.4
  238.8 0.9 add_select_fusion.4
  239.8 0.9 add_select_fusion.4
  240.8 0.9 add_select_fusion.4
  241.8 0.9 add_select_fusion.4
  242.7 0.9 add_select_fusion.4
  243.7 0.9 add_select_fusion.4
  313.1 1.0 fusion.28
  316.7 157.6 %all-gather.7.cloned.1.call-done = f32[256,128,128]{2,1,0:T(8,128)} async-done(((f32[2,128,128]{2,1,0:T(8,128)}), f32[256,128,128]{2,1,0:T(8,128)}) %all-gather.7.cloned.1.call-update) | async-done | bytes 16777232 | tf_op jit(solution)/shard_map/all_gather | solution.py:11
  474.3 11.6 %rev.3 = f32[128,2,128,128]{3,2,1,0:T(8,128)} reverse(f32[128,2,128,128]{3,2,1,0:T(8,128)} %bitcast.86), dimensions={0} | reverse | bytes 33554432 | tf_op jit(solution)/shard_map/rev | solution.py:13
  485.9 123.6 %while.29 = (s32[]{:T(128)}, f32[2,128,128]{2,1,0:T(8,128)S(1)}, s32[]{:T(128)}, f32[128,2,128,128]{3,2,1,0:T(8,128)}, s32[]{:T(128)}, /*index=5*/s32[]{:T(128)}) while((s32[]{:T(128)}, f32[2,128,128]{2,1,0:T(8,128)S(1)}, s32[]{:T(128)}, f32[128,2,128,128]{3,2,1,0:T(8,128)}, s32[]{:T(128)}, /*index=5*/s32[]{:T(128)}) %tuple.72), condition=%wide.region_5.6_spmd.clone, body=%wide.region_4.5_spmd.clone.sunk | while | flops 98308 | bytes 393317 | solution.py:21
  (230 shorter events, 197.3 us)
Async XLA Ops:
  7.2 1.0 copy-start
  7.2 180.1 %all-gather.5.cloned.1.call-start = ((), (), s32[]{:S(2)}) async-start(), calls=%async_computation | async-start | bytes 16908288 | tf_op jit(solution)/shard_map/all_gather | solution.py:11
  9.1 465.2 %all-gather.7.cloned.1.call-start = ((), (), s32[]{:S(2)}) async-start(), calls=%async_computation.1 | async-start | bytes 16908288 | tf_op jit(solution)/shard_map/all_gather | solution.py:11
Sparse Core Ops, SparseCore 0:
  12.9 174.3 all-gather.4
  314.3 159.9 all-gather.6
where the time goes:
time: 623 us; the launch traced here: 619 us
  waiting for transfers between devices  333 us (53%)
  other arithmetic  245 us (39%)
  local copies, waits for them, and re-layouts  15.2 us (2%)
  between operations  14.2 us (2%)
    all_gather x2, waiting for transfers between devices, prefix_2(): pieces = lax.all_gather(value, axis)  333 us
    select_n x254, other arithmetic, step(): return jnp.where(position < mine, longer, so_far)  241 us
  transfers between devices with their start and end apart: 2, of which 2 were waited for; matrix products, arithmetic and copies ran while one was open for 1% of the time, Pallas kernels for 0%

commit v1 on v0

v1 whole, which is shorter than its diff:
```python
import functools

import jax
import jax.numpy as jnp
from jax import lax
from jax.experimental import pallas as pl
from jax.experimental.pallas import tpu as pltpu
from jax.sharding import Mesh, PartitionSpec as P

HD = 128
F32 = jnp.float32
BF16 = jnp.bfloat16
VMEM = pl.BlockSpec(memory_space=pltpu.VMEM)
SMEM = pl.BlockSpec(memory_space=pltpu.SMEM)
NN = (((1,), (0,)), ((), ()))
NT = (((1,), (1,)), ((), ()))
TN = (((0,), (0,)), ((), ()))


def halves(wide):
    high = wide.astype(BF16)
    low = (wide - high.astype(F32)).astype(BF16)
    return high, low


def one(left, right, dims):
    return lax.dot_general(left, right, dims, preferred_element_type=F32)


def product(left, right, dims):
    if not isinstance(left, tuple):
        return one(left, right[0], dims) + one(left, right[1], dims)
    if not isinstance(right, tuple):
        return one(left[0], right, dims) + one(left[1], right, dims)
    return one(left[0], right[0], dims) + (one(left[0], right[1], dims) + one(left[1], right[0], dims))


def feature(raw):
    wide = raw.astype(F32)
    return jnp.where(wide > 0, wide + 1.0, jnp.exp(jnp.minimum(wide, 0.0)))


def slope(raw):
    wide = raw.astype(F32)
    return jnp.where(wide > 0, 1.0, jnp.exp(jnp.minimum(wide, 0.0)))


def causal(size):
    row = lax.broadcasted_iota(jnp.int32, (size, size), 0)
    column = lax.broadcasted_iota(jnp.int32, (size, size), 1)
    return row >= column


def columns(index):
    return pl.ds(pl.multiple_of(index * HD, HD), HD)


def pack_kernel(core_ref, q_ref, k_ref, v_ref, g_ref, out_ref):
    other = 1 - core_ref[0]
    for place, ref in enumerate((q_ref, k_ref, v_ref, g_ref)):
        out_ref[place] = ref[:, columns(other)].astype(F32)


def local_kernel(core_ref, q_ref, k_ref, v_ref, g_ref, got_ref, qo_ref, ko_ref, vo_ref, go_ref, state_ref):
    core = core_ref[0]
    other = 1 - core
    pairs = ((q_ref, qo_ref), (k_ref, ko_ref), (v_ref, vo_ref), (g_ref, go_ref))
    for place, (ref, out_ref) in enumerate(pairs):
        out_ref[columns(core), :] = ref[:, columns(core)]
        out_ref[columns(other), :] = got_ref[other, place].astype(BF16)
    state_ref[...] = product(halves(feature(ko_ref[...])), vo_ref[...], TN)


def prefix_kernel(rows, backward, pieces_ref, out_ref):
    size = pieces_ref.shape[0]
    row = lax.broadcasted_iota(jnp.int32, (size, size), 0)
    column = lax.broadcasted_iota(jnp.int32, (size, size), 1)
    same = lax.rem(row, rows) == lax.rem(column, rows)
    apart = row - column if not backward else column - row
    taken = jnp.where(same & (apart > 0), 1.0, 0.0).astype(BF16)
    out_ref[...] = product(taken, halves(pieces_ref[...]), NN)


def forward_kernel(q_ref, k_ref, v_ref, g_ref, gain_ref, prefix_ref, scores_ref, grad_ref, state_ref):
    size = q_ref.shape[0]
    query = halves(feature(q_ref[...]))
    key = halves(feature(k_ref[...]))
    scores = jnp.where(causal(size), product(query, key, NT), 0.0)
    scores_ref[...] = scores
    output = product(halves(scores), v_ref[...], NN) + product(query, halves(prefix_ref[...]), NN)
    inverse = lax.rsqrt(jnp.mean(output * output, axis=-1, keepdims=True) + 1e-06)
    normed = output * inverse
    scaled = gain_ref[...] * g_ref[...].astype(F32)
    grad = inverse * (scaled - normed * jnp.mean(scaled * normed, axis=-1, keepdims=True))
    grad_ref[...] = grad
    state_ref[...] = product(query, halves(grad), TN)


def inner_kernel(q_ref, k_ref, v_ref, scores_ref, grad_ref, prefix_ref, dq_ref, dk_ref, dv_ref):
    size = q_ref.shape[0]
    query = halves(feature(q_ref[...]))
    key = halves(feature(k_ref[...]))
    grad = halves(grad_ref[...])
    grad_scores = halves(jnp.where(causal(size), product(grad, v_ref[...], NT), 0.0))
    dq = product(grad_scores, key, NN) + product(grad, halves(prefix_ref[...]), NT)
    dq_ref[...] = slope(q_ref[...]) * dq
    dk_ref[...] = product(grad_scores, query, TN)
    dv_ref[...] = product(halves(scores_ref[...]), grad, TN)


def backward_kernel(core_ref, k_ref, v_ref, dq_ref, dk_ref, dv_ref, suffix_ref, own_ref, send_ref):
    core = core_ref[0]
    suffix = halves(suffix_ref[...])

    def finish(index, out_ref):
        rows = columns(index)
        raw = k_ref[rows, :]
        out_ref[0] = dq_ref[rows, :]
        out_ref[1] = slope(raw) * (dk_ref[rows, :] + product(v_ref[rows, :], suffix, NT))
        out_ref[2] = dv_ref[rows, :] + product(halves(feature(raw)), suffix, NN)

    finish(core, own_ref)
    finish(1 - core, send_ref)


def place_kernel(core_ref, own_ref, got_ref, dq_ref, dk_ref, dv_ref):
    core = core_ref[0]
    other = 1 - core
    for place, ref in enumerate((dq_ref, dk_ref, dv_ref)):
        ref[:, columns(core)] = own_ref[place]
        ref[:, columns(other)] = got_ref[other, place]


def call(kernel, outs, *operands, scalars=0):
    return pl.pallas_call(
        kernel,
        out_shape=[jax.ShapeDtypeStruct(shape, dtype) for shape, dtype in outs],
        in_specs=[SMEM] * scalars + [VMEM] * (len(operands) - scalars),
        out_specs=[VMEM] * len(outs),
    )(*operands)


def scan_chips(state, backward):
    chips = lax.axis_size("x") * lax.axis_size("z")
    rows = HD // chips
    pieces = lax.all_to_all(state.reshape(chips, rows, HD), ("x", "z"), 0, 0)
    kernel = functools.partial(prefix_kernel, rows, backward)
    (sums,) = call(kernel, [((HD, HD), F32)], pieces.reshape(HD, HD))
    return lax.all_to_all(sums.reshape(chips, rows, HD), ("x", "z"), 0, 0).reshape(HD, HD)


def body(query, key, value, gain, grad_out):
    tokens = query.shape[0]
    core = lax.axis_index("c")
    at = core.reshape(1)
    gain_row = lax.dynamic_slice(gain, (core * HD,), (HD,)).reshape(1, HD)
    (sent,) = call(pack_kernel, [((4, tokens, HD), F32)], at, query, key, value, grad_out, scalars=1)
    got = lax.all_gather(sent, "c")
    pair = (2 * tokens, HD)
    q, k, v, g, state = call(
        local_kernel,
        [(pair, BF16)] * 4 + [((HD, HD), F32)],
        at, query, key, value, grad_out, got,
        scalars=1,
    )
    prefix = scan_chips(state, False)
    scores, grad, state = call(
        forward_kernel,
        [((2 * tokens, 2 * tokens), F32), (pair, F32), ((HD, HD), F32)],
        q, k, v, g, gain_row, prefix,
    )
    suffix = scan_chips(state, True)
    dq, dk, dv = call(inner_kernel, [(pair, F32)] * 3, q, k, v, scores, grad, prefix)
    own, send = call(backward_kernel, [((3, tokens, HD), F32)] * 2, at, k, v, dq, dk, dv, suffix, scalars=1)
    got = lax.all_gather(send, "c")
    return tuple(call(place_kernel, [((tokens, 2 * HD), F32)] * 3, at, own, got, scalars=1))


def over(devices):
    mesh = Mesh(devices, ("x", "z", "c", "h"))
    placed = P(("x", "z", "c"), "h")
    return jax.shard_map(
        body,
        mesh=mesh,
        in_specs=(placed, placed, placed, P("h"), placed),
        out_specs=(placed, placed, placed),
        check_vma=False,
    )


def solution(mesh):
    seq, head = mesh.devices.shape
    return over(mesh.devices.reshape(4, seq // 8, 2, head))
```

time: 623 us -> 123 us (0.20)
  waiting for transfers between devices: 333 us -> 23.9 us
  other arithmetic: 245 us -> 0 us
  blocking collectives: 0 us -> 69.9 us
  Pallas kernels: 0 us -> 16.1 us
  between operations: 14.2 us -> 0.68 us
  local copies, waits for them, and re-layouts: 15.2 us -> 1.84 us
  starting transfers between devices: 0.08 us -> 10 us
    all_gather x2 -> x0, waiting for transfers between devices: 333 us -> none  [prefix_2(): pieces = lax.all_gather(value, axis)]
    select_n x257 -> x0, other arithmetic: 243 us -> none  [the longest x254 241 us: step(): return jnp.where(position < mine, longer, so_far)]
    all_to_all x0 -> x2, blocking collectives: none -> 41.8 us  [scan_chips(): pieces = lax.all_to_all(state.reshape(chips, rows, HD), ('x', 'z'), 0, 0)]
    all_gather x0 -> x2, blocking collectives: none -> 28.1 us  [the longest x1 19.1 us: body(): got = lax.all_gather(sent, 'c')]
    all_to_all x0 -> x2, waiting for transfers between devices: none -> 23.9 us  [scan_chips(): lax.all_to_all(sums.reshape(chips, rows, HD), ('x', 'z'), 0, 0)]
    pallas_call x0 -> x8, Pallas kernels: none -> 16.1 us  [call(): pl.pallas_call(kernel, out_shape=[jax.ShapeDtypeStruct(shape, dtype) for...]
    rev x1 -> x0, local copies, waits for them, and re-layouts: 11.6 us -> none  [prefix_2(): pieces = pieces[::-1]]
    all_to_all x0 -> x2, starting transfers between devices: none -> 10 us  [scan_chips(): lax.all_to_all(sums.reshape(chips, rows, HD), ('x', 'z'), 0, 0)]
  transfers between devices with their start and end apart: 2 -> 2, of which waited for: 2 -> 2; matrix products, arithmetic and copies ran while one was open for 1% -> 0% of each run, Pallas kernels for 0% -> 2%
where the time goes in v1:
time: 123 us; the launch traced here: 122 us
  blocking collectives  69.9 us (57%)
  waiting for transfers between devices  23.9 us (19%)
  Pallas kernels  16.1 us (13%)
  starting transfers between devices  10 us (8%)
  local copies, waits for them, and re-layouts  1.84 us (1%)
    all_to_all x2, blocking collectives, scan_chips(): pieces = lax.all_to_all(state.reshape(chips, rows, HD), ('x', 'z'), 0, 0)  41.8 us
    all_to_all x2, waiting for transfers between devices, scan_chips(): lax.all_to_all(sums.reshape(chips, rows, HD), ('x', 'z'), 0, 0)  23.9 us
    all_gather x1, blocking collectives, body(): got = lax.all_gather(sent, 'c')  19.1 us
    pallas_call x8, Pallas kernels, call(): pl.pallas_call(kernel, out_shape=[jax.ShapeDtypeStruct(shape, dtype) for...  16.1 us
    all_to_all x2, starting transfers between devices, scan_chips(): lax.all_to_all(sums.reshape(chips, rows, HD), ('x', 'z'), 0, 0)  10 us
    all_gather x1, blocking collectives, body(): got = lax.all_gather(send, 'c')  8.97 us
  transfers between devices with their start and end apart: 2, of which 2 were waited for; matrix products, arithmetic and copies ran while one was open for 0% of the time, Pallas kernels for 2%

profile of v1, /device:TPU:1, one launch (start us, length us, event | category | flops | bytes accessed | tf_op | source)
XLA Modules:
  0.0 122.4 jit_solution(5798643227284903908)
XLA Ops:
  0.6 0.0 copy-start
  0.6 1.6 %shard_map.76 = f32[4,128,128]{2,1,0:T(8,128)} custom-call(s32[1]{0:T(128)} %bitcast.core_ref, bf16[128,256]{1,0:T(8,128)(2,1)} %q_ref.3, bf16[128,256]{1,0:T(8,128)(2,1)} %k_ref.3, bf16[128,256]{1,0:T(8,128)(2,1)} %v_ref.3, bf16[128,256]{1,0:T(8,128)(2,1)} %g_ref.3), custom_call_target="tpu_custom_call" | custom-call | tf_op jit(solution)/shard_map/pallas_call | solution.py:135
  2.3 19.1 %all-gather = f32[8,128,128]{2,1,0:T(8,128)} all-gather(f32[4,128,128]{2,1,0:T(8,128)} %shard_map.76), channel_id=2, replica_groups=mesh['x'=4,'z'=16,'c'=2,'h'=8] {'c'}, dimensions={0}, use_global_device_ids=true | all-gather | bytes 786432 | tf_op jit(solution)/shard_map/all_gather | solution.py:158
  21.4 2.1 %shard_map.77 = (bf16[256,128]{1,0:T(8,128)(2,1)}, bf16[256,128]{1,0:T(8,128)(2,1)}, bf16[256,128]{1,0:T(8,128)(2,1)}, bf16[256,128]{1,0:T(8,128)(2,1)}, f32[128,128]{1,0:T(8,128)}) custom-call(s32[1]{0:T(128)} %bitcast.core_ref, bf16[128,256]{1,0:T(8,128)(2,1)} %q_ref.3, bf16[128,256]{1,0:T(8,128)(2,1)} %k_ref.3, bf16[128,256]{1,0:T(8,128)(2,1)} %v_ref.3, ...), custom_call_target="tpu_custom_call" | custom-call | tf_op jit(solution)/shard_map/pallas_call | solution.py:135
  23.5 22.9 %all_to_all.20 = f32[64,2,128]{2,1,0:T(2,128)} all-to-all(f32[64,2,128]{2,1,0:T(2,128)} %bitcast.22), channel_id=1, replica_groups=mesh['x'=4,'z'=16,'c'=2,'h'=8] {'x','z'}, dimensions={0} | all-to-all | bytes 131072 | tf_op jit(solution)/shard_map/all_to_all | solution.py:146
  46.4 1.6 %shard_map.78 = f32[128,128]{1,0:T(8,128)} custom-call(f32[128,128]{1,0:T(8,128)} %bitcast.19), custom_call_target="tpu_custom_call" | custom-call | tf_op jit(solution)/shard_map/pallas_call | solution.py:135
  48.1 5.4 %all-to-all-start.1 = ((f32[64,2,128]{2,1,0:T(2,128)}), f32[64,2,128]{2,1,0:T(2,128)S(1)}, u32[]{:S(2)}, u32[]{:S(2)}) async-start(f32[64,2,128]{2,1,0:T(2,128)} %bitcast.17), calls=%async_computation.1 | async-start | bytes 131072 | tf_op jit(solution)/shard_map/all_to_all | solution.py:149
  53.5 0.0 copy-done
  53.5 0.6 dynamic-slice_bitcast_fusion.gain_ref
  54.1 12.9 %all-to-all-done.1 = f32[64,2,128]{2,1,0:T(2,128)S(1)} async-done(((f32[64,2,128]{2,1,0:T(2,128)}), f32[64,2,128]{2,1,0:T(2,128)S(1)}, u32[]{:S(2)}, u32[]{:S(2)}) %all-to-all-start.1) | async-done | bytes 65568 | tf_op jit(solution)/shard_map/all_to_all | solution.py:149
  67.0 0.0 copy-start.1
  67.0 0.6 copy-done.1
  67.6 2.6 %shard_map.79 = (f32[256,256]{1,0:T(8,128)}, f32[256,128]{1,0:T(8,128)}, f32[128,128]{1,0:T(8,128)}) custom-call(bf16[256,128]{1,0:T(8,128)(2,1)} %get-tuple-element.18.q_ref, bf16[256,128]{1,0:T(8,128)(2,1)} %get-tuple-element.16.k_ref, bf16[256,128]{1,0:T(8,128)(2,1)} %get-tuple-element.17.v_ref, bf16[256,128]{1,0:T(8,128)(2,1)} %get-tuple-element.19.g_ref, ...), custom_call_target="tpu_custom_call" | custom-call | tf_op jit(solution)/shard_map/pallas_call | solution.py:135
  70.3 18.9 %all_to_all.21 = f32[64,2,128]{2,1,0:T(2,128)} all-to-all(f32[64,2,128]{2,1,0:T(2,128)} %bitcast.23), channel_id=1, replica_groups=mesh['x'=4,'z'=16,'c'=2,'h'=8] {'x','z'}, dimensions={0} | all-to-all | bytes 131072 | tf_op jit(solution)/shard_map/all_to_all | solution.py:146
  89.2 1.6 %shard_map.81 = f32[128,128]{1,0:T(8,128)} custom-call(f32[128,128]{1,0:T(8,128)} %bitcast.20), custom_call_target="tpu_custom_call" | custom-call | tf_op jit(solution)/shard_map/pallas_call | solution.py:135
  90.8 4.6 %all-to-all-start.3 = ((f32[64,2,128]{2,1,0:T(2,128)}), f32[64,2,128]{2,1,0:T(2,128)S(1)}, u32[]{:S(2)}, u32[]{:S(2)}) async-start(f32[64,2,128]{2,1,0:T(2,128)} %bitcast.18), calls=%async_computation.3 | async-start | bytes 131072 | tf_op jit(solution)/shard_map/all_to_all | solution.py:149
  95.4 2.5 %shard_map.80 = (f32[256,128]{1,0:T(8,128)}, f32[256,128]{1,0:T(8,128)}, f32[256,128]{1,0:T(8,128)}) custom-call(bf16[256,128]{1,0:T(8,128)(2,1)} %get-tuple-element.18.q_ref, bf16[256,128]{1,0:T(8,128)(2,1)} %get-tuple-element.16.k_ref, bf16[256,128]{1,0:T(8,128)(2,1)} %get-tuple-element.17.v_ref, f32[256,256]{1,0:T(8,128)} %get-tuple-element.21.scores_ref, ...), custom_call_target="tpu_custom_call" | custom-call | tf_op jit(solution)/shard_map/pallas_call | solution.py:135
  97.9 11.0 %all-to-all-done.3 = f32[64,2,128]{2,1,0:T(2,128)S(1)} async-done(((f32[64,2,128]{2,1,0:T(2,128)}), f32[64,2,128]{2,1,0:T(2,128)S(1)}, u32[]{:S(2)}, u32[]{:S(2)}) %all-to-all-start.3) | async-done | bytes 65568 | tf_op jit(solution)/shard_map/all_to_all | solution.py:149
  108.9 0.0 copy-start.2
  108.9 0.6 copy-done.2
  109.5 2.1 %shard_map.82 = (f32[3,128,128]{2,1,0:T(8,128)}, f32[3,128,128]{2,1,0:T(8,128)}) custom-call(s32[1]{0:T(128)} %bitcast.core_ref, bf16[256,128]{1,0:T(8,128)(2,1)} %get-tuple-element.16.k_ref, bf16[256,128]{1,0:T(8,128)(2,1)} %get-tuple-element.17.v_ref, f32[256,128]{1,0:T(8,128)} %get-tuple-element.23.dq_ref, f32[256,128]{1,0:T(8,128)} %get-tuple-element.24.dk_ref, ...), custom_call_target="tpu_custom_call" | custom-call | tf_op jit(solution)/shard_map/pallas_call | solution.py:135
  111.6 9.0 %all-gather.1 = f32[6,128,128]{2,1,0:T(8,128)} all-gather(f32[3,128,128]{2,1,0:T(8,128)} %get-tuple-element.28), channel_id=3, replica_groups=mesh['x'=4,'z'=16,'c'=2,'h'=8] {'c'}, dimensions={0}, use_global_device_ids=true | all-gather | bytes 589824 | tf_op jit(solution)/shard_map/all_gather | solution.py:175
  120.6 1.9 %shard_map.83 = (f32[128,256]{1,0:T(8,128)}, f32[128,256]{1,0:T(8,128)}, f32[128,256]{1,0:T(8,128)}) custom-call(s32[1]{0:T(128)} %bitcast.core_ref, f32[3,128,128]{2,1,0:T(8,128)} %get-tuple-element.27.own_ref, f32[2,3,128,128]{3,2,1,0:T(8,128)} %bitcast.14), custom_call_target="tpu_custom_call" | custom-call | tf_op jit(solution)/shard_map/pallas_call | solution.py:135
Async XLA Ops:
  0.6 52.9 %copy-start = (f32[256]{0:T(256)S(1)}, f32[256]{0:T(256)}, u32[]{:S(2)}) copy-start(f32[256]{0:T(256)} %param.8) | copy-start | bytes 3076
  48.1 18.9 %all-to-all-start.1 = ((f32[64,2,128]{2,1,0:T(2,128)}), f32[64,2,128]{2,1,0:T(2,128)S(1)}, u32[]{:S(2)}, u32[]{:S(2)}) async-start(f32[64,2,128]{2,1,0:T(2,128)} %bitcast.17), calls=%async_computation.1 | async-start | bytes 131072 | tf_op jit(solution)/shard_map/all_to_all | solution.py:149
  67.0 0.6 copy-start.1
  90.8 18.1 %all-to-all-start.3 = ((f32[64,2,128]{2,1,0:T(2,128)}), f32[64,2,128]{2,1,0:T(2,128)S(1)}, u32[]{:S(2)}, u32[]{:S(2)}) async-start(f32[64,2,128]{2,1,0:T(2,128)} %bitcast.18), calls=%async_computation.3 | async-start | bytes 131072 | tf_op jit(solution)/shard_map/all_to_all | solution.py:149
  108.9 0.6 copy-start.2

commit v2 on v1

--- a/solution.py
+++ b/solution.py
@@ -55,18 +55,26 @@
     return pl.ds(pl.multiple_of(index * HD, HD), HD)
 
 
-def pack_kernel(core_ref, q_ref, k_ref, v_ref, g_ref, out_ref):
-    other = 1 - core_ref[0]
-    for place, ref in enumerate((q_ref, k_ref, v_ref, g_ref)):
-        out_ref[place] = ref[:, columns(other)].astype(F32)
-
-
-def local_kernel(core_ref, q_ref, k_ref, v_ref, g_ref, got_ref, qo_ref, ko_ref, vo_ref, go_ref, state_ref):
+def pack_kernel(core_ref, q_ref, k_ref, v_ref, g_ref, send_ref, own_ref, other_ref, sems):
+    core = core_ref[0]
+    copies = []
+    for part, (head, into) in enumerate(((1 - core, other_ref), (core, own_ref))):
+        for place, ref in enumerate((q_ref, k_ref, v_ref, g_ref)):
+            copy = pltpu.make_async_copy(ref.at[:, columns(head)], into.at[place], sems.at[4 * part + place])
+            copy.start()
+            copies.append(copy)
+    for place in range(4):
+        copies[place].wait()
+        send_ref[place] = other_ref[place].astype(F32)
+    for copy in copies[4:]:
+        copy.wait()
+
+
+def local_kernel(core_ref, own_ref, got_ref, qo_ref, ko_ref, vo_ref, go_ref, state_ref):
     core = core_ref[0]
     other = 1 - core
-    pairs = ((q_ref, qo_ref), (k_ref, ko_ref), (v_ref, vo_ref), (g_ref, go_ref))
-    for place, (ref, out_ref) in enumerate(pairs):
-        out_ref[columns(core), :] = ref[:, columns(core)]
+    for place, out_ref in enumerate((qo_ref, ko_ref, vo_ref, go_ref)):
+        out_ref[columns(core), :] = own_ref[place]
         out_ref[columns(other), :] = got_ref[other, place].astype(BF16)
     state_ref[...] = product(halves(feature(ko_ref[...])), vo_ref[...], TN)
 
@@ -81,13 +89,17 @@
     out_ref[...] = product(taken, halves(pieces_ref[...]), NN)
 
 
-def forward_kernel(q_ref, k_ref, v_ref, g_ref, gain_ref, prefix_ref, scores_ref, grad_ref, state_ref):
-    size = q_ref.shape[0]
+def scores_kernel(q_ref, k_ref, v_ref, scores_ref, near_ref):
     query = halves(feature(q_ref[...]))
     key = halves(feature(k_ref[...]))
-    scores = jnp.where(causal(size), product(query, key, NT), 0.0)
+    scores = jnp.where(causal(q_ref.shape[0]), product(query, key, NT), 0.0)
     scores_ref[...] = scores
-    output = product(halves(scores), v_ref[...], NN) + product(query, halves(prefix_ref[...]), NN)
+    near_ref[...] = product(halves(scores), v_ref[...], NN)
+
+
+def forward_kernel(q_ref, g_ref, gain_ref, near_ref, prefix_ref, grad_ref, state_ref):
+    query = halves(feature(q_ref[...]))
+    output = near_ref[...] + product(query, halves(prefix_ref[...]), NN)
     inverse = lax.rsqrt(jnp.mean(output * output, axis=-1, keepdims=True) + 1e-06)
     normed = output * inverse
     scaled = gain_ref[...] * g_ref[...].astype(F32)
@@ -96,31 +108,19 @@
     state_ref[...] = product(query, halves(grad), TN)
 
 
-def inner_kernel(q_ref, k_ref, v_ref, scores_ref, grad_ref, prefix_ref, dq_ref, dk_ref, dv_ref):
-    size = q_ref.shape[0]
+def inner_kernel(core_ref, q_ref, k_ref, v_ref, scores_ref, grad_ref, prefix_ref, own_ref, send_ref, all_ref):
+    core = core_ref[0]
     query = halves(feature(q_ref[...]))
     key = halves(feature(k_ref[...]))
     grad = halves(grad_ref[...])
-    grad_scores = halves(jnp.where(causal(size), product(grad, v_ref[...], NT), 0.0))
+    grad_scores = halves(jnp.where(causal(q_ref.shape[0]), product(grad, v_ref[...], NT), 0.0))
     dq = product(grad_scores, key, NN) + product(grad, halves(prefix_ref[...]), NT)
-    dq_ref[...] = slope(q_ref[...]) * dq
-    dk_ref[...] = product(grad_scores, query, TN)
-    dv_ref[...] = product(halves(scores_ref[...]), grad, TN)
-
-
-def backward_kernel(core_ref, k_ref, v_ref, dq_ref, dk_ref, dv_ref, suffix_ref, own_ref, send_ref):
-    core = core_ref[0]
-    suffix = halves(suffix_ref[...])
-
-    def finish(index, out_ref):
-        rows = columns(index)
-        raw = k_ref[rows, :]
-        out_ref[0] = dq_ref[rows, :]
-        out_ref[1] = slope(raw) * (dk_ref[rows, :] + product(v_ref[rows, :], suffix, NT))
-        out_ref[2] = dv_ref[rows, :] + product(halves(feature(raw)), suffix, NN)
-
-    finish(core, own_ref)
-    finish(1 - core, send_ref)
+    all_ref[0] = slope(q_ref[...]) * dq
+    all_ref[1] = product(grad_scores, query, TN)
+    all_ref[2] = product(halves(scores_ref[...]), grad, TN)
+    for place in range(3):
+        own_ref[place] = all_ref[place, columns(core), :]
+        send_ref[place] = all_ref[place, columns(1 - core), :]
 
 
 def place_kernel(core_ref, own_ref, got_ref, dq_ref, dk_ref, dv_ref):
@@ -131,12 +131,24 @@
         ref[:, columns(other)] = got_ref[other, place]
 
 
-def call(kernel, outs, *operands, scalars=0):
+def backward_kernel(k_ref, v_ref, near_dk_ref, near_dv_ref, suffix_ref, dk_ref, dv_ref):
+    for head in range(2):
+        part = slice(head * HD, head * HD + HD)
+        suffix = halves(suffix_ref[head])
+        raw = k_ref[:, part]
+        dk_ref[:, part] = slope(raw) * (near_dk_ref[:, part] + product(v_ref[:, part], suffix, NT))
+        dv_ref[:, part] = near_dv_ref[:, part] + product(halves(feature(raw)), suffix, NN)
+
+
+def call(kernel, outs, *operands, scalars=0, space=pltpu.VMEM, scratch=()):
+    others = [pl.BlockSpec(memory_space=space)] * (len(operands) - scalars)
     return pl.pallas_call(
         kernel,
         out_shape=[jax.ShapeDtypeStruct(shape, dtype) for shape, dtype in outs],
-        in_specs=[SMEM] * scalars + [VMEM] * (len(operands) - scalars),
+        in_specs=[SMEM] * scalars + others,
         out_specs=[VMEM] * len(outs),
+        scratch_shapes=scratch,
+        compiler_params=pltpu.CompilerParams(vmem_limit_bytes=8 << 20),
     )(*operands)
 
 
@@ -154,26 +166,30 @@
     core = lax.axis_index("c")
     at = core.reshape(1)
     gain_row = lax.dynamic_slice(gain, (core * HD,), (HD,)).reshape(1, HD)
-    (sent,) = call(pack_kernel, [((4, tokens, HD), F32)], at, query, key, value, grad_out, scalars=1)
-    got = lax.all_gather(sent, "c")
-    pair = (2 * tokens, HD)
-    q, k, v, g, state = call(
-        local_kernel,
-        [(pair, BF16)] * 4 + [((HD, HD), F32)],
-        at, query, key, value, grad_out, got,
-        scalars=1,
+    four, three, pair, state_shape = (4, tokens, HD), (3, tokens, HD), (2 * tokens, HD), (HD, HD)
+    send, own = call(
+        pack_kernel,
+        [(four, F32), (four, BF16)],
+        at, *(pltpu.with_memory_space_constraint(array, pltpu.HBM) for array in (query, key, value, grad_out)),
+        scalars=1, space=pltpu.HBM, scratch=[pltpu.VMEM(four, BF16), pltpu.SemaphoreType.DMA((8,))],
     )
+    got = lax.all_gather(send, "c")
+    q, k, v, g, state = call(local_kernel, [(pair, BF16)] * 4 + [(state_shape, F32)], at, own, got, scalars=1)
     prefix = scan_chips(state, False)
-    scores, grad, state = call(
-        forward_kernel,
-        [((2 * tokens, 2 * tokens), F32), (pair, F32), ((HD, HD), F32)],
-        q, k, v, g, gain_row, prefix,
+    scores, near = call(scores_kernel, [((2 * tokens, 2 * tokens), F32), (pair, F32)], q, k, v)
+    grad, state = call(forward_kernel, [(pair, F32), (state_shape, F32)], q, g, gain_row, near, prefix)
+    suffix = scan_chips(state, True)
+    own, send = call(
+        inner_kernel,
+        [(three, F32)] * 2,
+        at, q, k, v, scores, grad, prefix,
+        scalars=1, scratch=[pltpu.VMEM((3,) + pair, F32)],
     )
-    suffix = scan_chips(state, True)
-    dq, dk, dv = call(inner_kernel, [(pair, F32)] * 3, q, k, v, scores, grad, prefix)
-    own, send = call(backward_kernel, [((3, tokens, HD), F32)] * 2, at, k, v, dq, dk, dv, suffix, scalars=1)
     got = lax.all_gather(send, "c")
-    return tuple(call(place_kernel, [((tokens, 2 * HD), F32)] * 3, at, own, got, scalars=1))
+    whole = ((tokens, 2 * HD), F32)
+    dq, dk, dv = call(place_kernel, [whole] * 3, at, own, got, scalars=1)
+    dk, dv = call(backward_kernel, [whole] * 2, key, value, dk, dv, lax.all_gather(suffix, "c"))
+    return dq, dk, dv
 
 
 def over(devices):

time: 123 us -> 105 us (0.85)
  Pallas kernels: 16.1 us -> 6.41 us
  waiting for transfers between devices: 23.9 us -> 19.5 us
  local copies, waits for them, and re-layouts: 1.84 us -> 0.1 us
  blocking collectives: 69.9 us -> 68.4 us
    all_gather x1, blocking collectives: 19.1 us -> 6.54 us  [body(): lax.all_gather(suffix, 'c')]
    all_gather x1 -> x2, blocking collectives: 8.97 us -> 21.4 us  [body(): got = lax.all_gather(send, 'c')]
    pallas_call x8 -> x9, Pallas kernels: 16.1 us -> 6.41 us  [call(): pl.pallas_call(kernel, out_shape=[jax.ShapeDtypeStruct(shape, dtype) for...]
    all_to_all x2, waiting for transfers between devices: 23.9 us -> 19.5 us  [scan_chips(): lax.all_to_all(sums.reshape(chips, rows, HD), ('x', 'z'), 0, 0)]
    all_to_all x2, blocking collectives: 41.8 us -> 40.5 us  [scan_chips(): pieces = lax.all_to_all(state.reshape(chips, rows, HD), ('x', 'z'), 0, 0)]
    unnamed x6, local copies, waits for them, and re-layouts: 1.26 us -> 0.02 us
where the time goes in v2:
time: 105 us
  blocking collectives  68.4 us (65%)
  waiting for transfers between devices  19.5 us (19%)
  starting transfers between devices  9.84 us (9%)
  Pallas kernels  6.41 us (6%)
    all_to_all x2, blocking collectives, scan_chips(): pieces = lax.all_to_all(state.reshape(chips, rows, HD), ('x', 'z'), 0, 0)  40.5 us
    all_gather x2, blocking collectives, body(): got = lax.all_gather(send, 'c')  21.4 us
    all_to_all x2, waiting for transfers between devices, scan_chips(): lax.all_to_all(sums.reshape(chips, rows, HD), ('x', 'z'), 0, 0)  19.5 us
    all_to_all x2, starting transfers between devices, scan_chips(): lax.all_to_all(sums.reshape(chips, rows, HD), ('x', 'z'), 0, 0)  9.84 us
    all_gather x1, blocking collectives, body(): lax.all_gather(suffix, 'c')  6.54 us
    pallas_call x9, Pallas kernels, call(): pl.pallas_call(kernel, out_shape=[jax.ShapeDtypeStruct(shape, dtype) for...  6.41 us
  transfers between devices with their start and end apart: 2, of which 2 were waited for; matrix products, arithmetic and copies ran while one was open for 0% of the time, Pallas kernels for 2%

profile of v2, /device:TPU:1, one launch (start us, length us, event | category | flops | bytes accessed | tf_op | source)
XLA Modules:
  0.0 105.0 jit_solution(17252747738079156046)
XLA Ops:
  0.6 0.0 copy-start
  0.7 0.9 shard_map.76
  1.6 16.0 %all-gather = f32[8,128,128]{2,1,0:T(8,128)S(1)} all-gather(f32[4,128,128]{2,1,0:T(8,128)S(1)} %get-tuple-element.22), channel_id=2, replica_groups=mesh['x'=4,'z'=16,'c'=2,'h'=8] {'c'}, dimensions={0}, use_global_device_ids=true | all-gather | bytes 786432 | tf_op jit(solution)/shard_map/all_gather | solution.py:176
  17.6 0.3 shard_map.77
  17.8 22.7 %all_to_all.20 = f32[64,2,128]{2,1,0:T(2,128)S(1)} all-to-all(f32[64,2,128]{2,1,0:T(2,128)S(1)} %bitcast.19), channel_id=1, replica_groups=mesh['x'=4,'z'=16,'c'=2,'h'=8] {'x','z'}, dimensions={0} | all-to-all | bytes 131072 | tf_op jit(solution)/shard_map/all_to_all | solution.py:158
  40.5 0.8 shard_map.79
  41.3 5.2 %all-to-all-start.1 = ((f32[64,2,128]{2,1,0:T(2,128)}), f32[64,2,128]{2,1,0:T(2,128)S(1)}, u32[]{:S(2)}, u32[]{:S(2)}) async-start(f32[64,2,128]{2,1,0:T(2,128)} %bitcast.5), calls=%async_computation.1 | async-start | bytes 131072 | tf_op jit(solution)/shard_map/all_to_all | solution.py:161
  46.5 0.5 shard_map.78
  47.1 0.0 copy-done
  47.1 0.1 dynamic-slice_bitcast_fusion.gain_ref
  47.1 12.9 %all-to-all-done.1 = f32[64,2,128]{2,1,0:T(2,128)S(1)} async-done(((f32[64,2,128]{2,1,0:T(2,128)}), f32[64,2,128]{2,1,0:T(2,128)S(1)}, u32[]{:S(2)}, u32[]{:S(2)}) %all-to-all-start.1) | async-done | bytes 65568 | tf_op jit(solution)/shard_map/all_to_all | solution.py:161
  60.0 0.6 shard_map.80
  60.7 17.8 %all_to_all.21 = f32[64,2,128]{2,1,0:T(2,128)S(1)} all-to-all(f32[64,2,128]{2,1,0:T(2,128)S(1)} %bitcast.20), channel_id=1, replica_groups=mesh['x'=4,'z'=16,'c'=2,'h'=8] {'x','z'}, dimensions={0} | all-to-all | bytes 131072 | tf_op jit(solution)/shard_map/all_to_all | solution.py:158
  78.5 0.8 shard_map.83
  79.3 4.6 %all-to-all-start.3 = ((f32[64,2,128]{2,1,0:T(2,128)}), f32[64,2,128]{2,1,0:T(2,128)S(1)}, u32[]{:S(2)}, u32[]{:S(2)}) async-start(f32[64,2,128]{2,1,0:T(2,128)} %bitcast.10), calls=%async_computation.3 | async-start | bytes 131072 | tf_op jit(solution)/shard_map/all_to_all | solution.py:161
  83.9 0.8 shard_map.81
  84.8 5.4 %all-gather.1 = f32[6,128,128]{2,1,0:T(8,128)S(1)} all-gather(f32[3,128,128]{2,1,0:T(8,128)S(1)} %get-tuple-element.32), channel_id=3, replica_groups=mesh['x'=4,'z'=16,'c'=2,'h'=8] {'c'}, dimensions={0}, use_global_device_ids=true | all-gather | bytes 589824 | tf_op jit(solution)/shard_map/all_gather | solution.py:188
  90.2 0.7 shard_map.82
  90.9 6.6 %all-to-all-done.3 = f32[64,2,128]{2,1,0:T(2,128)S(1)} async-done(((f32[64,2,128]{2,1,0:T(2,128)}), f32[64,2,128]{2,1,0:T(2,128)S(1)}, u32[]{:S(2)}, u32[]{:S(2)}) %all-to-all-start.3) | async-done | bytes 65568 | tf_op jit(solution)/shard_map/all_to_all | solution.py:161
  97.5 0.0 copy-start.1
  97.5 0.0 copy-start.2
  97.5 6.5 %all_gather.19.suffix_ref = f32[2,128,128]{2,1,0:T(8,128)S(1)} all-gather(f32[1,128,128]{2,1,0:T(8,128)S(1)} %bitcast.21), channel_id=1, replica_groups=mesh['x'=4,'z'=16,'c'=2,'h'=8] {'c'}, dimensions={0}, use_global_device_ids=true | all-gather | bytes 196608 | tf_op jit(solution)/shard_map/all_gather | solution.py:191
  104.0 0.0 copy-done.1
  104.0 0.0 copy-done.2
  104.0 1.0 shard_map.84
Async XLA Ops:
  0.6 46.4 %copy-start = (f32[256]{0:T(256)S(1)}, f32[256]{0:T(256)}, u32[]{:S(2)}) copy-start(f32[256]{0:T(256)} %param.8) | copy-start | bytes 3076
  41.3 18.8 %all-to-all-start.1 = ((f32[64,2,128]{2,1,0:T(2,128)}), f32[64,2,128]{2,1,0:T(2,128)S(1)}, u32[]{:S(2)}, u32[]{:S(2)}) async-start(f32[64,2,128]{2,1,0:T(2,128)} %bitcast.5), calls=%async_computation.1 | async-start | bytes 131072 | tf_op jit(solution)/shard_map/all_to_all | solution.py:161
  79.3 18.1 %all-to-all-start.3 = ((f32[64,2,128]{2,1,0:T(2,128)}), f32[64,2,128]{2,1,0:T(2,128)S(1)}, u32[]{:S(2)}, u32[]{:S(2)}) async-start(f32[64,2,128]{2,1,0:T(2,128)} %bitcast.10), calls=%async_computation.3 | async-start | bytes 131072 | tf_op jit(solution)/shard_map/all_to_all | solution.py:161
  97.5 6.5 %copy-start.1 = (bf16[128,256]{1,0:T(8,128)(2,1)S(1)}, bf16[128,256]{1,0:T(8,128)(2,1)}, u32[]{:S(2)}) copy-start(bf16[128,256]{1,0:T(8,128)(2,1)} %k_ref.3) | copy-start | bytes 196612
  97.5 6.5 %copy-start.2 = (bf16[128,256]{1,0:T(8,128)(2,1)S(1)}, bf16[128,256]{1,0:T(8,128)(2,1)}, u32[]{:S(2)}) copy-start(bf16[128,256]{1,0:T(8,128)(2,1)} %v_ref.3) | copy-start | bytes 196612

commit v3 on v2

--- a/solution.py
+++ b/solution.py
@@ -55,14 +55,20 @@
     return pl.ds(pl.multiple_of(index * HD, HD), HD)
 
 
-def pack_kernel(core_ref, q_ref, k_ref, v_ref, g_ref, send_ref, own_ref, other_ref, sems):
-    core = core_ref[0]
+def core_of(at_ref):
+    return lax.rem(at_ref[0], 2)
+
+
+def pack_kernel(at_ref, q_ref, k_ref, v_ref, g_ref, gain_ref, send_ref, own_ref, gain_out_ref, other_ref, sems):
+    core = core_of(at_ref)
     copies = []
     for part, (head, into) in enumerate(((1 - core, other_ref), (core, own_ref))):
         for place, ref in enumerate((q_ref, k_ref, v_ref, g_ref)):
             copy = pltpu.make_async_copy(ref.at[:, columns(head)], into.at[place], sems.at[4 * part + place])
             copy.start()
             copies.append(copy)
+    copies.append(pltpu.make_async_copy(gain_ref, gain_out_ref, sems.at[8]))
+    copies[8].start()
     for place in range(4):
         copies[place].wait()
         send_ref[place] = other_ref[place].astype(F32)
@@ -70,23 +76,41 @@
         copy.wait()
 
 
-def local_kernel(core_ref, own_ref, got_ref, qo_ref, ko_ref, vo_ref, go_ref, state_ref):
-    core = core_ref[0]
+def local_kernel(at_ref, own_ref, got_ref, gain_ref, qo_ref, ko_ref, vo_ref, scaled_ref, state_ref):
+    core = core_of(at_ref)
     other = 1 - core
-    for place, out_ref in enumerate((qo_ref, ko_ref, vo_ref, go_ref)):
+    gain_row = gain_ref[pl.ds(core, 1), :]
+    for place, out_ref in enumerate((qo_ref, ko_ref, vo_ref)):
         out_ref[columns(core), :] = own_ref[place]
         out_ref[columns(other), :] = got_ref[other, place].astype(BF16)
+    scaled_ref[columns(core), :] = gain_row * own_ref[3].astype(F32)
+    scaled_ref[columns(other), :] = gain_row * got_ref[other, 3]
     state_ref[...] = product(halves(feature(ko_ref[...])), vo_ref[...], TN)
 
 
-def prefix_kernel(rows, backward, pieces_ref, out_ref):
-    size = pieces_ref.shape[0]
-    row = lax.broadcasted_iota(jnp.int32, (size, size), 0)
-    column = lax.broadcasted_iota(jnp.int32, (size, size), 1)
-    same = lax.rem(row, rows) == lax.rem(column, rows)
-    apart = row - column if not backward else column - row
-    taken = jnp.where(same & (apart > 0), 1.0, 0.0).astype(BF16)
-    out_ref[...] = product(taken, halves(pieces_ref[...]), NN)
+def total_kernel(pieces_ref, out_ref):
+    total = pieces_ref[:, 0]
+    for place in range(1, pieces_ref.shape[1]):
+        total = total + pieces_ref[:, place]
+    for block in range(out_ref.shape[0]):
+        out_ref[block] = total
+
+
+def prefix_kernel(backward, at_ref, pieces_ref, totals_ref, out_ref):
+    x_size, place_size = pieces_ref.shape[:2]
+    blocks = totals_ref.shape[0]
+    block = lax.rem(lax.div(at_ref[0], 2 * place_size), blocks)
+    base = jnp.zeros(pieces_ref.shape[2:], F32)
+    for x in range(x_size)[:: -1 if backward else 1]:
+        so_far, row = base, jnp.zeros_like(base)
+        for other in range(blocks):
+            total = totals_ref[other, x]
+            row = row + total
+            so_far = so_far + jnp.where(other > block if backward else other < block, total, 0.0)
+        for place in range(place_size)[:: -1 if backward else 1]:
+            out_ref[x, place] = so_far
+            so_far = so_far + pieces_ref[x, place]
+        base = base + row
 
 
 def scores_kernel(q_ref, k_ref, v_ref, scores_ref, near_ref):
@@ -97,19 +121,19 @@
     near_ref[...] = product(halves(scores), v_ref[...], NN)
 
 
-def forward_kernel(q_ref, g_ref, gain_ref, near_ref, prefix_ref, grad_ref, state_ref):
+def forward_kernel(q_ref, scaled_ref, near_ref, prefix_ref, grad_ref, state_ref):
     query = halves(feature(q_ref[...]))
     output = near_ref[...] + product(query, halves(prefix_ref[...]), NN)
     inverse = lax.rsqrt(jnp.mean(output * output, axis=-1, keepdims=True) + 1e-06)
     normed = output * inverse
-    scaled = gain_ref[...] * g_ref[...].astype(F32)
+    scaled = scaled_ref[...]
     grad = inverse * (scaled - normed * jnp.mean(scaled * normed, axis=-1, keepdims=True))
     grad_ref[...] = grad
     state_ref[...] = product(query, halves(grad), TN)
 
 
-def inner_kernel(core_ref, q_ref, k_ref, v_ref, scores_ref, grad_ref, prefix_ref, own_ref, send_ref, all_ref):
-    core = core_ref[0]
+def inner_kernel(at_ref, q_ref, k_ref, v_ref, scores_ref, grad_ref, prefix_ref, own_ref, send_ref, all_ref):
+    core = core_of(at_ref)
     query = halves(feature(q_ref[...]))
     key = halves(feature(k_ref[...]))
     grad = halves(grad_ref[...])
@@ -123,8 +147,8 @@
         send_ref[place] = all_ref[place, columns(1 - core), :]
 
 
-def place_kernel(core_ref, own_ref, got_ref, dq_ref, dk_ref, dv_ref):
-    core = core_ref[0]
+def place_kernel(at_ref, own_ref, got_ref, dq_ref, dk_ref, dv_ref):
+    core = core_of(at_ref)
     other = 1 - core
     for place, ref in enumerate((dq_ref, dk_ref, dv_ref)):
         ref[:, columns(core)] = own_ref[place]
@@ -152,33 +176,36 @@
     )(*operands)
 
 
-def scan_chips(state, backward):
-    chips = lax.axis_size("x") * lax.axis_size("z")
-    rows = HD // chips
-    pieces = lax.all_to_all(state.reshape(chips, rows, HD), ("x", "z"), 0, 0)
-    kernel = functools.partial(prefix_kernel, rows, backward)
-    (sums,) = call(kernel, [((HD, HD), F32)], pieces.reshape(HD, HD))
-    return lax.all_to_all(sums.reshape(chips, rows, HD), ("x", "z"), 0, 0).reshape(HD, HD)
+def scan_chips(at, state, backward):
+    blocks, x_size, place_size = lax.axis_size("zb"), lax.axis_size("x"), lax.axis_size("zp")
+    members = x_size * place_size
+    piece = (HD // members, HD)
+    near = (x_size, place_size) + piece
+    pieces = lax.all_to_all(state.reshape((members,) + piece), ("x", "zp"), 0, 0).reshape(near)
+    far = (blocks, x_size) + piece
+    (totals,) = call(total_kernel, [(far, F32)], pieces)
+    totals = lax.all_to_all(totals, "zb", 0, 0)
+    (sums,) = call(functools.partial(prefix_kernel, backward), [(near, F32)], at, pieces, totals, scalars=1)
+    return lax.all_to_all(sums.reshape((members,) + piece), ("x", "zp"), 0, 0).reshape(HD, HD)
 
 
 def body(query, key, value, gain, grad_out):
     tokens = query.shape[0]
-    core = lax.axis_index("c")
-    at = core.reshape(1)
-    gain_row = lax.dynamic_slice(gain, (core * HD,), (HD,)).reshape(1, HD)
+    at = lax.axis_index(("x", "zb", "zp", "c")).reshape(1)
     four, three, pair, state_shape = (4, tokens, HD), (3, tokens, HD), (2 * tokens, HD), (HD, HD)
-    send, own = call(
+    send, own, gain = call(
         pack_kernel,
-        [(four, F32), (four, BF16)],
-        at, *(pltpu.with_memory_space_constraint(array, pltpu.HBM) for array in (query, key, value, grad_out)),
-        scalars=1, space=pltpu.HBM, scratch=[pltpu.VMEM(four, BF16), pltpu.SemaphoreType.DMA((8,))],
+        [(four, F32), (four, BF16), ((2, HD), F32)],
+        at, *(pltpu.with_memory_space_constraint(array, pltpu.HBM) for array in (query, key, value, grad_out, gain.reshape(2, HD))),
+        scalars=1, space=pltpu.HBM, scratch=[pltpu.VMEM(four, BF16), pltpu.SemaphoreType.DMA((9,))],
     )
     got = lax.all_gather(send, "c")
-    q, k, v, g, state = call(local_kernel, [(pair, BF16)] * 4 + [(state_shape, F32)], at, own, got, scalars=1)
-    prefix = scan_chips(state, False)
+    outs = [(pair, BF16)] * 3 + [(pair, F32), (state_shape, F32)]
+    q, k, v, scaled, state = call(local_kernel, outs, at, own, got, gain, scalars=1)
+    prefix = scan_chips(at, state, False)
     scores, near = call(scores_kernel, [((2 * tokens, 2 * tokens), F32), (pair, F32)], q, k, v)
-    grad, state = call(forward_kernel, [(pair, F32), (state_shape, F32)], q, g, gain_row, near, prefix)
-    suffix = scan_chips(state, True)
+    grad, state = call(forward_kernel, [(pair, F32), (state_shape, F32)], q, scaled, near, prefix)
+    suffix = scan_chips(at, state, True)
     own, send = call(
         inner_kernel,
         [(three, F32)] * 2,
@@ -193,8 +220,8 @@
 
 
 def over(devices):
-    mesh = Mesh(devices, ("x", "z", "c", "h"))
-    placed = P(("x", "z", "c"), "h")
+    mesh = Mesh(devices, ("x", "zb", "zp", "c", "h"))
+    placed = P(("x", "zb", "zp", "c"), "h")
     return jax.shard_map(
         body,
         mesh=mesh,
@@ -206,4 +233,4 @@
 
 def solution(mesh):
     seq, head = mesh.devices.shape
-    return over(mesh.devices.reshape(4, seq // 8, 2, head))
+    return over(mesh.devices.reshape(4, 4, seq // 32, 2, head))

time: 105 us -> 107 us (1.019)
  blocking collectives: 68.4 us -> 85.8 us
  waiting for transfers between devices: 19.5 us -> 6.45 us
  starting transfers between devices: 9.84 us -> 7.01 us
    all_to_all x2 -> x4, blocking collectives: 40.5 us -> 55.5 us  [the longest x2 36.3 us: scan_chips(): totals = lax.all_to_all(totals, 'zb', 0, 0)]
    all_to_all x2, waiting for transfers between devices: 19.5 us -> 6.45 us  [scan_chips(): lax.all_to_all(sums.reshape((members,) + piece), ('x', 'zp'), 0, 0)]
    all_to_all x2, starting transfers between devices: 9.84 us -> 7.01 us  [scan_chips(): lax.all_to_all(sums.reshape((members,) + piece), ('x', 'zp'), 0, 0)]
    all_gather x2, blocking collectives: 21.4 us -> 23.8 us  [body(): got = lax.all_gather(send, 'c')]
    pallas_call x9 -> x11, Pallas kernels: 6.41 us -> 6.24 us  [call(): pl.pallas_call(kernel, out_shape=[jax.ShapeDtypeStruct(shape, dtype) for...]
  transfers between devices with their start and end apart: 2 -> 2, of which waited for: 2 -> 1; matrix products, arithmetic and copies ran while one was open for 0% -> 0% of each run, Pallas kernels for 2% -> 2%
where the time goes in v3:
time: 107 us; the launch traced here: 106 us
  blocking collectives  85.8 us (80%)
  starting transfers between devices  7.01 us (7%)
  waiting for transfers between devices  6.45 us (6%)
  Pallas kernels  6.24 us (6%)
    all_to_all x2, blocking collectives, scan_chips(): totals = lax.all_to_all(totals, 'zb', 0, 0)  36.3 us
    all_gather x2, blocking collectives, body(): got = lax.all_gather(send, 'c')  23.8 us
    all_to_all x2, blocking collectives, scan_chips(): lax.all_to_all(state.reshape((members,) + piece), ('x', 'zp'), 0, 0)  19.2 us
    all_to_all x2, starting transfers between devices, scan_chips(): lax.all_to_all(sums.reshape((members,) + piece), ('x', 'zp'), 0, 0)  7.01 us
    all_gather x1, blocking collectives, body(): lax.all_gather(suffix, 'c')  6.46 us
    all_to_all x2, waiting for transfers between devices, scan_chips(): lax.all_to_all(sums.reshape((members,) + piece), ('x', 'zp'), 0, 0)  6.45 us
    pallas_call x11, Pallas kernels, call(): pl.pallas_call(kernel, out_shape=[jax.ShapeDtypeStruct(shape, dtype) for...  6.24 us
  transfers between devices with their start and end apart: 2, of which 1 were waited for; matrix products, arithmetic and copies ran while one was open for 0% of the time, Pallas kernels for 2%

profile of v3, /device:TPU:1, one launch (start us, length us, event | category | flops | bytes accessed | tf_op | source)
XLA Modules:
  0.0 106.2 jit_solution(15377300937572948993)
XLA Ops:
  0.6 1.0 shard_map.76
  1.6 16.0 %all-gather = f32[8,128,128]{2,1,0:T(8,128)S(1)} all-gather(f32[4,128,128]{2,1,0:T(8,128)S(1)} %get-tuple-element.23), channel_id=2, replica_groups=mesh['x'=4,'zb'=4,'zp'=4,'c'=2,'h'=8] {'c'}, dimensions={0}, use_global_device_ids=true | all-gather | bytes 786432 | tf_op jit(solution)/shard_map/all_gather | solution.py:202
  17.6 0.3 shard_map.77
  17.8 9.6 %all_to_all.30 = f32[16,8,128]{2,1,0:T(8,128)S(1)} all-to-all(f32[16,8,128]{2,1,0:T(8,128)S(1)} %bitcast.20), channel_id=1, replica_groups=mesh['x'=4,'zb'=4,'zp'=4,'c'=2,'h'=8] {'x','zp'}, dimensions={0} | all-to-all | bytes 131072 | tf_op jit(solution)/shard_map/all_to_all | solution.py:184
  27.5 22.3 %all_to_all.31.totals_ref = f32[4,4,8,128]{3,2,1,0:T(8,128)S(1)} all-to-all(f32[4,4,8,128]{3,2,1,0:T(8,128)S(1)} %shard_map.79), channel_id=1, replica_groups=mesh['x'=4,'zb'=4,'zp'=4,'c'=2,'h'=8] {'zb'}, dimensions={0} | all-to-all | bytes 131072 | tf_op jit(solution)/shard_map/all_to_all | solution.py:187
  49.8 0.6 shard_map.80
  50.4 3.5 %all-to-all-start.2 = ((f32[16,8,128]{2,1,0:T(8,128)}), f32[16,8,128]{2,1,0:T(8,128)S(1)}, u32[]{:S(2)}, u32[]{:S(2)}) async-start(f32[16,8,128]{2,1,0:T(8,128)} %bitcast.5), calls=%async_computation.2 | async-start | bytes 131072 | tf_op jit(solution)/shard_map/all_to_all | solution.py:189
  53.9 0.5 shard_map.78
  54.4 6.4 %all-to-all-done.2 = f32[16,8,128]{2,1,0:T(8,128)S(1)} async-done(((f32[16,8,128]{2,1,0:T(8,128)}), f32[16,8,128]{2,1,0:T(8,128)S(1)}, u32[]{:S(2)}, u32[]{:S(2)}) %all-to-all-start.2) | async-done | bytes 65568 | tf_op jit(solution)/shard_map/all_to_all | solution.py:189
  60.9 0.6 shard_map.81
  61.5 9.5 %all_to_all.32 = f32[16,8,128]{2,1,0:T(8,128)S(1)} all-to-all(f32[16,8,128]{2,1,0:T(8,128)S(1)} %bitcast.21), channel_id=1, replica_groups=mesh['x'=4,'zb'=4,'zp'=4,'c'=2,'h'=8] {'x','zp'}, dimensions={0} | all-to-all | bytes 131072 | tf_op jit(solution)/shard_map/all_to_all | solution.py:184
  71.1 14.1 %all_to_all.33.totals_ref = f32[4,4,8,128]{3,2,1,0:T(8,128)S(1)} all-to-all(f32[4,4,8,128]{3,2,1,0:T(8,128)S(1)} %shard_map.84), channel_id=1, replica_groups=mesh['x'=4,'zb'=4,'zp'=4,'c'=2,'h'=8] {'zb'}, dimensions={0} | all-to-all | bytes 131072 | tf_op jit(solution)/shard_map/all_to_all | solution.py:187
  85.2 0.6 shard_map.85
  85.8 3.5 %all-to-all-start.5 = ((f32[16,8,128]{2,1,0:T(8,128)}), f32[16,8,128]{2,1,0:T(8,128)S(1)}, u32[]{:S(2)}, u32[]{:S(2)}) async-start(f32[16,8,128]{2,1,0:T(8,128)} %bitcast.10), calls=%async_computation.5 | async-start | bytes 131072 | tf_op jit(solution)/shard_map/all_to_all | solution.py:189
  89.3 0.9 shard_map.82
  90.2 7.9 %all-gather.1 = f32[6,128,128]{2,1,0:T(8,128)S(1)} all-gather(f32[3,128,128]{2,1,0:T(8,128)S(1)} %get-tuple-element.34), channel_id=3, replica_groups=mesh['x'=4,'zb'=4,'zp'=4,'c'=2,'h'=8] {'c'}, dimensions={0}, use_global_device_ids=true | all-gather | bytes 589824 | tf_op jit(solution)/shard_map/all_gather | solution.py:215
  98.1 0.7 shard_map.83
  98.8 0.0 all-to-all-done.5
  98.8 0.0 copy-start
  98.8 0.0 copy-start.1
  98.8 6.5 %all_gather.19.suffix_ref = f32[2,128,128]{2,1,0:T(8,128)S(1)} all-gather(f32[1,128,128]{2,1,0:T(8,128)S(1)} %bitcast.22), channel_id=1, replica_groups=mesh['x'=4,'zb'=4,'zp'=4,'c'=2,'h'=8] {'c'}, dimensions={0}, use_global_device_ids=true | all-gather | bytes 196608 | tf_op jit(solution)/shard_map/all_gather | solution.py:218
  105.2 0.0 copy-done
  105.2 0.0 copy-done.1
  105.2 1.0 shard_map.86
  (2 shorter events, 0.0 us)
Async XLA Ops:
  50.4 10.5 %all-to-all-start.2 = ((f32[16,8,128]{2,1,0:T(8,128)}), f32[16,8,128]{2,1,0:T(8,128)S(1)}, u32[]{:S(2)}, u32[]{:S(2)}) async-start(f32[16,8,128]{2,1,0:T(8,128)} %bitcast.5), calls=%async_computation.2 | async-start | bytes 131072 | tf_op jit(solution)/shard_map/all_to_all | solution.py:189
  85.8 13.0 %all-to-all-start.5 = ((f32[16,8,128]{2,1,0:T(8,128)}), f32[16,8,128]{2,1,0:T(8,128)S(1)}, u32[]{:S(2)}, u32[]{:S(2)}) async-start(f32[16,8,128]{2,1,0:T(8,128)} %bitcast.10), calls=%async_computation.5 | async-start | bytes 131072 | tf_op jit(solution)/shard_map/all_to_all | solution.py:189
  98.8 6.5 %copy-start = (bf16[128,256]{1,0:T(8,128)(2,1)S(1)}, bf16[128,256]{1,0:T(8,128)(2,1)}, u32[]{:S(2)}) copy-start(bf16[128,256]{1,0:T(8,128)(2,1)} %k_ref.3) | copy-start | bytes 196612
  98.8 6.5 %copy-start.1 = (bf16[128,256]{1,0:T(8,128)(2,1)S(1)}, bf16[128,256]{1,0:T(8,128)(2,1)}, u32[]{:S(2)}) copy-start(bf16[128,256]{1,0:T(8,128)(2,1)} %v_ref.3) | copy-start | bytes 196612

commit v4 on v3

v4 whole, which is shorter than its diff:
```python
import functools

import jax
import jax.numpy as jnp
from jax import lax
from jax.experimental import pallas as pl
from jax.experimental.pallas import tpu as pltpu
from jax.sharding import Mesh, PartitionSpec as P

HD = 128
HEADS = 2
F32 = jnp.float32
BF16 = jnp.bfloat16
VMEM = pl.BlockSpec(memory_space=pltpu.VMEM)
SMEM = pl.BlockSpec(memory_space=pltpu.SMEM)
HBM = pl.BlockSpec(memory_space=pltpu.HBM)
NN = (((1,), (0,)), ((), ()))
NT = (((1,), (1,)), ((), ()))
TN = (((0,), (0,)), ((), ()))
NEAR = ("x", "zp", "c")


def halves(wide):
    high = wide.astype(BF16)
    low = (wide - high.astype(F32)).astype(BF16)
    return high, low


def one(left, right, dims):
    return lax.dot_general(left, right, dims, preferred_element_type=F32)


def product(left, right, dims):
    if not isinstance(left, tuple):
        return one(left, right[0], dims) + one(left, right[1], dims)
    if not isinstance(right, tuple):
        return one(left[0], right, dims) + one(left[1], right, dims)
    return one(left[0], right[0], dims) + (one(left[0], right[1], dims) + one(left[1], right[0], dims))


def feature(raw):
    wide = raw.astype(F32)
    return jnp.where(wide > 0, wide + 1.0, jnp.exp(jnp.minimum(wide, 0.0)))


def slope(raw):
    wide = raw.astype(F32)
    return jnp.where(wide > 0, 1.0, jnp.exp(jnp.minimum(wide, 0.0)))


def causal(size):
    row = lax.broadcasted_iota(jnp.int32, (size, size), 0)
    column = lax.broadcasted_iota(jnp.int32, (size, size), 1)
    return row >= column


def features_of(head):
    return slice(head * HD, head * HD + HD)


def local_kernel(block_ref, k_in, v_in, q_in, g_in, gain_in, k_ref, v_ref, q_ref, g_ref, gain_ref, state_ref, sems):
    pairs = ((k_in, k_ref), (v_in, v_ref), (q_in, q_ref), (g_in, g_ref), (gain_in, gain_ref))
    copies = [pltpu.make_async_copy(start, end, sems.at[place]) for place, (start, end) in enumerate(pairs)]
    for copy in copies:
        copy.start()
    copies[0].wait()
    copies[1].wait()
    for head in range(HEADS):
        part = features_of(head)
        state_ref[head] = product(halves(feature(k_ref[:, part])), v_ref[:, part], TN)
    for copy in copies[2:]:
        copy.wait()


def total_kernel(pieces_ref, out_ref):
    total = pieces_ref[:, 0]
    for place in range(1, pieces_ref.shape[1]):
        total = total + pieces_ref[:, place]
    for block in range(out_ref.shape[0]):
        out_ref[block] = total


def prefix_kernel(backward, block_ref, pieces_ref, totals_ref, out_ref):
    x_size, place_size = pieces_ref.shape[:2]
    block = block_ref[0]
    base = jnp.zeros(pieces_ref.shape[2:], F32)
    for x in range(x_size)[:: -1 if backward else 1]:
        so_far, row = base, jnp.zeros_like(base)
        for other in range(totals_ref.shape[0]):
            total = totals_ref[other, x]
            row = row + total
            so_far = so_far + jnp.where(other > block if backward else other < block, total, 0.0)
        for place in range(place_size)[:: -1 if backward else 1]:
            out_ref[x, place] = so_far
            so_far = so_far + pieces_ref[x, place]
        base = base + row


def forward_kernel(q_ref, k_ref, v_ref, g_ref, gain_ref, prefix_ref, scores_ref, grad_ref, state_ref):
    mask = causal(q_ref.shape[0])
    for head in range(HEADS):
        part = features_of(head)
        query = halves(feature(q_ref[:, part]))
        key = halves(feature(k_ref[:, part]))
        scores = jnp.where(mask, product(query, key, NT), 0.0)
        scores_ref[head] = scores
        output = product(halves(scores), v_ref[:, part], NN) + product(query, halves(prefix_ref[head]), NN)
        inverse = lax.rsqrt(jnp.mean(output * output, axis=-1, keepdims=True) + 1e-06)
        normed = output * inverse
        scaled = gain_ref[head : head + 1, :] * g_ref[:, part].astype(F32)
        grad = inverse * (scaled - normed * jnp.mean(scaled * normed, axis=-1, keepdims=True))
        grad_ref[head] = grad
        state_ref[head] = product(query, halves(grad), TN)


def backward_kernel(
    q_ref, k_ref, v_ref, scores_ref, grad_ref, prefix_ref, suffix_ref, dq_out, dk_out, dv_out, dq_ref, dk_ref, dv_ref, sems
):
    mask = causal(q_ref.shape[0])
    copies = []

    def write(start, end):
        copies.append(pltpu.make_async_copy(start, end, sems.at[len(copies)]))
        copies[-1].start()

    grads = [halves(grad_ref[head]) for head in range(HEADS)]
    keys = [halves(feature(k_ref[:, features_of(head)])) for head in range(HEADS)]
    suffixes = [halves(suffix_ref[head]) for head in range(HEADS)]
    grad_scores = []
    for head in range(HEADS):
        part = features_of(head)
        grad_scores.append(halves(jnp.where(mask, product(grads[head], v_ref[:, part], NT), 0.0)))
        dq = product(grad_scores[head], keys[head], NN) + product(grads[head], halves(prefix_ref[head]), NT)
        dq_ref[:, part] = slope(q_ref[:, part]) * dq
    write(dq_ref, dq_out)
    for head in range(HEADS):
        part = features_of(head)
        query = halves(feature(q_ref[:, part]))
        dk = product(grad_scores[head], query, TN) + product(v_ref[:, part], suffixes[head], NT)
        dk_ref[:, part] = slope(k_ref[:, part]) * dk
    write(dk_ref, dk_out)
    for head in range(HEADS):
        part = features_of(head)
        dv = product(halves(scores_ref[head]), grads[head], TN) + product(keys[head], suffixes[head], NN)
        dv_ref[:, part] = dv
    write(dv_ref, dv_out)
    for copy in copies:
        copy.wait()


def call(kernel, outs, *operands, scalars=0, inputs=VMEM, outputs=VMEM, scratch=()):
    return pl.pallas_call(
        kernel,
        out_shape=[jax.ShapeDtypeStruct(shape, dtype) for shape, dtype in outs],
        in_specs=[SMEM] * scalars + [inputs] * (len(operands) - scalars),
        out_specs=[outputs] * len(outs),
        scratch_shapes=scratch,
        compiler_params=pltpu.CompilerParams(vmem_limit_bytes=8 << 20),
    )(*operands)


def scan_devices(block, states, backward):
    blocks, x_size, members = lax.axis_size("zb"), lax.axis_size("x"), lax.axis_size(NEAR)
    piece = (HEADS * HD // members, HD)
    flat, near, far = (members,) + piece, (x_size, members // x_size) + piece, (blocks, x_size) + piece
    pieces = lax.all_to_all(states.reshape(flat), NEAR, 0, 0).reshape(near)
    (totals,) = call(total_kernel, [(far, F32)], pieces)
    totals = lax.all_to_all(totals, "zb", 0, 0)
    (sums,) = call(functools.partial(prefix_kernel, backward), [(near, F32)], block, pieces, totals, scalars=1)
    return lax.all_to_all(sums.reshape(flat), NEAR, 0, 0).reshape(HEADS, HD, HD)


def body(query, key, value, gain, grad_out):
    tokens = query.shape[0]
    block = lax.axis_index("zb").reshape(1)
    wide, per_head, state = (tokens, HEADS * HD), (HEADS, tokens, HD), ((HEADS, HD, HD), F32)
    given = (key, value, query, grad_out, gain.reshape(HEADS, HD))
    k, v, q, g, gain, states = call(
        local_kernel,
        [(wide, BF16)] * 4 + [((HEADS, HD), F32), state],
        block,
        *(pltpu.with_memory_space_constraint(array, pltpu.HBM) for array in given),
        scalars=1,
        inputs=HBM,
        scratch=[pltpu.SemaphoreType.DMA((5,))],
    )
    prefix = scan_devices(block, states, False)
    scores, grad, states = call(
        forward_kernel, [((HEADS, tokens, tokens), F32), (per_head, F32), state], q, k, v, g, gain, prefix
    )
    suffix = scan_devices(block, states, True)
    return tuple(
        call(
            backward_kernel,
            [(wide, F32)] * 3,
            *(q, k, v, scores, grad, prefix, suffix),
            outputs=HBM,
            scratch=[pltpu.VMEM(wide, F32)] * 3 + [pltpu.SemaphoreType.DMA((3,))],
        )
    )


def over(devices):
    mesh = Mesh(devices, ("x", "zb", "zp", "c", "h"))
    placed = P(("x", "zb", "zp", "c"), "h")
    return jax.shard_map(
        body,
        mesh=mesh,
        in_specs=(placed, placed, placed, P("h"), placed),
        out_specs=(placed, placed, placed),
        check_vma=False,
    )


def solution(mesh):
    seq, head = mesh.devices.shape
    return over(mesh.devices.reshape(4, 4, seq // 32, 2, head))
```

time: 107 us -> 107 us (level)
  blocking collectives: 85.8 us -> 102 us
  starting transfers between devices: 7.01 us -> 0 us
  waiting for transfers between devices: 6.45 us -> 0 us
  Pallas kernels: 6.24 us -> 3.88 us
    all_to_all x4 -> x6, blocking collectives: 55.5 us -> 102 us  [the longest x2 37.7 us: scan_devices(): pieces = lax.all_to_all(states.reshape(flat), NEAR, 0, 0).reshape(near)]
    all_gather x3 -> x0, blocking collectives: 30.3 us -> none  [the longest x2 23.8 us: body(): got = lax.all_gather(send, 'c')]
    all_to_all x2 -> x0, starting transfers between devices: 7.01 us -> none  [scan_chips(): lax.all_to_all(sums.reshape((members,) + piece), ('x', 'zp'), 0, 0)]
    all_to_all x2 -> x0, waiting for transfers between devices: 6.45 us -> none  [scan_chips(): lax.all_to_all(sums.reshape((members,) + piece), ('x', 'zp'), 0, 0)]
    pallas_call x11 -> x7, Pallas kernels: 6.24 us -> 3.88 us  [call(): pl.pallas_call(kernel, out_shape=[jax.ShapeDtypeStruct(shape, dtype) for...]
  transfers between devices with their start and end apart: 2 -> 0, of which waited for: 1 -> 0; matrix products, arithmetic and copies ran while one was open for 0% -> 0% of each run, Pallas kernels for 2% -> 0%
where the time goes in v4:
time: 107 us
  blocking collectives  102 us (95%)
  Pallas kernels  3.88 us (4%)
    all_to_all x2, blocking collectives, scan_devices(): pieces = lax.all_to_all(states.reshape(flat), NEAR, 0, 0).reshape(near)  37.7 us
    all_to_all x2, blocking collectives, scan_devices(): totals = lax.all_to_all(totals, 'zb', 0, 0)  35.6 us
    all_to_all x2, blocking collectives, scan_devices(): return lax.all_to_all(sums.reshape(flat), NEAR, 0, 0).reshape(HEADS, HD, HD)  28.7 us
    pallas_call x7, Pallas kernels, call(): pl.pallas_call(kernel, out_shape=[jax.ShapeDtypeStruct(shape, dtype) for...  3.88 us

profile of v4, /device:TPU:1, one launch (start us, length us, event | category | flops | bytes accessed | tf_op | source)
XLA Modules:
  0.0 106.6 jit_solution(5210254986858018251)
XLA Ops:
  0.6 1.2 %shard_map.76 = (bf16[128,256]{1,0:T(8,128)(2,1)S(1)}, bf16[128,256]{1,0:T(8,128)(2,1)S(1)}, bf16[128,256]{1,0:T(8,128)(2,1)S(1)}, bf16[128,256]{1,0:T(8,128)(2,...) custom-call(s32[1]{0:T(128)} %bitcast.block_ref, bf16[128,256]{1,0:T(8,128)(2,1)} %k_in.1, ...), custom_call_target="tpu_custom_call" | custom-call | tf_op jit(solution)/shard_map/pallas_call | solution.py:152
  1.8 25.6 %all_to_all.30 = f32[32,8,128]{2,1,0:T(8,128)S(1)} all-to-all(f32[32,8,128]{2,1,0:T(8,128)S(1)} %bitcast.19), channel_id=1, replica_groups=mesh['x'=4,'zb'=4,'zp'=4,'c'=2,'h'=8] {'x','zp','c'}, dimensions={0} | all-to-all | bytes 262144 | tf_op jit(solution)/shard_map/all_to_all | solution.py:166
  27.4 21.5 %all_to_all.31.totals_ref = f32[4,4,8,128]{3,2,1,0:T(8,128)S(1)} all-to-all(f32[4,4,8,128]{3,2,1,0:T(8,128)S(1)} %shard_map.77), channel_id=1, replica_groups=mesh['x'=4,'zb'=4,'zp'=4,'c'=2,'h'=8] {'zb'}, dimensions={0} | all-to-all | bytes 131072 | tf_op jit(solution)/shard_map/all_to_all | solution.py:168
  49.0 14.4 %all_to_all.32 = f32[32,8,128]{2,1,0:T(8,128)S(1)} all-to-all(f32[32,8,128]{2,1,0:T(8,128)S(1)} %bitcast.17), channel_id=1, replica_groups=mesh['x'=4,'zb'=4,'zp'=4,'c'=2,'h'=8] {'x','zp','c'}, dimensions={0} | all-to-all | bytes 262144 | tf_op jit(solution)/shard_map/all_to_all | solution.py:170
  63.4 1.2 %shard_map.79 = (f32[2,128,128]{2,1,0:T(8,128)S(1)}, f32[2,128,128]{2,1,0:T(8,128)S(1)}, f32[2,128,128]{2,1,0:T(8,128)S(1)}) custom-call(bf16[128,256]{1,0:T(8,128)(2,1)S(1)} %get-tuple-element.12.q_ref, bf16[128,256]{1,0:T(8,128)(2,1)S(1)} %get-tuple-element.13.k_ref, bf16[128,256]{1,0:T(8,128)(2,1)S(1)} %get-tuple-element.14.v_ref, ...), custom_call_target="tpu_custom_call" | custom-call | tf_op jit(solution)/shard_map/pallas_call | solution.py:152
  64.6 12.1 %all_to_all.33 = f32[32,8,128]{2,1,0:T(8,128)S(1)} all-to-all(f32[32,8,128]{2,1,0:T(8,128)S(1)} %bitcast.20), channel_id=1, replica_groups=mesh['x'=4,'zb'=4,'zp'=4,'c'=2,'h'=8] {'x','zp','c'}, dimensions={0} | all-to-all | bytes 262144 | tf_op jit(solution)/shard_map/all_to_all | solution.py:166
  76.7 14.1 %all_to_all.34.totals_ref = f32[4,4,8,128]{3,2,1,0:T(8,128)S(1)} all-to-all(f32[4,4,8,128]{3,2,1,0:T(8,128)S(1)} %shard_map.80), channel_id=1, replica_groups=mesh['x'=4,'zb'=4,'zp'=4,'c'=2,'h'=8] {'zb'}, dimensions={0} | all-to-all | bytes 131072 | tf_op jit(solution)/shard_map/all_to_all | solution.py:168
  90.7 14.4 %all_to_all.35 = f32[32,8,128]{2,1,0:T(8,128)S(1)} all-to-all(f32[32,8,128]{2,1,0:T(8,128)S(1)} %bitcast.16), channel_id=1, replica_groups=mesh['x'=4,'zb'=4,'zp'=4,'c'=2,'h'=8] {'x','zp','c'}, dimensions={0} | all-to-all | bytes 262144 | tf_op jit(solution)/shard_map/all_to_all | solution.py:170
  105.1 1.5 %shard_map.82 = (f32[128,256]{1,0:T(8,128)}, f32[128,256]{1,0:T(8,128)}, f32[128,256]{1,0:T(8,128)}) custom-call(bf16[128,256]{1,0:T(8,128)(2,1)S(1)} %get-tuple-element.12.q_ref, bf16[128,256]{1,0:T(8,128)(2,1)S(1)} %get-tuple-element.13.k_ref, bf16[128,256]{1,0:T(8,128)(2,1)S(1)} %get-tuple-element.14.v_ref, ...), custom_call_target="tpu_custom_call" | custom-call | tf_op jit(solution)/shard_map/pallas_call | solution.py:152
  (4 shorter events, 0.1 us)

commit v5 on v4

--- a/solution.py
+++ b/solution.py
@@ -17,7 +17,7 @@
 NN = (((1,), (0,)), ((), ()))
 NT = (((1,), (1,)), ((), ()))
 TN = (((0,), (0,)), ((), ()))
-NEAR = ("x", "zp", "c")
+NEAR = ("x", "zp")
 
 
 def halves(wide):
@@ -58,7 +58,7 @@
     return slice(head * HD, head * HD + HD)
 
 
-def local_kernel(block_ref, k_in, v_in, q_in, g_in, gain_in, k_ref, v_ref, q_ref, g_ref, gain_ref, state_ref, sems):
+def local_kernel(at_ref, k_in, v_in, q_in, g_in, gain_in, k_ref, v_ref, q_ref, g_ref, gain_ref, state_ref, sems):
     pairs = ((k_in, k_ref), (v_in, v_ref), (q_in, q_ref), (g_in, g_ref), (gain_in, gain_ref))
     copies = [pltpu.make_async_copy(start, end, sems.at[place]) for place, (start, end) in enumerate(pairs)]
     for copy in copies:
@@ -72,31 +72,45 @@
         copy.wait()
 
 
-def total_kernel(pieces_ref, out_ref):
+def core_of(at_ref):
+    return lax.rem(at_ref[0], 2)
+
+
+def total_kernel(pieces_ref, copy_ref, out_ref):
+    copy_ref[...] = pieces_ref[...]
     total = pieces_ref[:, 0]
     for place in range(1, pieces_ref.shape[1]):
         total = total + pieces_ref[:, place]
-    for block in range(out_ref.shape[0]):
-        out_ref[block] = total
-
-
-def prefix_kernel(backward, block_ref, pieces_ref, totals_ref, out_ref):
+    out_ref[...] = total
+
+
+def prefix_kernel(backward, steps, at_ref, pieces_ref, *refs):
+    far_refs, out_ref = refs[:-1], refs[-1]
+    pieces_ref = pieces_ref.at[1]
     x_size, place_size = pieces_ref.shape[:2]
-    block = block_ref[0]
+    blocks = len(steps) + 1
+    block = lax.rem(lax.div(at_ref[0], 2 * place_size), blocks)
     base = jnp.zeros(pieces_ref.shape[2:], F32)
     for x in range(x_size)[:: -1 if backward else 1]:
-        so_far, row = base, jnp.zeros_like(base)
-        for other in range(totals_ref.shape[0]):
-            total = totals_ref[other, x]
+        so_far = row = base
+        for step, far_ref in zip(steps, far_refs):
+            other = lax.rem(block + blocks - step, blocks)
+            total = far_ref[x]
             row = row + total
             so_far = so_far + jnp.where(other > block if backward else other < block, total, 0.0)
         for place in range(place_size)[:: -1 if backward else 1]:
             out_ref[x, place] = so_far
             so_far = so_far + pieces_ref[x, place]
-        base = base + row
-
-
-def forward_kernel(q_ref, k_ref, v_ref, g_ref, gain_ref, prefix_ref, scores_ref, grad_ref, state_ref):
+            row = row + pieces_ref[x, place]
+        base = row
+
+
+def with_core(at_ref, sums_ref, states_ref, head, backward):
+    first, second = (1, 0) if backward else (0, 1)
+    return sums_ref[0, head] + jnp.where(core_of(at_ref) == second, states_ref[first, head], 0.0)
+
+
+def forward_kernel(at_ref, q_ref, k_ref, v_ref, g_ref, gain_ref, sums_ref, states_ref, scores_ref, grad_ref, prefix_ref, state_ref):
     mask = causal(q_ref.shape[0])
     for head in range(HEADS):
         part = features_of(head)
@@ -104,7 +118,9 @@
         key = halves(feature(k_ref[:, part]))
         scores = jnp.where(mask, product(query, key, NT), 0.0)
         scores_ref[head] = scores
-        output = product(halves(scores), v_ref[:, part], NN) + product(query, halves(prefix_ref[head]), NN)
+        prefix = with_core(at_ref, sums_ref, states_ref, head, False)
+        prefix_ref[head] = prefix
+        output = product(halves(scores), v_ref[:, part], NN) + product(query, halves(prefix), NN)
         inverse = lax.rsqrt(jnp.mean(output * output, axis=-1, keepdims=True) + 1e-06)
         normed = output * inverse
         scaled = gain_ref[head : head + 1, :] * g_ref[:, part].astype(F32)
@@ -113,9 +129,9 @@
         state_ref[head] = product(query, halves(grad), TN)
 
 
-def backward_kernel(
-    q_ref, k_ref, v_ref, scores_ref, grad_ref, prefix_ref, suffix_ref, dq_out, dk_out, dv_out, dq_ref, dk_ref, dv_ref, sems
-):
+def backward_kernel(at_ref, *refs):
+    q_ref, k_ref, v_ref, scores_ref, grad_ref, prefix_ref, sums_ref, states_ref = refs[:8]
+    dq_out, dk_out, dv_out, dq_ref, dk_ref, dv_ref, sems = refs[8:]
     mask = causal(q_ref.shape[0])
     copies = []
 
@@ -125,7 +141,7 @@
 
     grads = [halves(grad_ref[head]) for head in range(HEADS)]
     keys = [halves(feature(k_ref[:, features_of(head)])) for head in range(HEADS)]
-    suffixes = [halves(suffix_ref[head]) for head in range(HEADS)]
+    suffixes = [halves(with_core(at_ref, sums_ref, states_ref, head, True)) for head in range(HEADS)]
     grad_scores = []
     for head in range(HEADS):
         part = features_of(head)
@@ -159,41 +175,65 @@
     )(*operands)
 
 
-def scan_devices(block, states, backward):
+def scan_devices(at, states, backward):
     blocks, x_size, members = lax.axis_size("zb"), lax.axis_size("x"), lax.axis_size(NEAR)
+    core = lax.axis_index("c")
     piece = (HEADS * HD // members, HD)
-    flat, near, far = (members,) + piece, (x_size, members // x_size) + piece, (blocks, x_size) + piece
-    pieces = lax.all_to_all(states.reshape(flat), NEAR, 0, 0).reshape(near)
-    (totals,) = call(total_kernel, [(far, F32)], pieces)
-    totals = lax.all_to_all(totals, "zb", 0, 0)
-    (sums,) = call(functools.partial(prefix_kernel, backward), [(near, F32)], block, pieces, totals, scalars=1)
-    return lax.all_to_all(sums.reshape(flat), NEAR, 0, 0).reshape(HEADS, HD, HD)
+    flat, near, far = (members,) + piece, (x_size, members // x_size) + piece, (x_size,) + piece
+    cores = lax.all_gather(states, "c")
+
+    def scatter(cores):
+        pieces = lax.all_to_all((cores[0] + cores[1]).reshape(flat), NEAR, 0, 0).reshape(near)
+        return tuple(call(total_kernel, [(near, F32), (far, F32)], pieces))
+
+    def idle(cores):
+        return jnp.zeros(near, F32), jnp.zeros(far, F32)
+
+    pieces, total = lax.cond(core == 1, scatter, idle, cores)
+    steps = sorted(range(1, blocks), key=lambda step: -min(step, blocks - step))
+    totals = [
+        lax.ppermute(total, ("zb", "c"), [(2 * block + 1, 2 * ((block + step) % blocks)) for block in range(blocks)])
+        for step in steps
+    ]
+    pieces = lax.all_gather(pieces, "c")
+
+    def gather(operands):
+        kernel = functools.partial(prefix_kernel, backward, steps)
+        (sums,) = call(kernel, [(near, F32)], at, *operands, scalars=1)
+        return lax.all_to_all(sums.reshape(flat), NEAR, 0, 0).reshape(HEADS, HD, HD)
+
+    sums = lax.cond(core == 0, gather, lambda operands: jnp.zeros((HEADS, HD, HD), F32), [pieces, *totals])
+    return lax.all_gather(sums, "c"), cores
 
 
 def body(query, key, value, gain, grad_out):
     tokens = query.shape[0]
-    block = lax.axis_index("zb").reshape(1)
+    at = lax.axis_index(("x", "zb", "zp", "c")).reshape(1)
     wide, per_head, state = (tokens, HEADS * HD), (HEADS, tokens, HD), ((HEADS, HD, HD), F32)
     given = (key, value, query, grad_out, gain.reshape(HEADS, HD))
     k, v, q, g, gain, states = call(
         local_kernel,
         [(wide, BF16)] * 4 + [((HEADS, HD), F32), state],
-        block,
+        at,
         *(pltpu.with_memory_space_constraint(array, pltpu.HBM) for array in given),
         scalars=1,
         inputs=HBM,
         scratch=[pltpu.SemaphoreType.DMA((5,))],
     )
-    prefix = scan_devices(block, states, False)
-    scores, grad, states = call(
-        forward_kernel, [((HEADS, tokens, tokens), F32), (per_head, F32), state], q, k, v, g, gain, prefix
-    )
-    suffix = scan_devices(block, states, True)
+    earlier = scan_devices(at, states, False)
+    scores, grad, prefix, states = call(
+        forward_kernel,
+        [((HEADS, tokens, tokens), F32), (per_head, F32), state, state],
+        *(at, q, k, v, g, gain, *earlier),
+        scalars=1,
+    )
+    later = scan_devices(at, states, True)
     return tuple(
         call(
             backward_kernel,
             [(wide, F32)] * 3,
-            *(q, k, v, scores, grad, prefix, suffix),
+            *(at, q, k, v, scores, grad, prefix, *later),
+            scalars=1,
             outputs=HBM,
             scratch=[pltpu.VMEM(wide, F32)] * 3 + [pltpu.SemaphoreType.DMA((3,))],
         )

time: 107 us -> 91.6 us (0.86)
  blocking collectives: 102 us -> 78.7 us
  starting transfers between devices: 0 us -> 7.75 us
    all_to_all x6 -> x2, blocking collectives: 102 us -> 19.6 us  [scatter(): lax.all_to_all((cores[0] + cores[1]).reshape(flat), NEAR, 0, 0)]
    all_gather x0 -> x6, blocking collectives: none -> 59.1 us  [the longest x2 37.3 us: scan_devices(): return (lax.all_gather(sums, 'c'), cores)]
    ppermute x0 -> x6, starting transfers between devices: none -> 7.75 us  [scan_devices(): lax.ppermute(total, ('zb', 'c'), [(2 * block + 1, 2 * ((block + step) % b...]
    pallas_call x7 -> x5, Pallas kernels: 3.88 us -> 3.84 us  [call(): pl.pallas_call(kernel, out_shape=[jax.ShapeDtypeStruct(shape, dtype) for...]
  transfers between devices with their start and end apart: 0 -> 6, of which waited for: 0 -> 0; matrix products, arithmetic and copies ran while one was open for 0% -> 0% of each run, Pallas kernels for 0% -> 0%
where the time goes in v5:
time: 91.6 us; the launch traced here: 91.2 us
  blocking collectives  78.7 us (86%)
  starting transfers between devices  7.75 us (8%)
  Pallas kernels  3.84 us (4%)
    all_gather x2, blocking collectives, scan_devices(): return (lax.all_gather(sums, 'c'), cores)  37.3 us
    all_to_all x2, blocking collectives, scatter(): lax.all_to_all((cores[0] + cores[1]).reshape(flat), NEAR, 0, 0)  19.6 us
    all_gather x2, blocking collectives, scan_devices(): cores = lax.all_gather(states, 'c')  17.8 us
    ppermute x6, starting transfers between devices, scan_devices(): lax.ppermute(total, ('zb', 'c'), [(2 * block + 1, 2 * ((block + step) % b...  7.75 us
    all_gather x2, blocking collectives, scan_devices(): pieces = lax.all_gather(pieces, 'c')  3.99 us
    pallas_call x5, Pallas kernels, call(): pl.pallas_call(kernel, out_shape=[jax.ShapeDtypeStruct(shape, dtype) for...  3.84 us
  transfers between devices with their start and end apart: 6, of which 0 were waited for; matrix products, arithmetic and copies ran while one was open for 0% of the time, Pallas kernels for 0%

profile of v5, /device:TPU:1, one launch (start us, length us, event | category | flops | bytes accessed | tf_op | source)
XLA Modules:
  0.0 91.2 jit_solution(17388474449419684010)
XLA Ops:
  0.6 1.2 %shard_map.76 = (bf16[128,256]{1,0:T(8,128)(2,1)S(1)}, bf16[128,256]{1,0:T(8,128)(2,1)S(1)}, bf16[128,256]{1,0:T(8,128)(2,1)S(1)}, bf16[128,256]{1,0:T(8,128)(2,...) custom-call(s32[1]{0:T(128)} %bitcast.10.at_ref, bf16[128,256]{1,0:T(8,128)(2,1)} %k_in.1, ...), custom_call_target="tpu_custom_call" | custom-call | tf_op jit(solution)/shard_map/pallas_call | solution.py:168
  1.8 15.8 %all-gather = f32[4,128,128]{2,1,0:T(8,128)S(1)} all-gather(f32[2,128,128]{2,1,0:T(8,128)S(1)} %get-tuple-element.60), channel_id=2, replica_groups=mesh['x'=4,'zb'=4,'zp'=4,'c'=2,'h'=8] {'c'}, dimensions={0}, use_global_device_ids=true | all-gather | bytes 393216 | tf_op jit(solution)/shard_map/all_gather | solution.py:183
  17.6 9.8 %conditional.4 = ((f32[4,4,16,128]{3,2,1,0:T(8,128)S(1)}, f32[4,16,128]{2,1,0:T(8,128)S(1)})) conditional(s32[]{:T(128)} %convert_element_type.9, () %tuple.34, f32[2,2,128,128]{3,2,1,0:T(8,128)S(1)} %bitcast.22), branch_computations={%region_0.0_spmd, %region_1.0_spmd} | conditional | flops 32768 | bytes 655368 | solution.py:192
  17.6 9.8 %all_to_all.16 = f32[16,16,128]{2,1,0:T(8,128)S(1)} all-to-all(f32[16,16,128]{2,1,0:T(8,128)S(1)} %bitcast.30), channel_id=1, replica_groups=mesh['x'=4,'zb'=4,'zp'=4,'c'=2,'h'=8] {'x','zp'}, dimensions={0} | all-to-all | bytes 262144 | tf_op jit(solution)/shard_map/cond/branch_1_fun/all_to_all | solution.py:186
  27.5 1.3 %collective-permute-start.2 = (f32[4,16,128]{2,1,0:T(8,128)S(1)}, f32[4,16,128]{2,1,0:T(8,128)S(1)}, u32[]{:S(2)}, u32[]{:S(2)}) collective-permute-start(f32[4,16,128]{2,1,0:T(8,128)S(1)} %get-tuple-element.62), channel_id=1, source_target_pairs={{8,192},{72,0},{136,64},{200,128},{9,193},{73,1},{137,65},{201,129... | collective-permute-start | bytes 98312 | tf_op jit(solution)/shard_map/ppermute | solution.py:195
  28.8 1.3 %collective-permute-start.1 = (f32[4,16,128]{2,1,0:T(8,128)S(1)}, f32[4,16,128]{2,1,0:T(8,128)S(1)}, u32[]{:S(2)}, u32[]{:S(2)}) collective-permute-start(f32[4,16,128]{2,1,0:T(8,128)S(1)} %get-tuple-element.62), channel_id=1, source_target_pairs={{8,64},{72,128},{136,192},{200,0},{9,65},{73,129},{137,193},{201,1... | collective-permute-start | bytes 98312 | tf_op jit(solution)/shard_map/ppermute | solution.py:195
  30.1 1.3 %collective-permute-start = (f32[4,16,128]{2,1,0:T(8,128)S(1)}, f32[4,16,128]{2,1,0:T(8,128)S(1)}, u32[]{:S(2)}, u32[]{:S(2)}) collective-permute-start(f32[4,16,128]{2,1,0:T(8,128)S(1)} %get-tuple-element.62), channel_id=1, source_target_pairs={{8,128},{72,192},{136,0},{200,64},{9,129},{73,193},{137,1},{201,65... | collective-permute-start | bytes 98312 | tf_op jit(solution)/shard_map/ppermute | solution.py:195
  31.4 2.0 %all-gather.1 = f32[8,4,16,128]{3,2,1,0:T(8,128)S(1)} all-gather(f32[4,4,16,128]{3,2,1,0:T(8,128)S(1)} %get-tuple-element.61), channel_id=3, replica_groups=mesh['x'=4,'zb'=4,'zp'=4,'c'=2,'h'=8] {'c'}, dimensions={0}, use_global_device_ids=true | all-gather | bytes 393216 | tf_op jit(solution)/shard_map/all_gather | solution.py:198
  33.4 0.0 collective-permute-done.2
  33.4 0.0 collective-permute-done.1
  33.4 0.0 collective-permute-done
  33.4 21.4 %all-gather.2 = f32[4,128,128]{2,1,0:T(8,128)S(1)} all-gather(f32[2,128,128]{2,1,0:T(8,128)S(1)} %get-tuple-element.80), channel_id=4, replica_groups=mesh['x'=4,'zb'=4,'zp'=4,'c'=2,'h'=8] {'c'}, dimensions={0}, use_global_device_ids=true | all-gather | bytes 393216 | tf_op jit(solution)/shard_map/all_gather | solution.py:206
  54.8 1.2 %shard_map.77 = (f32[2,128,128]{2,1,0:T(8,128)S(1)}, f32[2,128,128]{2,1,0:T(8,128)S(1)}, f32[2,128,128]{2,1,0:T(8,128)S(1)}, f32[2,128,128]{2,1,0:T(8,128)S(1)}) custom-call(s32[1]{0:T(128)} %bitcast.10.at_ref, bf16[128,256]{1,0:T(8,128)(2,1)S(1)} %get-tuple-element.55.q_ref.refs_0_, bf16[128,256]{1,0:T(8,128)(2,1)S(1)} %get-tuple-element.56.k_ref.refs_1_, ...), custom_call_target="tpu_custom_call" | custom-call | tf_op jit(solution)/shard_map/pallas_call | solution.py:168
  56.0 2.0 %all-gather.3 = f32[4,128,128]{2,1,0:T(8,128)S(1)} all-gather(f32[2,128,128]{2,1,0:T(8,128)S(1)} %get-tuple-element.66), channel_id=5, replica_groups=mesh['x'=4,'zb'=4,'zp'=4,'c'=2,'h'=8] {'c'}, dimensions={0}, use_global_device_ids=true | all-gather | bytes 393216 | tf_op jit(solution)/shard_map/all_gather | solution.py:183
  58.0 9.8 %conditional.6 = ((f32[4,4,16,128]{3,2,1,0:T(8,128)S(1)}, f32[4,16,128]{2,1,0:T(8,128)S(1)})) conditional(s32[]{:T(128)} %convert_element_type.9, () %tuple.37, f32[2,2,128,128]{3,2,1,0:T(8,128)S(1)} %bitcast.24), branch_computations={%region_4.0_spmd, %region_5.0_spmd} | conditional | flops 32768 | bytes 655368 | solution.py:192
  58.0 9.8 %all_to_all.18 = f32[16,16,128]{2,1,0:T(8,128)S(1)} all-to-all(f32[16,16,128]{2,1,0:T(8,128)S(1)} %bitcast.31), channel_id=1, replica_groups=mesh['x'=4,'zb'=4,'zp'=4,'c'=2,'h'=8] {'x','zp'}, dimensions={0} | all-to-all | bytes 262144 | tf_op jit(solution)/shard_map/cond/branch_1_fun/all_to_all | solution.py:186
  67.8 1.3 %collective-permute-start.5 = (f32[4,16,128]{2,1,0:T(8,128)S(1)}, f32[4,16,128]{2,1,0:T(8,128)S(1)}, u32[]{:S(2)}, u32[]{:S(2)}) collective-permute-start(f32[4,16,128]{2,1,0:T(8,128)S(1)} %get-tuple-element.68), channel_id=1, source_target_pairs={{8,192},{72,0},{136,64},{200,128},{9,193},{73,1},{137,65},{201,129... | collective-permute-start | bytes 98312 | tf_op jit(solution)/shard_map/ppermute | solution.py:195
  69.1 1.3 %collective-permute-start.4 = (f32[4,16,128]{2,1,0:T(8,128)S(1)}, f32[4,16,128]{2,1,0:T(8,128)S(1)}, u32[]{:S(2)}, u32[]{:S(2)}) collective-permute-start(f32[4,16,128]{2,1,0:T(8,128)S(1)} %get-tuple-element.68), channel_id=1, source_target_pairs={{8,64},{72,128},{136,192},{200,0},{9,65},{73,129},{137,193},{201,1... | collective-permute-start | bytes 98312 | tf_op jit(solution)/shard_map/ppermute | solution.py:195
  70.4 1.3 %collective-permute-start.3 = (f32[4,16,128]{2,1,0:T(8,128)S(1)}, f32[4,16,128]{2,1,0:T(8,128)S(1)}, u32[]{:S(2)}, u32[]{:S(2)}) collective-permute-start(f32[4,16,128]{2,1,0:T(8,128)S(1)} %get-tuple-element.68), channel_id=1, source_target_pairs={{8,128},{72,192},{136,0},{200,64},{9,129},{73,193},{137,1},{201,65... | collective-permute-start | bytes 98312 | tf_op jit(solution)/shard_map/ppermute | solution.py:195
  71.7 2.0 %all-gather.4 = f32[8,4,16,128]{3,2,1,0:T(8,128)S(1)} all-gather(f32[4,4,16,128]{3,2,1,0:T(8,128)S(1)} %get-tuple-element.67), channel_id=6, replica_groups=mesh['x'=4,'zb'=4,'zp'=4,'c'=2,'h'=8] {'c'}, dimensions={0}, use_global_device_ids=true | all-gather | bytes 393216 | tf_op jit(solution)/shard_map/all_gather | solution.py:198
  73.7 0.0 collective-permute-done.5
  73.7 0.0 collective-permute-done.4
  73.7 0.0 collective-permute-done.3
  73.8 15.9 %all-gather.5 = f32[4,128,128]{2,1,0:T(8,128)S(1)} all-gather(f32[2,128,128]{2,1,0:T(8,128)S(1)} %get-tuple-element.82), channel_id=7, replica_groups=mesh['x'=4,'zb'=4,'zp'=4,'c'=2,'h'=8] {'c'}, dimensions={0}, use_global_device_ids=true | all-gather | bytes 393216 | tf_op jit(solution)/shard_map/all_gather | solution.py:206
  89.7 1.5 %shard_map.78 = (f32[128,256]{1,0:T(8,128)}, f32[128,256]{1,0:T(8,128)}, f32[128,256]{1,0:T(8,128)}) custom-call(s32[1]{0:T(128)} %bitcast.10.at_ref, bf16[128,256]{1,0:T(8,128)(2,1)S(1)} %get-tuple-element.55.q_ref.refs_0_, bf16[128,256]{1,0:T(8,128)(2,1)S(1)} %get-tuple-element.56.k_ref.refs_1_, bf16[128,256]{1,0:T(8,128)(2,1)S(1)} %get-tuple-element.57.v_ref.refs_2_, ...), custom_call_target="tpu_custom_call" | custom-call | tf_op jit(solution)/shard_map/pallas_call | solution.py:168
  (8 shorter events, 0.1 us)
Async XLA Ops:
  27.5 5.9 %collective-permute-start.2 = (f32[4,16,128]{2,1,0:T(8,128)S(1)}, f32[4,16,128]{2,1,0:T(8,128)S(1)}, u32[]{:S(2)}, u32[]{:S(2)}) collective-permute-start(f32[4,16,128]{2,1,0:T(8,128)S(1)} %get-tuple-element.62), channel_id=1, source_target_pairs={{8,192},{72,0},{136,64},{200,128},{9,193},{73,1},{137,65},{201,129... | collective-permute-start | bytes 98312 | tf_op jit(solution)/shard_map/ppermute | solution.py:195
  28.8 4.6 %collective-permute-start.1 = (f32[4,16,128]{2,1,0:T(8,128)S(1)}, f32[4,16,128]{2,1,0:T(8,128)S(1)}, u32[]{:S(2)}, u32[]{:S(2)}) collective-permute-start(f32[4,16,128]{2,1,0:T(8,128)S(1)} %get-tuple-element.62), channel_id=1, source_target_pairs={{8,64},{72,128},{136,192},{200,0},{9,65},{73,129},{137,193},{201,1... | collective-permute-start | bytes 98312 | tf_op jit(solution)/shard_map/ppermute | solution.py:195
  30.1 3.3 %collective-permute-start = (f32[4,16,128]{2,1,0:T(8,128)S(1)}, f32[4,16,128]{2,1,0:T(8,128)S(1)}, u32[]{:S(2)}, u32[]{:S(2)}) collective-permute-start(f32[4,16,128]{2,1,0:T(8,128)S(1)} %get-tuple-element.62), channel_id=1, source_target_pairs={{8,128},{72,192},{136,0},{200,64},{9,129},{73,193},{137,1},{201,65... | collective-permute-start | bytes 98312 | tf_op jit(solution)/shard_map/ppermute | solution.py:195
  67.8 5.9 %collective-permute-start.5 = (f32[4,16,128]{2,1,0:T(8,128)S(1)}, f32[4,16,128]{2,1,0:T(8,128)S(1)}, u32[]{:S(2)}, u32[]{:S(2)}) collective-permute-start(f32[4,16,128]{2,1,0:T(8,128)S(1)} %get-tuple-element.68), channel_id=1, source_target_pairs={{8,192},{72,0},{136,64},{200,128},{9,193},{73,1},{137,65},{201,129... | collective-permute-start | bytes 98312 | tf_op jit(solution)/shard_map/ppermute | solution.py:195
  69.1 4.6 %collective-permute-start.4 = (f32[4,16,128]{2,1,0:T(8,128)S(1)}, f32[4,16,128]{2,1,0:T(8,128)S(1)}, u32[]{:S(2)}, u32[]{:S(2)}) collective-permute-start(f32[4,16,128]{2,1,0:T(8,128)S(1)} %get-tuple-element.68), channel_id=1, source_target_pairs={{8,64},{72,128},{136,192},{200,0},{9,65},{73,129},{137,193},{201,1... | collective-permute-start | bytes 98312 | tf_op jit(solution)/shard_map/ppermute | solution.py:195
  70.4 3.3 %collective-permute-start.3 = (f32[4,16,128]{2,1,0:T(8,128)S(1)}, f32[4,16,128]{2,1,0:T(8,128)S(1)}, u32[]{:S(2)}, u32[]{:S(2)}) collective-permute-start(f32[4,16,128]{2,1,0:T(8,128)S(1)} %get-tuple-element.68), channel_id=1, source_target_pairs={{8,128},{72,192},{136,0},{200,64},{9,129},{73,193},{137,1},{201,65... | collective-permute-start | bytes 98312 | tf_op jit(solution)/shard_map/ppermute | solution.py:195

commit v6 on v5

v6 whole, which is shorter than its diff:
```python
import functools

import jax
import jax.numpy as jnp
from jax import lax
from jax.experimental import pallas as pl
from jax.experimental.pallas import tpu as pltpu
from jax.sharding import Mesh, PartitionSpec as P

HD = 128
HEADS = 2
F32 = jnp.float32
BF16 = jnp.bfloat16
VMEM = pl.BlockSpec(memory_space=pltpu.VMEM)
SMEM = pl.BlockSpec(memory_space=pltpu.SMEM)
HBM = pl.BlockSpec(memory_space=pltpu.HBM)
NN = (((1,), (0,)), ((), ()))
NT = (((1,), (1,)), ((), ()))
TN = (((0,), (0,)), ((), ()))
NEAR = ("x", "zp")


def halves(wide):
    high = wide.astype(BF16)
    low = (wide - high.astype(F32)).astype(BF16)
    return high, low


def one(left, right, dims):
    return lax.dot_general(left, right, dims, preferred_element_type=F32)


def product(left, right, dims):
    if not isinstance(left, tuple):
        return one(left, right[0], dims) + one(left, right[1], dims)
    if not isinstance(right, tuple):
        return one(left[0], right, dims) + one(left[1], right, dims)
    return one(left[0], right[0], dims) + (one(left[0], right[1], dims) + one(left[1], right[0], dims))


def feature(raw):
    wide = raw.astype(F32)
    return jnp.where(wide > 0, wide + 1.0, jnp.exp(jnp.minimum(wide, 0.0)))


def slope(raw):
    wide = raw.astype(F32)
    return jnp.where(wide > 0, 1.0, jnp.exp(jnp.minimum(wide, 0.0)))


def causal(size):
    row = lax.broadcasted_iota(jnp.int32, (size, size), 0)
    column = lax.broadcasted_iota(jnp.int32, (size, size), 1)
    return row >= column


def features_of(head):
    return slice(head * HD, head * HD + HD)


def local_kernel(at_ref, k_in, v_in, q_in, g_in, gain_in, k_ref, v_ref, q_ref, first_ref, g_ref, gain_ref, sems):
    pairs = ((k_in, k_ref), (v_in, v_ref), (g_in, g_ref), (gain_in, gain_ref), (q_in, q_ref))
    copies = [pltpu.make_async_copy(start, end, sems.at[place]) for place, (start, end) in enumerate(pairs)]
    for copy in copies:
        copy.start()
    copies[0].wait()
    copies[1].wait()
    for head in range(HEADS):
        part = features_of(head)
        first_ref[head] = product(halves(feature(k_ref[:, part])), v_ref[:, part], TN)
    for copy in copies[2:]:
        copy.wait()
    for head in range(HEADS):
        first_ref[HEADS + head] = gain_ref[head : head + 1, :] * g_ref[:, features_of(head)].astype(F32)


def core_of(at_ref):
    return lax.rem(at_ref[0], 2)


def total_kernel(pieces_ref, copy_ref, out_ref):
    copy_ref[...] = pieces_ref[...]
    total = pieces_ref[:, 0]
    for place in range(1, pieces_ref.shape[1]):
        total = total + pieces_ref[:, place]
    out_ref[...] = total


def total_and_pack_kernel(pieces_ref, prefix_ref, grad_ref, third_ref, out_ref):
    x_size, place_size, rows = pieces_ref.shape[:3]
    each = HD // rows
    for x in range(x_size):
        total = pieces_ref[x, 0]
        for place in range(1, place_size):
            total = total + pieces_ref[x, place]
        out_ref[x] = total
        for place in range(place_size):
            member = x * place_size + place
            third_ref[member // each, pl.ds(member % each * rows, rows), :] = pieces_ref[x, place]
    third_ref[HEADS : 2 * HEADS] = prefix_ref[...]
    third_ref[2 * HEADS :] = grad_ref[...]


def prefix_kernel(backward, steps, place_size, source, at_ref, pieces_ref, *refs):
    far_refs, out_ref = refs[:-1], refs[-1]
    x_size, rows = far_refs[0].shape[:2]
    each = HD // rows
    blocks = len(steps) + 1
    block = lax.rem(lax.div(at_ref[0], 2 * place_size), blocks)
    base = jnp.zeros((rows, HD), F32)
    for x in range(x_size)[:: -1 if backward else 1]:
        so_far = row = base
        for step, far_ref in zip(steps, far_refs):
            other = lax.rem(block + blocks - step, blocks)
            total = far_ref[x]
            row = row + total
            so_far = so_far + jnp.where(other > block if backward else other < block, total, 0.0)
        for place in range(place_size)[:: -1 if backward else 1]:
            member = x * place_size + place
            piece = pieces_ref[source, member // each, pl.ds(member % each * rows, rows), :]
            out_ref[x, place] = so_far
            so_far = so_far + piece
            row = row + piece
        base = row


def scores_kernel(q_ref, k_ref, v_ref, pieces_ref, scores_ref, second_ref):
    mask = causal(q_ref.shape[0])
    second_ref[:HEADS] = pieces_ref[...]
    for head in range(HEADS):
        part = features_of(head)
        query = halves(feature(q_ref[:, part]))
        key = halves(feature(k_ref[:, part]))
        scores = jnp.where(mask, product(query, key, NT), 0.0)
        scores_ref[head] = scores
        second_ref[HEADS + head] = product(halves(scores), v_ref[:, part], NN)
        second_ref[2 * HEADS + head] = q_ref[:, part].astype(F32)


def forward_kernel(first_ref, second_ref, prefix_ref, grad0_ref, grad1_ref, chip_ref, other_ref):
    for head in range(HEADS):
        states = []
        for core in range(2):
            query = halves(feature(second_ref[core, 2 * HEADS + head]))
            prefix = prefix_ref[head]
            if core:
                prefix = prefix + first_ref[0, head]
            output = second_ref[core, HEADS + head] + product(query, halves(prefix), NN)
            inverse = lax.rsqrt(jnp.mean(output * output, axis=-1, keepdims=True) + 1e-06)
            normed = output * inverse
            scaled = first_ref[core, HEADS + head]
            grad = inverse * (scaled - normed * jnp.mean(scaled * normed, axis=-1, keepdims=True))
            (grad0_ref, grad1_ref)[core][head] = grad
            states.append(product(query, halves(grad), TN))
        chip_ref[head] = states[0] + states[1]
        other_ref[head] = states[1]


def backward_kernel(at_ref, *refs):
    q_ref, k_ref, v_ref, scores_ref, grad_ref, other_ref, first_ref, third_ref, last_ref = refs[:9]
    dq_out, dk_out, dv_out, dq_ref, dk_ref, dv_ref, sems = refs[9:]
    mask = causal(q_ref.shape[0])
    late = core_of(at_ref) == 1
    copies = []

    def write(start, end):
        copies.append(pltpu.make_async_copy(start, end, sems.at[len(copies)]))
        copies[-1].start()

    heads = range(HEADS)
    grads = [halves(jnp.where(late, third_ref[0, 2 * HEADS + head], grad_ref[head])) for head in heads]
    prefixes = [halves(third_ref[0, HEADS + head] + jnp.where(late, first_ref[0, head], 0.0)) for head in heads]
    suffixes = [halves(last_ref[1, head] + jnp.where(late, 0.0, other_ref[head])) for head in heads]
    keys = [halves(feature(k_ref[:, features_of(head)])) for head in heads]
    grad_scores = []
    for head in heads:
        part = features_of(head)
        grad_scores.append(halves(jnp.where(mask, product(grads[head], v_ref[:, part], NT), 0.0)))
        dq = product(grad_scores[head], keys[head], NN) + product(grads[head], prefixes[head], NT)
        dq_ref[:, part] = slope(q_ref[:, part]) * dq
    write(dq_ref, dq_out)
    for head in heads:
        part = features_of(head)
        query = halves(feature(q_ref[:, part]))
        dk = product(grad_scores[head], query, TN) + product(v_ref[:, part], suffixes[head], NT)
        dk_ref[:, part] = slope(k_ref[:, part]) * dk
    write(dk_ref, dk_out)
    for head in heads:
        part = features_of(head)
        dv = product(halves(scores_ref[head]), grads[head], TN) + product(keys[head], suffixes[head], NN)
        dv_ref[:, part] = dv
    write(dv_ref, dv_out)
    for copy in copies:
        copy.wait()


def call(kernel, outs, *operands, scalars=0, inputs=VMEM, outputs=VMEM, scratch=()):
    return pl.pallas_call(
        kernel,
        out_shape=[jax.ShapeDtypeStruct(shape, dtype) for shape, dtype in outs],
        in_specs=[SMEM] * scalars + [inputs] * (len(operands) - scalars),
        out_specs=[outputs] * len(outs),
        scratch_shapes=scratch,
        compiler_params=pltpu.CompilerParams(vmem_limit_bytes=8 << 20),
    )(*operands)


def body(query, key, value, gain, grad_out):
    tokens = query.shape[0]
    at = lax.axis_index(("x", "zb", "zp", "c")).reshape(1)
    core = lax.axis_index("c")
    blocks, x_size, place_size = lax.axis_size("zb"), lax.axis_size("x"), lax.axis_size("zp")
    members = x_size * place_size
    piece = (HEADS * HD // members, HD)
    flat, near, far = (members,) + piece, (x_size, place_size) + piece, (x_size,) + piece
    state, three, wide = (HEADS, HD, HD), (3 * HEADS, HD, HD), (tokens, HEADS * HD)
    steps = sorted(range(1, blocks), key=lambda step: min(step, blocks - step))

    def within(pieces, shape):
        return lax.all_to_all(pieces.reshape(flat), NEAR, 0, 0).reshape(shape)

    def to_blocks(total, source):
        ends = [(step, [(2 * block + source, 2 * ((block + step) % blocks) + 1 - source) for block in range(blocks)]) for step in steps]
        return [lax.ppermute(total, ("zb", "c"), pairs) for step, pairs in ends]

    def none(*shapes):
        return lambda *operands: tuple(jnp.zeros(shape, F32) for shape in shapes)

    def sums(backward, source, pieces, totals):
        kernel = functools.partial(prefix_kernel, backward, steps, place_size, source)
        return within(call(kernel, [(near, F32)], at, pieces, *totals, scalars=1)[0], state)

    given = (key, value, query, grad_out, gain.reshape(HEADS, HD))
    k, v, q, first = call(
        local_kernel,
        [(wide, BF16)] * 3 + [((2 * HEADS, HD, HD), F32)],
        at,
        *(pltpu.with_memory_space_constraint(array, pltpu.HBM) for array in given),
        scalars=1,
        inputs=HBM,
        scratch=[pltpu.VMEM(wide, BF16), pltpu.VMEM((HEADS, HD), F32), pltpu.SemaphoreType.DMA((5,))],
    )
    firsts = lax.all_gather(first, "c")

    def start(firsts):
        chip = firsts[0, :HEADS] + firsts[1, :HEADS]
        return tuple(call(total_kernel, [(near, F32), (far, F32)], within(chip, near)))

    pieces, total = lax.cond(core == 1, start, none(near, far), firsts)
    totals = to_blocks(total, 1)
    scores, second = call(scores_kernel, [(state, F32), (three, F32)], q, k, v, pieces.reshape(state))
    seconds = lax.all_gather(second, "c")

    def middle(firsts, seconds, totals):
        prefix = sums(False, 1, seconds, totals)
        grad0, grad1, chip, other = call(forward_kernel, [(state, F32)] * 4, firsts, seconds, prefix)
        third, total = call(total_and_pack_kernel, [(three, F32), (far, F32)], within(chip, near), prefix, grad1)
        return third, total, grad0, other

    third, total, grad, other = lax.cond(core == 0, middle, none(three, far, state, state), firsts, seconds, totals)
    totals = to_blocks(total, 0)
    thirds = lax.all_gather(third, "c")

    def end(thirds, totals):
        return (sums(True, 0, thirds, totals),)

    (last,) = lax.cond(core == 1, end, none(state), thirds, totals)
    lasts = lax.all_gather(last, "c")
    return tuple(
        call(
            backward_kernel,
            [(wide, F32)] * 3,
            *(at, q, k, v, scores, grad, other, firsts, thirds, lasts),
            scalars=1,
            outputs=HBM,
            scratch=[pltpu.VMEM(wide, F32)] * 3 + [pltpu.SemaphoreType.DMA((3,))],
        )
    )


def over(devices):
    mesh = Mesh(devices, ("x", "zb", "zp", "c", "h"))
    placed = P(("x", "zb", "zp", "c"), "h")
    return jax.shard_map(
        body,
        mesh=mesh,
        in_specs=(placed, placed, placed, P("h"), placed),
        out_specs=(placed, placed, placed),
        check_vma=False,
    )


def solution(mesh):
    seq, head = mesh.devices.shape
    return over(mesh.devices.reshape(4, 4, seq // 32, 2, head))
```

time: 91.6 us -> 87 us (0.950)
  blocking collectives: 78.7 us -> 72.4 us
  waiting for transfers between devices: 0.02 us -> 2 us
    all_gather x6 -> x4, blocking collectives: 59.1 us -> 52.7 us  [the longest x1 32.4 us: body(): thirds = lax.all_gather(third, 'c')]
    ppermute x6, waiting for transfers between devices: 0.02 us -> 2 us  [to_blocks(): return [lax.ppermute(total, ('zb', 'c'), pairs) for step, pairs in ends]]
  transfers between devices with their start and end apart: 6 -> 6, of which waited for: 0 -> 3; matrix products, arithmetic and copies ran while one was open for 0% -> 0% of each run, Pallas kernels for 0% -> 1%
where the time goes in v6:
time: 87 us; the launch traced here: 86.3 us
  blocking collectives  72.4 us (83%)
  starting transfers between devices  7.75 us (9%)
  Pallas kernels  3.31 us (4%)
  waiting for transfers between devices  2 us (2%)
    all_gather x1, blocking collectives, body(): thirds = lax.all_gather(third, 'c')  32.4 us
    all_to_all x2, blocking collectives, within(): return lax.all_to_all(pieces.reshape(flat), NEAR, 0, 0).reshape(shape)  19.7 us
    all_gather x1, blocking collectives, body(): firsts = lax.all_gather(first, 'c')  16 us
    ppermute x6, starting transfers between devices, to_blocks(): return [lax.ppermute(total, ('zb', 'c'), pairs) for step, pairs in ends]  7.75 us
    pallas_call x5, Pallas kernels, call(): pl.pallas_call(kernel, out_shape=[jax.ShapeDtypeStruct(shape, dtype) for...  3.31 us
    all_gather x1, blocking collectives, body(): seconds = lax.all_gather(second, 'c')  2.37 us
    ppermute x6, waiting for transfers between devices, to_blocks(): return [lax.ppermute(total, ('zb', 'c'), pairs) for step, pairs in ends]  2 us
    all_gather x1, blocking collectives, body(): lasts = lax.all_gather(last, 'c')  1.98 us
  transfers between devices with their start and end apart: 6, of which 3 were waited for; matrix products, arithmetic and copies ran while one was open for 0% of the time, Pallas kernels for 1%

profile of v6, /device:TPU:1, one launch (start us, length us, event | category | flops | bytes accessed | tf_op | source)
XLA Modules:
  0.0 86.3 jit_solution(13154413924157448969)
XLA Ops:
  0.6 1.2 %shard_map.76 = (bf16[128,256]{1,0:T(8,128)(2,1)S(1)}, bf16[128,256]{1,0:T(8,128)(2,1)S(1)}, bf16[128,256]{1,0:T(8,128)(2,1)S(1)}, f32[4,128,128]{2,1,0:T(8,128)S(1)}) custom-call(s32[1]{0:T(128)} %bitcast.10.at_ref, bf16[128,256]{1,0:T(8,128)(2,1)} %k_in.1, bf16[128,256]{1,0:T(8,128)(2,1)} %v_in.1, bf16[128,256]{1,0:T(8,128)(2,1)} %q_in.1, ...), custom_call_target="tpu_custom_call" | custom-call | tf_op jit(solution)/shard_map/pallas_call | solution.py:198
  1.8 16.0 %all-gather = f32[8,128,128]{2,1,0:T(8,128)S(1)} all-gather(f32[4,128,128]{2,1,0:T(8,128)S(1)} %get-tuple-element.66), channel_id=2, replica_groups=mesh['x'=4,'zb'=4,'zp'=4,'c'=2,'h'=8] {'c'}, dimensions={0}, use_global_device_ids=true | all-gather | bytes 786432 | tf_op jit(solution)/shard_map/all_gather | solution.py:243
  17.8 9.8 %conditional.3 = (f32[4,16,128]{2,1,0:T(8,128)S(1)}, f32[2,128,128]{2,1,0:T(8,128)S(1)}) conditional(s32[]{:T(128)} %convert_element_type.7, () %tuple.31, f32[2,4,128,128]{3,2,1,0:T(8,128)S(1)} %bitcast.27), branch_computations={%region_0.0_spmd, %region_1.0_spmd} | conditional | flops 32768 | bytes 655376 | solution.py:249
  17.8 9.8 %all_to_all.16 = f32[16,16,128]{2,1,0:T(8,128)S(1)} all-to-all(f32[16,16,128]{2,1,0:T(8,128)S(1)} %bitcast.31), channel_id=1, replica_groups=mesh['x'=4,'zb'=4,'zp'=4,'c'=2,'h'=8] {'x','zp'}, dimensions={0} | all-to-all | bytes 262144 | tf_op jit(solution)/shard_map/cond/branch_1_fun/all_to_all | solution.py:220
  27.6 1.3 %collective-permute-start.2 = (f32[4,16,128]{2,1,0:T(8,128)S(1)}, f32[4,16,128]{2,1,0:T(8,128)S(1)}, u32[]{:S(2)}, u32[]{:S(2)}) collective-permute-start(f32[4,16,128]{2,1,0:T(8,128)S(1)} %get-tuple-element.70), channel_id=1, source_target_pairs={{8,128},{72,192},{136,0},{200,64},{9,129},{73,193},{137,1},{201,65... | collective-permute-start | bytes 98312 | tf_op jit(solution)/shard_map/ppermute | solution.py:224
  28.9 1.3 %collective-permute-start.1 = (f32[4,16,128]{2,1,0:T(8,128)S(1)}, f32[4,16,128]{2,1,0:T(8,128)S(1)}, u32[]{:S(2)}, u32[]{:S(2)}) collective-permute-start(f32[4,16,128]{2,1,0:T(8,128)S(1)} %get-tuple-element.70), channel_id=1, source_target_pairs={{8,192},{72,0},{136,64},{200,128},{9,193},{73,1},{137,65},{201,129... | collective-permute-start | bytes 98312 | tf_op jit(solution)/shard_map/ppermute | solution.py:224
  30.2 1.3 %collective-permute-start = (f32[4,16,128]{2,1,0:T(8,128)S(1)}, f32[4,16,128]{2,1,0:T(8,128)S(1)}, u32[]{:S(2)}, u32[]{:S(2)}) collective-permute-start(f32[4,16,128]{2,1,0:T(8,128)S(1)} %get-tuple-element.70), channel_id=1, source_target_pairs={{8,64},{72,128},{136,192},{200,0},{9,65},{73,129},{137,193},{201,1... | collective-permute-start | bytes 98312 | tf_op jit(solution)/shard_map/ppermute | solution.py:224
  31.5 0.6 shard_map.77
  32.2 2.4 %all-gather.1 = f32[12,128,128]{2,1,0:T(8,128)S(1)} all-gather(f32[6,128,128]{2,1,0:T(8,128)S(1)} %get-tuple-element.69), channel_id=3, replica_groups=mesh['x'=4,'zb'=4,'zp'=4,'c'=2,'h'=8] {'c'}, dimensions={0}, use_global_device_ids=true | all-gather | bytes 1179648 | tf_op jit(solution)/shard_map/all_gather | solution.py:252
  34.5 0.0 collective-permute-done.2
  34.5 0.0 collective-permute-done.1
  34.6 0.0 collective-permute-done
  34.6 0.1 conditional.4
  34.7 1.3 %collective-permute-start.5 = (f32[4,16,128]{2,1,0:T(8,128)S(1)}, f32[4,16,128]{2,1,0:T(8,128)S(1)}, u32[]{:S(2)}, u32[]{:S(2)}) collective-permute-start(f32[4,16,128]{2,1,0:T(8,128)S(1)} %get-tuple-element.74), channel_id=1, source_target_pairs={{0,136},{64,200},{128,8},{192,72},{1,137},{65,201},{129,9},{193,73... | collective-permute-start | bytes 98312 | tf_op jit(solution)/shard_map/ppermute | solution.py:224
  36.0 1.3 %collective-permute-start.4 = (f32[4,16,128]{2,1,0:T(8,128)S(1)}, f32[4,16,128]{2,1,0:T(8,128)S(1)}, u32[]{:S(2)}, u32[]{:S(2)}) collective-permute-start(f32[4,16,128]{2,1,0:T(8,128)S(1)} %get-tuple-element.74), channel_id=1, source_target_pairs={{0,200},{64,8},{128,72},{192,136},{1,201},{65,9},{129,73},{193,137... | collective-permute-start | bytes 98312 | tf_op jit(solution)/shard_map/ppermute | solution.py:224
  37.3 1.3 %collective-permute-start.3 = (f32[4,16,128]{2,1,0:T(8,128)S(1)}, f32[4,16,128]{2,1,0:T(8,128)S(1)}, u32[]{:S(2)}, u32[]{:S(2)}) collective-permute-start(f32[4,16,128]{2,1,0:T(8,128)S(1)} %get-tuple-element.74), channel_id=1, source_target_pairs={{0,72},{64,136},{128,200},{192,8},{1,73},{65,137},{129,201},{193,9... | collective-permute-start | bytes 98312 | tf_op jit(solution)/shard_map/ppermute | solution.py:224
  38.6 32.4 %all-gather.2 = f32[12,128,128]{2,1,0:T(8,128)S(1)} all-gather(f32[6,128,128]{2,1,0:T(8,128)S(1)} %get-tuple-element.73), channel_id=4, replica_groups=mesh['x'=4,'zb'=4,'zp'=4,'c'=2,'h'=8] {'c'}, dimensions={0}, use_global_device_ids=true | all-gather | bytes 1179648 | tf_op jit(solution)/shard_map/all_gather | solution.py:262
  71.0 0.6 collective-permute-done.5
  71.6 1.1 %collective-permute-done.4 = f32[4,16,128]{2,1,0:T(8,128)S(1)} collective-permute-done((f32[4,16,128]{2,1,0:T(8,128)S(1)}, f32[4,16,128]{2,1,0:T(8,128)S(1)}, u32[]{:S(2)}, u32[]{:S(2)}) %collective-permute-start.4) | collective-permute-done | bytes 32800 | tf_op jit(solution)/shard_map/ppermute | solution.py:224
  72.7 0.2 collective-permute-done.3
  73.0 9.9 %conditional.5 = (f32[2,128,128]{2,1,0:T(8,128)S(1)}) conditional(s32[]{:T(128)} %convert_element_type.7, () %tuple.34, (s32[1]{0:T(128)}, f32[2,6,128,128]{3,2,1,0:T(8,128)S(1)}, f32[4,16,128]{2,1,0:T(8,128)S(1)}, f32[4,16,128]{2,1,0:T(8,128)S(1)}, f32[4,16,128]{2,1,0:T(8,128)S(1)}) %tuple.42), branch_computations={%region_4.0_spmd, %region_5.0_spmd} | conditional | bytes 262152 | solution.py:267
  73.0 9.8 %all_to_all.19 = f32[16,16,128]{2,1,0:T(8,128)S(1)} all-to-all(f32[16,16,128]{2,1,0:T(8,128)S(1)} %bitcast.20), channel_id=1, replica_groups=mesh['x'=4,'zb'=4,'zp'=4,'c'=2,'h'=8] {'x','zp'}, dimensions={0} | all-to-all | bytes 262144 | tf_op jit(solution)/shard_map/cond/branch_1_fun/all_to_all | solution.py:220
  82.9 2.0 %all-gather.3 = f32[4,128,128]{2,1,0:T(8,128)S(1)} all-gather(f32[2,128,128]{2,1,0:T(8,128)S(1)} %get-tuple-element.88), channel_id=5, replica_groups=mesh['x'=4,'zb'=4,'zp'=4,'c'=2,'h'=8] {'c'}, dimensions={0}, use_global_device_ids=true | all-gather | bytes 393216 | tf_op jit(solution)/shard_map/all_gather | solution.py:268
  84.9 1.5 %shard_map.78 = (f32[128,256]{1,0:T(8,128)}, f32[128,256]{1,0:T(8,128)}, f32[128,256]{1,0:T(8,128)}) custom-call(s32[1]{0:T(128)} %bitcast.10.at_ref, bf16[128,256]{1,0:T(8,128)(2,1)S(1)} %get-tuple-element.63.q_ref.refs_0_, bf16[128,256]{1,0:T(8,128)(2,1)S(1)} %get-tuple-element.64.k_ref.refs_1_, bf16[128,256]{1,0:T(8,128)(2,1)S(1)} %get-tuple-element.65.v_ref.refs_2_, ...), custom_call_target="tpu_custom_call" | custom-call | tf_op jit(solution)/shard_map/pallas_call | solution.py:198
  (7 shorter events, 0.1 us)
Async XLA Ops:
  27.6 6.9 %collective-permute-start.2 = (f32[4,16,128]{2,1,0:T(8,128)S(1)}, f32[4,16,128]{2,1,0:T(8,128)S(1)}, u32[]{:S(2)}, u32[]{:S(2)}) collective-permute-start(f32[4,16,128]{2,1,0:T(8,128)S(1)} %get-tuple-element.70), channel_id=1, source_target_pairs={{8,128},{72,192},{136,0},{200,64},{9,129},{73,193},{137,1},{201,65... | collective-permute-start | bytes 98312 | tf_op jit(solution)/shard_map/ppermute | solution.py:224
  28.9 5.6 %collective-permute-start.1 = (f32[4,16,128]{2,1,0:T(8,128)S(1)}, f32[4,16,128]{2,1,0:T(8,128)S(1)}, u32[]{:S(2)}, u32[]{:S(2)}) collective-permute-start(f32[4,16,128]{2,1,0:T(8,128)S(1)} %get-tuple-element.70), channel_id=1, source_target_pairs={{8,192},{72,0},{136,64},{200,128},{9,193},{73,1},{137,65},{201,129... | collective-permute-start | bytes 98312 | tf_op jit(solution)/shard_map/ppermute | solution.py:224
  30.2 4.3 %collective-permute-start = (f32[4,16,128]{2,1,0:T(8,128)S(1)}, f32[4,16,128]{2,1,0:T(8,128)S(1)}, u32[]{:S(2)}, u32[]{:S(2)}) collective-permute-start(f32[4,16,128]{2,1,0:T(8,128)S(1)} %get-tuple-element.70), channel_id=1, source_target_pairs={{8,64},{72,128},{136,192},{200,0},{9,65},{73,129},{137,193},{201,1... | collective-permute-start | bytes 98312 | tf_op jit(solution)/shard_map/ppermute | solution.py:224
  34.7 37.0 %collective-permute-start.5 = (f32[4,16,128]{2,1,0:T(8,128)S(1)}, f32[4,16,128]{2,1,0:T(8,128)S(1)}, u32[]{:S(2)}, u32[]{:S(2)}) collective-permute-start(f32[4,16,128]{2,1,0:T(8,128)S(1)} %get-tuple-element.74), channel_id=1, source_target_pairs={{0,136},{64,200},{128,8},{192,72},{1,137},{65,201},{129,9},{193,73... | collective-permute-start | bytes 98312 | tf_op jit(solution)/shard_map/ppermute | solution.py:224
  36.0 36.8 %collective-permute-start.4 = (f32[4,16,128]{2,1,0:T(8,128)S(1)}, f32[4,16,128]{2,1,0:T(8,128)S(1)}, u32[]{:S(2)}, u32[]{:S(2)}) collective-permute-start(f32[4,16,128]{2,1,0:T(8,128)S(1)} %get-tuple-element.74), channel_id=1, source_target_pairs={{0,200},{64,8},{128,72},{192,136},{1,201},{65,9},{129,73},{193,137... | collective-permute-start | bytes 98312 | tf_op jit(solution)/shard_map/ppermute | solution.py:224
  37.3 35.7 %collective-permute-start.3 = (f32[4,16,128]{2,1,0:T(8,128)S(1)}, f32[4,16,128]{2,1,0:T(8,128)S(1)}, u32[]{:S(2)}, u32[]{:S(2)}) collective-permute-start(f32[4,16,128]{2,1,0:T(8,128)S(1)} %get-tuple-element.74), channel_id=1, source_target_pairs={{0,72},{64,136},{128,200},{192,8},{1,73},{65,137},{129,201},{193,9... | collective-permute-start | bytes 98312 | tf_op jit(solution)/shard_map/ppermute | solution.py:224

commit v7 on v6

--- a/solution.py
+++ b/solution.py
@@ -17,7 +17,7 @@
 NN = (((1,), (0,)), ((), ()))
 NT = (((1,), (1,)), ((), ()))
 TN = (((0,), (0,)), ((), ()))
-NEAR = ("x", "zp")
+SEQ = ("x", "zb", "zp", "c")
 
 
 def halves(wide):
@@ -99,6 +99,10 @@
             third_ref[member // each, pl.ds(member % each * rows, rows), :] = pieces_ref[x, place]
     third_ref[HEADS : 2 * HEADS] = prefix_ref[...]
     third_ref[2 * HEADS :] = grad_ref[...]
+
+
+def slots(place_size):
+    return (1, 0) + tuple(range(2, place_size))
 
 
 def prefix_kernel(backward, steps, place_size, source, at_ref, pieces_ref, *refs):
@@ -116,9 +120,10 @@
             row = row + total
             so_far = so_far + jnp.where(other > block if backward else other < block, total, 0.0)
         for place in range(place_size)[:: -1 if backward else 1]:
-            member = x * place_size + place
+            slot = slots(place_size)[place]
+            member = x * place_size + slot
             piece = pieces_ref[source, member // each, pl.ds(member % each * rows, rows), :]
-            out_ref[x, place] = so_far
+            out_ref[x, slot] = so_far
             so_far = so_far + piece
             row = row + piece
         base = row
@@ -156,40 +161,35 @@
         other_ref[head] = states[1]
 
 
-def backward_kernel(at_ref, *refs):
-    q_ref, k_ref, v_ref, scores_ref, grad_ref, other_ref, first_ref, third_ref, last_ref = refs[:9]
-    dq_out, dk_out, dv_out, dq_ref, dk_ref, dv_ref, sems = refs[9:]
+def inner_kernel(at_ref, *refs):
+    q_ref, k_ref, v_ref, scores_ref, grad_ref, first_ref, third_ref, dq_ref, dk_ref, dv_ref = refs
     mask = causal(q_ref.shape[0])
     late = core_of(at_ref) == 1
-    copies = []
-
-    def write(start, end):
-        copies.append(pltpu.make_async_copy(start, end, sems.at[len(copies)]))
-        copies[-1].start()
-
-    heads = range(HEADS)
-    grads = [halves(jnp.where(late, third_ref[0, 2 * HEADS + head], grad_ref[head])) for head in heads]
-    prefixes = [halves(third_ref[0, HEADS + head] + jnp.where(late, first_ref[0, head], 0.0)) for head in heads]
-    suffixes = [halves(last_ref[1, head] + jnp.where(late, 0.0, other_ref[head])) for head in heads]
-    keys = [halves(feature(k_ref[:, features_of(head)])) for head in heads]
-    grad_scores = []
-    for head in heads:
-        part = features_of(head)
-        grad_scores.append(halves(jnp.where(mask, product(grads[head], v_ref[:, part], NT), 0.0)))
-        dq = product(grad_scores[head], keys[head], NN) + product(grads[head], prefixes[head], NT)
-        dq_ref[:, part] = slope(q_ref[:, part]) * dq
-    write(dq_ref, dq_out)
-    for head in heads:
+    for head in range(HEADS):
         part = features_of(head)
         query = halves(feature(q_ref[:, part]))
-        dk = product(grad_scores[head], query, TN) + product(v_ref[:, part], suffixes[head], NT)
-        dk_ref[:, part] = slope(k_ref[:, part]) * dk
-    write(dk_ref, dk_out)
-    for head in heads:
-        part = features_of(head)
-        dv = product(halves(scores_ref[head]), grads[head], TN) + product(keys[head], suffixes[head], NN)
-        dv_ref[:, part] = dv
-    write(dv_ref, dv_out)
+        key = halves(feature(k_ref[:, part]))
+        grad = halves(jnp.where(late, third_ref[0, 2 * HEADS + head], grad_ref[head]))
+        prefix = halves(third_ref[0, HEADS + head] + jnp.where(late, first_ref[0, head], 0.0))
+        grad_scores = halves(jnp.where(mask, product(grad, v_ref[:, part], NT), 0.0))
+        dq_ref[:, part] = slope(q_ref[:, part]) * (product(grad_scores, key, NN) + product(grad, prefix, NT))
+        dk_ref[:, part] = product(grad_scores, query, TN)
+        dv_ref[:, part] = product(halves(scores_ref[head]), grad, TN)
+
+
+def backward_kernel(at_ref, k_ref, v_ref, near_dk_ref, near_dv_ref, other_ref, last_ref, dk_out, dv_out, dk_ref, dv_ref, sems):
+    late = core_of(at_ref) == 1
+    suffixes = [halves(last_ref[1, head] + jnp.where(late, 0.0, other_ref[head])) for head in range(HEADS)]
+    copies = [pltpu.make_async_copy(dk_ref, dk_out, sems.at[0]), pltpu.make_async_copy(dv_ref, dv_out, sems.at[1])]
+    for head in range(HEADS):
+        part = features_of(head)
+        raw = k_ref[:, part]
+        dk_ref[:, part] = slope(raw) * (near_dk_ref[:, part] + product(v_ref[:, part], suffixes[head], NT))
+    copies[0].start()
+    for head in range(HEADS):
+        part = features_of(head)
+        dv_ref[:, part] = near_dv_ref[:, part] + product(halves(feature(k_ref[:, part])), suffixes[head], NN)
+    copies[1].start()
     for copy in copies:
         copy.wait()
 
@@ -207,7 +207,7 @@
 
 def body(query, key, value, gain, grad_out):
     tokens = query.shape[0]
-    at = lax.axis_index(("x", "zb", "zp", "c")).reshape(1)
+    at = lax.axis_index(SEQ).reshape(1)
     core = lax.axis_index("c")
     blocks, x_size, place_size = lax.axis_size("zb"), lax.axis_size("x"), lax.axis_size("zp")
     members = x_size * place_size
@@ -216,8 +216,15 @@
     state, three, wide = (HEADS, HD, HD), (3 * HEADS, HD, HD), (tokens, HEADS * HD)
     steps = sorted(range(1, blocks), key=lambda step: min(step, blocks - step))
 
+    leading = sorted(range(place_size), key=lambda place: slots(place_size)[place])
+    groups = [
+        [((x * blocks + block) * place_size + place) * 2 + one_core for x in range(x_size) for place in leading]
+        for block in range(blocks)
+        for one_core in range(2)
+    ]
+
     def within(pieces, shape):
-        return lax.all_to_all(pieces.reshape(flat), NEAR, 0, 0).reshape(shape)
+        return lax.all_to_all(pieces.reshape(flat), SEQ, 0, 0, axis_index_groups=groups).reshape(shape)
 
     def to_blocks(total, source):
         ends = [(step, [(2 * block + source, 2 * ((block + step) % blocks) + 1 - source) for block in range(blocks)]) for step in steps]
@@ -260,22 +267,22 @@
     third, total, grad, other = lax.cond(core == 0, middle, none(three, far, state, state), firsts, seconds, totals)
     totals = to_blocks(total, 0)
     thirds = lax.all_gather(third, "c")
+    dq, dk, dv = call(inner_kernel, [(wide, F32)] * 3, at, q, k, v, scores, grad, firsts, thirds, scalars=1)
 
     def end(thirds, totals):
         return (sums(True, 0, thirds, totals),)
 
     (last,) = lax.cond(core == 1, end, none(state), thirds, totals)
     lasts = lax.all_gather(last, "c")
-    return tuple(
-        call(
-            backward_kernel,
-            [(wide, F32)] * 3,
-            *(at, q, k, v, scores, grad, other, firsts, thirds, lasts),
-            scalars=1,
-            outputs=HBM,
-            scratch=[pltpu.VMEM(wide, F32)] * 3 + [pltpu.SemaphoreType.DMA((3,))],
-        )
+    dk, dv = call(
+        backward_kernel,
+        [(wide, F32)] * 2,
+        *(at, k, v, dk, dv, other, lasts),
+        scalars=1,
+        outputs=HBM,
+        scratch=[pltpu.VMEM(wide, F32)] * 2 + [pltpu.SemaphoreType.DMA((2,))],
     )
+    return dq, dk, dv
 
 
 def over(devices):

time: 87 us -> 83.7 us (0.962)
  blocking collectives: 72.4 us -> 69.9 us
  waiting for transfers between devices: 2 us -> 0.46 us
  Pallas kernels: 3.31 us -> 4.29 us
    ppermute x6, waiting for transfers between devices: 2 us -> 0.46 us  [to_blocks(): return [lax.ppermute(total, ('zb', 'c'), pairs) for step, pairs in ends]]
    all_gather x1, blocking collectives: 32.4 us -> 31.2 us  [body(): thirds = lax.all_gather(third, 'c')]
    all_to_all x2, blocking collectives: 19.7 us -> 18.4 us  [within(): lax.all_to_all(pieces.reshape(flat), SEQ, 0, 0, axis_index_groups=groups)]
    pallas_call x5 -> x6, Pallas kernels: 3.31 us -> 4.29 us  [call(): pl.pallas_call(kernel, out_shape=[jax.ShapeDtypeStruct(shape, dtype) for...]
  transfers between devices with their start and end apart: 6 -> 6, of which waited for: 3 -> 1; matrix products, arithmetic and copies ran while one was open for 0% -> 0% of each run, Pallas kernels for 1% -> 3%
where the time goes in v7:
time: 83.7 us; the launch traced here: 83.3 us
  blocking collectives  69.9 us (84%)
  starting transfers between devices  7.75 us (9%)
  Pallas kernels  4.29 us (5%)
    all_gather x1, blocking collectives, body(): thirds = lax.all_gather(third, 'c')  31.2 us
    all_to_all x2, blocking collectives, within(): lax.all_to_all(pieces.reshape(flat), SEQ, 0, 0, axis_index_groups=groups)  18.4 us
    all_gather x1, blocking collectives, body(): firsts = lax.all_gather(first, 'c')  16 us
    ppermute x6, starting transfers between devices, to_blocks(): return [lax.ppermute(total, ('zb', 'c'), pairs) for step, pairs in ends]  7.75 us
    pallas_call x6, Pallas kernels, call(): pl.pallas_call(kernel, out_shape=[jax.ShapeDtypeStruct(shape, dtype) for...  4.29 us
    all_gather x1, blocking collectives, body(): seconds = lax.all_gather(second, 'c')  2.37 us
    all_gather x1, blocking collectives, body(): lasts = lax.all_gather(last, 'c')  1.98 us
  transfers between devices with their start and end apart: 6, of which 1 were waited for; matrix products, arithmetic and copies ran while one was open for 0% of the time, Pallas kernels for 3%

profile of v7, /device:TPU:1, one launch (start us, length us, event | category | flops | bytes accessed | tf_op | source)
XLA Modules:
  0.0 83.3 jit_solution(4159236317521505894)
XLA Ops:
  0.6 1.2 %shard_map.76 = (bf16[128,256]{1,0:T(8,128)(2,1)S(1)}, bf16[128,256]{1,0:T(8,128)(2,1)S(1)}, bf16[128,256]{1,0:T(8,128)(2,1)S(1)}, f32[4,128,128]{2,1,0:T(8,128)S(1)}) custom-call(s32[1]{0:T(128)} %bitcast.10.at_ref, bf16[128,256]{1,0:T(8,128)(2,1)} %k_in.1, bf16[128,256]{1,0:T(8,128)(2,1)} %v_in.1, bf16[128,256]{1,0:T(8,128)(2,1)} %q_in.1, ...), custom_call_target="tpu_custom_call" | custom-call | tf_op jit(solution)/shard_map/pallas_call | solution.py:198
  1.8 16.0 %all-gather = f32[8,128,128]{2,1,0:T(8,128)S(1)} all-gather(f32[4,128,128]{2,1,0:T(8,128)S(1)} %get-tuple-element.71), channel_id=2, replica_groups=mesh['x'=4,'zb'=4,'zp'=4,'c'=2,'h'=8] {'c'}, dimensions={0}, use_global_device_ids=true | all-gather | bytes 786432 | tf_op jit(solution)/shard_map/all_gather | solution.py:250
  17.8 9.0 %conditional.3 = (f32[4,16,128]{2,1,0:T(8,128)S(1)}, f32[2,128,128]{2,1,0:T(8,128)S(1)}) conditional(s32[]{:T(128)} %convert_element_type.7, () %tuple.32, f32[2,4,128,128]{3,2,1,0:T(8,128)S(1)} %bitcast.27), branch_computations={%region_0.0_spmd, %region_1.0_spmd} | conditional | flops 32768 | bytes 655376 | solution.py:256
  17.8 8.9 %all_to_all.16 = f32[16,16,128]{2,1,0:T(8,128)S(1)} all-to-all(f32[16,16,128]{2,1,0:T(8,128)S(1)} %bitcast.31), channel_id=1, replica_groups={{16,0,32,48,272,256,288,304,528,512,544,560,784,768,800,816},{24,8,40,5..., dimensions={0} | all-to-all | bytes 262144 | tf_op jit(solution)/shard_map/cond/branch_1_fun/all_to_all | solution.py:227
  26.8 1.3 %collective-permute-start.2 = (f32[4,16,128]{2,1,0:T(8,128)S(1)}, f32[4,16,128]{2,1,0:T(8,128)S(1)}, u32[]{:S(2)}, u32[]{:S(2)}) collective-permute-start(f32[4,16,128]{2,1,0:T(8,128)S(1)} %get-tuple-element.75), channel_id=1, source_target_pairs={{8,128},{72,192},{136,0},{200,64},{9,129},{73,193},{137,1},{201,65... | collective-permute-start | bytes 98312 | tf_op jit(solution)/shard_map/ppermute | solution.py:231
  28.1 1.3 %collective-permute-start.1 = (f32[4,16,128]{2,1,0:T(8,128)S(1)}, f32[4,16,128]{2,1,0:T(8,128)S(1)}, u32[]{:S(2)}, u32[]{:S(2)}) collective-permute-start(f32[4,16,128]{2,1,0:T(8,128)S(1)} %get-tuple-element.75), channel_id=1, source_target_pairs={{8,192},{72,0},{136,64},{200,128},{9,193},{73,1},{137,65},{201,129... | collective-permute-start | bytes 98312 | tf_op jit(solution)/shard_map/ppermute | solution.py:231
  29.4 1.3 %collective-permute-start = (f32[4,16,128]{2,1,0:T(8,128)S(1)}, f32[4,16,128]{2,1,0:T(8,128)S(1)}, u32[]{:S(2)}, u32[]{:S(2)}) collective-permute-start(f32[4,16,128]{2,1,0:T(8,128)S(1)} %get-tuple-element.75), channel_id=1, source_target_pairs={{8,64},{72,128},{136,192},{200,0},{9,65},{73,129},{137,193},{201,1... | collective-permute-start | bytes 98312 | tf_op jit(solution)/shard_map/ppermute | solution.py:231
  30.7 0.6 shard_map.77
  31.3 2.4 %all-gather.1 = f32[12,128,128]{2,1,0:T(8,128)S(1)} all-gather(f32[6,128,128]{2,1,0:T(8,128)S(1)} %get-tuple-element.74), channel_id=3, replica_groups=mesh['x'=4,'zb'=4,'zp'=4,'c'=2,'h'=8] {'c'}, dimensions={0}, use_global_device_ids=true | all-gather | bytes 1179648 | tf_op jit(solution)/shard_map/all_gather | solution.py:259
  33.7 0.0 collective-permute-done.2
  33.7 0.0 collective-permute-done.1
  33.7 0.0 collective-permute-done
  33.7 0.1 conditional.4
  33.8 1.3 %collective-permute-start.5 = (f32[4,16,128]{2,1,0:T(8,128)S(1)}, f32[4,16,128]{2,1,0:T(8,128)S(1)}, u32[]{:S(2)}, u32[]{:S(2)}) collective-permute-start(f32[4,16,128]{2,1,0:T(8,128)S(1)} %get-tuple-element.82), channel_id=1, source_target_pairs={{0,136},{64,200},{128,8},{192,72},{1,137},{65,201},{129,9},{193,73... | collective-permute-start | bytes 98312 | tf_op jit(solution)/shard_map/ppermute | solution.py:231
  35.1 1.3 %collective-permute-start.4 = (f32[4,16,128]{2,1,0:T(8,128)S(1)}, f32[4,16,128]{2,1,0:T(8,128)S(1)}, u32[]{:S(2)}, u32[]{:S(2)}) collective-permute-start(f32[4,16,128]{2,1,0:T(8,128)S(1)} %get-tuple-element.82), channel_id=1, source_target_pairs={{0,200},{64,8},{128,72},{192,136},{1,201},{65,9},{129,73},{193,137... | collective-permute-start | bytes 98312 | tf_op jit(solution)/shard_map/ppermute | solution.py:231
  36.4 1.3 %collective-permute-start.3 = (f32[4,16,128]{2,1,0:T(8,128)S(1)}, f32[4,16,128]{2,1,0:T(8,128)S(1)}, u32[]{:S(2)}, u32[]{:S(2)}) collective-permute-start(f32[4,16,128]{2,1,0:T(8,128)S(1)} %get-tuple-element.82), channel_id=1, source_target_pairs={{0,72},{64,136},{128,200},{192,8},{1,73},{65,137},{129,201},{193,9... | collective-permute-start | bytes 98312 | tf_op jit(solution)/shard_map/ppermute | solution.py:231
  37.7 31.2 %all-gather.2 = f32[12,128,128]{2,1,0:T(8,128)S(1)} all-gather(f32[6,128,128]{2,1,0:T(8,128)S(1)} %get-tuple-element.77), channel_id=4, replica_groups=mesh['x'=4,'zb'=4,'zp'=4,'c'=2,'h'=8] {'c'}, dimensions={0}, use_global_device_ids=true | all-gather | bytes 1179648 | tf_op jit(solution)/shard_map/all_gather | solution.py:269
  68.9 1.5 %shard_map.78 = (f32[128,256]{1,0:T(8,128)}, f32[128,256]{1,0:T(8,128)S(1)}, f32[128,256]{1,0:T(8,128)S(1)}) custom-call(s32[1]{0:T(128)} %bitcast.10.at_ref, bf16[128,256]{1,0:T(8,128)(2,1)S(1)} %get-tuple-element.68.q_ref.refs_0_, bf16[128,256]{1,0:T(8,128)(2,1)S(1)} %get-tuple-element.69.k_ref.refs_1_, ...), custom_call_target="tpu_custom_call" | custom-call | tf_op jit(solution)/shard_map/pallas_call | solution.py:198
  70.3 0.0 collective-permute-done.5
  70.3 0.4 collective-permute-done.4
  70.8 0.0 collective-permute-done.3
  70.8 9.5 %conditional.5 = (f32[2,128,128]{2,1,0:T(8,128)S(1)}) conditional(s32[]{:T(128)} %convert_element_type.7, () %tuple.35, (s32[1]{0:T(128)}, f32[2,6,128,128]{3,2,1,0:T(8,128)S(1)}, f32[4,16,128]{2,1,0:T(8,128)S(1)}, f32[4,16,128]{2,1,0:T(8,128)S(1)}, f32[4,16,128]{2,1,0:T(8,128)S(1)}) %tuple.44), branch_computations={%region_4.0_spmd, %region_5.0_spmd} | conditional | bytes 262152 | solution.py:275
  70.8 9.5 %all_to_all.19 = f32[16,16,128]{2,1,0:T(8,128)S(1)} all-to-all(f32[16,16,128]{2,1,0:T(8,128)S(1)} %bitcast.20), channel_id=1, replica_groups={{16,0,32,48,272,256,288,304,528,512,544,560,784,768,800,816},{24,8,40,5..., dimensions={0} | all-to-all | bytes 262144 | tf_op jit(solution)/shard_map/cond/branch_1_fun/all_to_all | solution.py:227
  80.3 2.0 %all-gather.3 = f32[4,128,128]{2,1,0:T(8,128)S(1)} all-gather(f32[2,128,128]{2,1,0:T(8,128)S(1)} %get-tuple-element.98), channel_id=5, replica_groups=mesh['x'=4,'zb'=4,'zp'=4,'c'=2,'h'=8] {'c'}, dimensions={0}, use_global_device_ids=true | all-gather | bytes 393216 | tf_op jit(solution)/shard_map/all_gather | solution.py:276
  82.3 1.0 %shard_map.79 = (f32[128,256]{1,0:T(8,128)}, f32[128,256]{1,0:T(8,128)}) custom-call(s32[1]{0:T(128)} %bitcast.10.at_ref, bf16[128,256]{1,0:T(8,128)(2,1)S(1)} %get-tuple-element.69.k_ref.refs_1_, bf16[128,256]{1,0:T(8,128)(2,1)S(1)} %get-tuple-element.70.v_ref.refs_2_, f32[128,256]{1,0:T(8,128)S(1)} %get-tuple-element.79.near_dk_ref, ...), custom_call_target="tpu_custom_call" | custom-call | tf_op jit(solution)/shard_map/pallas_call | solution.py:198
  (7 shorter events, 0.1 us)
Async XLA Ops:
  26.8 6.9 %collective-permute-start.2 = (f32[4,16,128]{2,1,0:T(8,128)S(1)}, f32[4,16,128]{2,1,0:T(8,128)S(1)}, u32[]{:S(2)}, u32[]{:S(2)}) collective-permute-start(f32[4,16,128]{2,1,0:T(8,128)S(1)} %get-tuple-element.75), channel_id=1, source_target_pairs={{8,128},{72,192},{136,0},{200,64},{9,129},{73,193},{137,1},{201,65... | collective-permute-start | bytes 98312 | tf_op jit(solution)/shard_map/ppermute | solution.py:231
  28.1 5.6 %collective-permute-start.1 = (f32[4,16,128]{2,1,0:T(8,128)S(1)}, f32[4,16,128]{2,1,0:T(8,128)S(1)}, u32[]{:S(2)}, u32[]{:S(2)}) collective-permute-start(f32[4,16,128]{2,1,0:T(8,128)S(1)} %get-tuple-element.75), channel_id=1, source_target_pairs={{8,192},{72,0},{136,64},{200,128},{9,193},{73,1},{137,65},{201,129... | collective-permute-start | bytes 98312 | tf_op jit(solution)/shard_map/ppermute | solution.py:231
  29.4 4.3 %collective-permute-start = (f32[4,16,128]{2,1,0:T(8,128)S(1)}, f32[4,16,128]{2,1,0:T(8,128)S(1)}, u32[]{:S(2)}, u32[]{:S(2)}) collective-permute-start(f32[4,16,128]{2,1,0:T(8,128)S(1)} %get-tuple-element.75), channel_id=1, source_target_pairs={{8,64},{72,128},{136,192},{200,0},{9,65},{73,129},{137,193},{201,1... | collective-permute-start | bytes 98312 | tf_op jit(solution)/shard_map/ppermute | solution.py:231
  33.8 36.5 %collective-permute-start.5 = (f32[4,16,128]{2,1,0:T(8,128)S(1)}, f32[4,16,128]{2,1,0:T(8,128)S(1)}, u32[]{:S(2)}, u32[]{:S(2)}) collective-permute-start(f32[4,16,128]{2,1,0:T(8,128)S(1)} %get-tuple-element.82), channel_id=1, source_target_pairs={{0,136},{64,200},{128,8},{192,72},{1,137},{65,201},{129,9},{193,73... | collective-permute-start | bytes 98312 | tf_op jit(solution)/shard_map/ppermute | solution.py:231
  35.1 35.7 %collective-permute-start.4 = (f32[4,16,128]{2,1,0:T(8,128)S(1)}, f32[4,16,128]{2,1,0:T(8,128)S(1)}, u32[]{:S(2)}, u32[]{:S(2)}) collective-permute-start(f32[4,16,128]{2,1,0:T(8,128)S(1)} %get-tuple-element.82), channel_id=1, source_target_pairs={{0,200},{64,8},{128,72},{192,136},{1,201},{65,9},{129,73},{193,137... | collective-permute-start | bytes 98312 | tf_op jit(solution)/shard_map/ppermute | solution.py:231
  36.4 34.4 %collective-permute-start.3 = (f32[4,16,128]{2,1,0:T(8,128)S(1)}, f32[4,16,128]{2,1,0:T(8,128)S(1)}, u32[]{:S(2)}, u32[]{:S(2)}) collective-permute-start(f32[4,16,128]{2,1,0:T(8,128)S(1)} %get-tuple-element.82), channel_id=1, source_target_pairs={{0,72},{64,136},{128,200},{192,8},{1,73},{65,137},{129,201},{193,9... | collective-permute-start | bytes 98312 | tf_op jit(solution)/shard_map/ppermute | solution.py:231

commit v8 on v7

--- a/solution.py
+++ b/solution.py
@@ -129,40 +129,45 @@
         base = row
 
 
-def scores_kernel(q_ref, k_ref, v_ref, pieces_ref, scores_ref, second_ref):
+def scores_kernel(at_ref, q_ref, k_ref, v_ref, pieces_ref, first_ref, scores_ref, second_ref):
     mask = causal(q_ref.shape[0])
+    late = core_of(at_ref) == 1
     second_ref[:HEADS] = pieces_ref[...]
     for head in range(HEADS):
         part = features_of(head)
-        query = halves(feature(q_ref[:, part]))
+        wide = feature(q_ref[:, part])
+        query = halves(wide)
         key = halves(feature(k_ref[:, part]))
         scores = jnp.where(mask, product(query, key, NT), 0.0)
         scores_ref[head] = scores
-        second_ref[HEADS + head] = product(halves(scores), v_ref[:, part], NN)
-        second_ref[2 * HEADS + head] = q_ref[:, part].astype(F32)
-
-
-def forward_kernel(first_ref, second_ref, prefix_ref, grad0_ref, grad1_ref, chip_ref, other_ref):
-    for head in range(HEADS):
-        states = []
-        for core in range(2):
-            query = halves(feature(second_ref[core, 2 * HEADS + head]))
-            prefix = prefix_ref[head]
-            if core:
-                prefix = prefix + first_ref[0, head]
-            output = second_ref[core, HEADS + head] + product(query, halves(prefix), NN)
-            inverse = lax.rsqrt(jnp.mean(output * output, axis=-1, keepdims=True) + 1e-06)
-            normed = output * inverse
-            scaled = first_ref[core, HEADS + head]
-            grad = inverse * (scaled - normed * jnp.mean(scaled * normed, axis=-1, keepdims=True))
-            (grad0_ref, grad1_ref)[core][head] = grad
-            states.append(product(query, halves(grad), TN))
-        chip_ref[head] = states[0] + states[1]
-        other_ref[head] = states[1]
+        before = halves(jnp.where(late, first_ref[0, head], 0.0))
+        second_ref[HEADS + head] = product(halves(scores), v_ref[:, part], NN) + product(query, before, NN)
+        second_ref[2 * HEADS + head] = wide
+
+
+def split_kernel(second_ref, high_ref, low_ref, high_t_ref, low_t_ref):
+    for head in range(HEADS):
+        wide = second_ref[:, 2 * HEADS + head].reshape(2 * HD, HD)
+        high_ref[head], low_ref[head] = halves(wide)
+        high_t_ref[head], low_t_ref[head] = halves(wide.T)
+
+
+def forward_kernel(first_ref, second_ref, high_ref, low_ref, high_t_ref, low_t_ref, prefix_ref, grad0_ref, grad1_ref, chip_ref):
+    for head in range(HEADS):
+        rows = (2 * HD, HD)
+        query = high_ref[head], low_ref[head]
+        output = second_ref[:, HEADS + head].reshape(rows) + product(query, halves(prefix_ref[head]), NN)
+        inverse = lax.rsqrt(jnp.mean(output * output, axis=-1, keepdims=True) + 1e-06)
+        normed = output * inverse
+        scaled = first_ref[:, HEADS + head].reshape(rows)
+        grad = inverse * (scaled - normed * jnp.mean(scaled * normed, axis=-1, keepdims=True))
+        chip_ref[head] = product((high_t_ref[head], low_t_ref[head]), halves(grad), NN)
+        grad0_ref[head] = grad[:HD]
+        grad1_ref[head] = grad[HD:]
 
 
 def inner_kernel(at_ref, *refs):
-    q_ref, k_ref, v_ref, scores_ref, grad_ref, first_ref, third_ref, dq_ref, dk_ref, dv_ref = refs
+    q_ref, k_ref, v_ref, scores_ref, grad_ref, first_ref, second_ref, third_ref, dq_ref, dk_ref, dv_ref, other_ref = refs
     mask = causal(q_ref.shape[0])
     late = core_of(at_ref) == 1
     for head in range(HEADS):
@@ -175,6 +180,8 @@
         dq_ref[:, part] = slope(q_ref[:, part]) * (product(grad_scores, key, NN) + product(grad, prefix, NT))
         dk_ref[:, part] = product(grad_scores, query, TN)
         dv_ref[:, part] = product(halves(scores_ref[head]), grad, TN)
+        later = halves(second_ref[1, 2 * HEADS + head]), halves(third_ref[0, 2 * HEADS + head])
+        other_ref[head] = product(*later, TN)
 
 
 def backward_kernel(at_ref, k_ref, v_ref, near_dk_ref, near_dv_ref, other_ref, last_ref, dk_out, dv_out, dk_ref, dv_ref, sems):
@@ -255,19 +262,22 @@
 
     pieces, total = lax.cond(core == 1, start, none(near, far), firsts)
     totals = to_blocks(total, 1)
-    scores, second = call(scores_kernel, [(state, F32), (three, F32)], q, k, v, pieces.reshape(state))
+    scores, second = call(scores_kernel, [(state, F32), (three, F32)], at, q, k, v, pieces.reshape(state), firsts, scalars=1)
     seconds = lax.all_gather(second, "c")
-
-    def middle(firsts, seconds, totals):
+    tall, flat_t = ((HEADS, 2 * tokens, HD), BF16), ((HEADS, HD, 2 * tokens), BF16)
+    queries = call(split_kernel, [tall, tall, flat_t, flat_t], seconds)
+
+    def middle(firsts, seconds, queries, totals):
         prefix = sums(False, 1, seconds, totals)
-        grad0, grad1, chip, other = call(forward_kernel, [(state, F32)] * 4, firsts, seconds, prefix)
+        grad0, grad1, chip = call(forward_kernel, [(state, F32)] * 3, firsts, seconds, *queries, prefix)
         third, total = call(total_and_pack_kernel, [(three, F32), (far, F32)], within(chip, near), prefix, grad1)
-        return third, total, grad0, other
-
-    third, total, grad, other = lax.cond(core == 0, middle, none(three, far, state, state), firsts, seconds, totals)
+        return third, total, grad0
+
+    third, total, grad = lax.cond(core == 0, middle, none(three, far, state), firsts, seconds, queries, totals)
     totals = to_blocks(total, 0)
     thirds = lax.all_gather(third, "c")
-    dq, dk, dv = call(inner_kernel, [(wide, F32)] * 3, at, q, k, v, scores, grad, firsts, thirds, scalars=1)
+    outs = [(wide, F32)] * 3 + [(state, F32)]
+    dq, dk, dv, other = call(inner_kernel, outs, at, q, k, v, scores, grad, firsts, seconds, thirds, scalars=1)
 
     def end(thirds, totals):
         return (sums(True, 0, thirds, totals),)

time: 83.7 us -> 83.6 us (level)
    pallas_call x6 -> x7, Pallas kernels: 4.29 us -> 4.52 us  [call(): pl.pallas_call(kernel, out_shape=[jax.ShapeDtypeStruct(shape, dtype) for...]
where the time goes in v8:
time: 83.6 us; the launch traced here: 83.2 us
  blocking collectives  69.6 us (83%)
  starting transfers between devices  7.75 us (9%)
  Pallas kernels  4.52 us (5%)
    all_gather x1, blocking collectives, body(): thirds = lax.all_gather(third, 'c')  30.9 us
    all_to_all x2, blocking collectives, within(): lax.all_to_all(pieces.reshape(flat), SEQ, 0, 0, axis_index_groups=groups)  18.4 us
    all_gather x1, blocking collectives, body(): firsts = lax.all_gather(first, 'c')  16 us
    ppermute x6, starting transfers between devices, to_blocks(): return [lax.ppermute(total, ('zb', 'c'), pairs) for step, pairs in ends]  7.75 us
    pallas_call x7, Pallas kernels, call(): pl.pallas_call(kernel, out_shape=[jax.ShapeDtypeStruct(shape, dtype) for...  4.52 us
    all_gather x1, blocking collectives, body(): seconds = lax.all_gather(second, 'c')  2.37 us
    all_gather x1, blocking collectives, body(): lasts = lax.all_gather(last, 'c')  1.98 us
  transfers between devices with their start and end apart: 6, of which 1 were waited for; matrix products, arithmetic and copies ran while one was open for 0% of the time, Pallas kernels for 3%

profile of v8, /device:TPU:1, one launch (start us, length us, event | category | flops | bytes accessed | tf_op | source)
XLA Modules:
  0.0 83.2 jit_solution(12519974254928129599)
XLA Ops:
  0.6 1.2 %shard_map.76 = (bf16[128,256]{1,0:T(8,128)(2,1)S(1)}, bf16[128,256]{1,0:T(8,128)(2,1)S(1)}, bf16[128,256]{1,0:T(8,128)(2,1)S(1)}, f32[4,128,128]{2,1,0:T(8,128)S(1)}) custom-call(s32[1]{0:T(128)} %bitcast.9.at_ref, bf16[128,256]{1,0:T(8,128)(2,1)} %k_in.1, bf16[128,256]{1,0:T(8,128)(2,1)} %v_in.1, bf16[128,256]{1,0:T(8,128)(2,1)} %q_in.1, ...), custom_call_target="tpu_custom_call" | custom-call | tf_op jit(solution)/shard_map/pallas_call | solution.py:205
  1.8 16.0 %all-gather = f32[8,128,128]{2,1,0:T(8,128)S(1)} all-gather(f32[4,128,128]{2,1,0:T(8,128)S(1)} %get-tuple-element.86), channel_id=2, replica_groups=mesh['x'=4,'zb'=4,'zp'=4,'c'=2,'h'=8] {'c'}, dimensions={0}, use_global_device_ids=true | all-gather | bytes 786432 | tf_op jit(solution)/shard_map/all_gather | solution.py:257
  17.8 9.0 %conditional.3 = (f32[4,16,128]{2,1,0:T(8,128)S(1)}, f32[2,128,128]{2,1,0:T(8,128)S(1)}) conditional(s32[]{:T(128)} %convert_element_type.7, () %tuple.32, f32[2,4,128,128]{3,2,1,0:T(8,128)S(1)} %bitcast.26), branch_computations={%region_0.0_spmd, %region_1.0_spmd} | conditional | flops 32768 | bytes 655376 | solution.py:263
  17.8 8.9 %all_to_all.16 = f32[16,16,128]{2,1,0:T(8,128)S(1)} all-to-all(f32[16,16,128]{2,1,0:T(8,128)S(1)} %bitcast.33), channel_id=1, replica_groups={{16,0,32,48,272,256,288,304,528,512,544,560,784,768,800,816},{24,8,40,5..., dimensions={0} | all-to-all | bytes 262144 | tf_op jit(solution)/shard_map/cond/branch_1_fun/all_to_all | solution.py:234
  26.8 1.3 %collective-permute-start.2 = (f32[4,16,128]{2,1,0:T(8,128)S(1)}, f32[4,16,128]{2,1,0:T(8,128)S(1)}, u32[]{:S(2)}, u32[]{:S(2)}) collective-permute-start(f32[4,16,128]{2,1,0:T(8,128)S(1)} %get-tuple-element.90), channel_id=1, source_target_pairs={{8,128},{72,192},{136,0},{200,64},{9,129},{73,193},{137,1},{201,65... | collective-permute-start | bytes 98312 | tf_op jit(solution)/shard_map/ppermute | solution.py:238
  28.1 1.3 %collective-permute-start.1 = (f32[4,16,128]{2,1,0:T(8,128)S(1)}, f32[4,16,128]{2,1,0:T(8,128)S(1)}, u32[]{:S(2)}, u32[]{:S(2)}) collective-permute-start(f32[4,16,128]{2,1,0:T(8,128)S(1)} %get-tuple-element.90), channel_id=1, source_target_pairs={{8,192},{72,0},{136,64},{200,128},{9,193},{73,1},{137,65},{201,129... | collective-permute-start | bytes 98312 | tf_op jit(solution)/shard_map/ppermute | solution.py:238
  29.4 1.3 %collective-permute-start = (f32[4,16,128]{2,1,0:T(8,128)S(1)}, f32[4,16,128]{2,1,0:T(8,128)S(1)}, u32[]{:S(2)}, u32[]{:S(2)}) collective-permute-start(f32[4,16,128]{2,1,0:T(8,128)S(1)} %get-tuple-element.90), channel_id=1, source_target_pairs={{8,64},{72,128},{136,192},{200,0},{9,65},{73,129},{137,193},{201,1... | collective-permute-start | bytes 98312 | tf_op jit(solution)/shard_map/ppermute | solution.py:238
  30.7 0.7 shard_map.77
  31.4 2.4 %all-gather.1 = f32[12,128,128]{2,1,0:T(8,128)S(1)} all-gather(f32[6,128,128]{2,1,0:T(8,128)S(1)} %get-tuple-element.89), channel_id=3, replica_groups=mesh['x'=4,'zb'=4,'zp'=4,'c'=2,'h'=8] {'c'}, dimensions={0}, use_global_device_ids=true | all-gather | bytes 1179648 | tf_op jit(solution)/shard_map/all_gather | solution.py:266
  33.8 0.1 shard_map.78
  33.9 0.0 collective-permute-done.2
  33.9 0.0 collective-permute-done.1
  34.0 0.0 collective-permute-done
  34.0 0.1 conditional.4
  34.1 1.3 %collective-permute-start.5 = (f32[4,16,128]{2,1,0:T(8,128)S(1)}, f32[4,16,128]{2,1,0:T(8,128)S(1)}, u32[]{:S(2)}, u32[]{:S(2)}) collective-permute-start(f32[4,16,128]{2,1,0:T(8,128)S(1)} %get-tuple-element.101), channel_id=1, source_target_pairs={{0,136},{64,200},{128,8},{192,72},{1,137},{65,201},{129,9},{193,73... | collective-permute-start | bytes 98312 | tf_op jit(solution)/shard_map/ppermute | solution.py:238
  35.4 1.3 %collective-permute-start.4 = (f32[4,16,128]{2,1,0:T(8,128)S(1)}, f32[4,16,128]{2,1,0:T(8,128)S(1)}, u32[]{:S(2)}, u32[]{:S(2)}) collective-permute-start(f32[4,16,128]{2,1,0:T(8,128)S(1)} %get-tuple-element.101), channel_id=1, source_target_pairs={{0,200},{64,8},{128,72},{192,136},{1,201},{65,9},{129,73},{193,137... | collective-permute-start | bytes 98312 | tf_op jit(solution)/shard_map/ppermute | solution.py:238
  36.7 1.3 %collective-permute-start.3 = (f32[4,16,128]{2,1,0:T(8,128)S(1)}, f32[4,16,128]{2,1,0:T(8,128)S(1)}, u32[]{:S(2)}, u32[]{:S(2)}) collective-permute-start(f32[4,16,128]{2,1,0:T(8,128)S(1)} %get-tuple-element.101), channel_id=1, source_target_pairs={{0,72},{64,136},{128,200},{192,8},{1,73},{65,137},{129,201},{193,9... | collective-permute-start | bytes 98312 | tf_op jit(solution)/shard_map/ppermute | solution.py:238
  38.0 30.9 %all-gather.2 = f32[12,128,128]{2,1,0:T(8,128)S(1)} all-gather(f32[6,128,128]{2,1,0:T(8,128)S(1)} %get-tuple-element.96), channel_id=4, replica_groups=mesh['x'=4,'zb'=4,'zp'=4,'c'=2,'h'=8] {'c'}, dimensions={0}, use_global_device_ids=true | all-gather | bytes 1179648 | tf_op jit(solution)/shard_map/all_gather | solution.py:278
  68.8 1.5 %shard_map.79 = (f32[128,256]{1,0:T(8,128)}, f32[128,256]{1,0:T(8,128)S(1)}, f32[128,256]{1,0:T(8,128)S(1)}, f32[2,128,128]{2,1,0:T(8,128)S(1)}) custom-call(s32[1]{0:T(128)} %bitcast.9.at_ref, bf16[128,256]{1,0:T(8,128)(2,1)S(1)} %get-tuple-element.83.q_ref.refs_0_, bf16[128,256]{1,0:T(8,128)(2,1)S(1)} %get-tuple-element.84.k_ref.refs_1_, ...), custom_call_target="tpu_custom_call" | custom-call | tf_op jit(solution)/shard_map/pallas_call | solution.py:205
  70.3 0.0 collective-permute-done.5
  70.3 0.5 collective-permute-done.4
  70.8 0.0 collective-permute-done.3
  70.8 9.5 %conditional.5 = (f32[2,128,128]{2,1,0:T(8,128)S(1)}) conditional(s32[]{:T(128)} %convert_element_type.7, () %tuple.35, (s32[1]{0:T(128)}, f32[2,6,128,128]{3,2,1,0:T(8,128)S(1)}, f32[4,16,128]{2,1,0:T(8,128)S(1)}, f32[4,16,128]{2,1,0:T(8,128)S(1)}, f32[4,16,128]{2,1,0:T(8,128)S(1)}) %tuple.46), branch_computations={%region_4.0_spmd, %region_5.0_spmd} | conditional | bytes 262152 | solution.py:285
  70.8 9.5 %all_to_all.19 = f32[16,16,128]{2,1,0:T(8,128)S(1)} all-to-all(f32[16,16,128]{2,1,0:T(8,128)S(1)} %bitcast.20), channel_id=1, replica_groups={{16,0,32,48,272,256,288,304,528,512,544,560,784,768,800,816},{24,8,40,5..., dimensions={0} | all-to-all | bytes 262144 | tf_op jit(solution)/shard_map/cond/branch_1_fun/all_to_all | solution.py:234
  80.3 2.0 %all-gather.3 = f32[4,128,128]{2,1,0:T(8,128)S(1)} all-gather(f32[2,128,128]{2,1,0:T(8,128)S(1)} %get-tuple-element.114), channel_id=5, replica_groups=mesh['x'=4,'zb'=4,'zp'=4,'c'=2,'h'=8] {'c'}, dimensions={0}, use_global_device_ids=true | all-gather | bytes 393216 | tf_op jit(solution)/shard_map/all_gather | solution.py:286
  82.3 1.0 %shard_map.80 = (f32[128,256]{1,0:T(8,128)}, f32[128,256]{1,0:T(8,128)}) custom-call(s32[1]{0:T(128)} %bitcast.9.at_ref, bf16[128,256]{1,0:T(8,128)(2,1)S(1)} %get-tuple-element.84.k_ref.refs_1_, bf16[128,256]{1,0:T(8,128)(2,1)S(1)} %get-tuple-element.85.v_ref.refs_2_, f32[128,256]{1,0:T(8,128)S(1)} %get-tuple-element.98.near_dk_ref, ...), custom_call_target="tpu_custom_call" | custom-call | tf_op jit(solution)/shard_map/pallas_call | solution.py:205
  (6 shorter events, 0.1 us)
Async XLA Ops:
  26.8 7.2 %collective-permute-start.2 = (f32[4,16,128]{2,1,0:T(8,128)S(1)}, f32[4,16,128]{2,1,0:T(8,128)S(1)}, u32[]{:S(2)}, u32[]{:S(2)}) collective-permute-start(f32[4,16,128]{2,1,0:T(8,128)S(1)} %get-tuple-element.90), channel_id=1, source_target_pairs={{8,128},{72,192},{136,0},{200,64},{9,129},{73,193},{137,1},{201,65... | collective-permute-start | bytes 98312 | tf_op jit(solution)/shard_map/ppermute | solution.py:238
  28.1 5.9 %collective-permute-start.1 = (f32[4,16,128]{2,1,0:T(8,128)S(1)}, f32[4,16,128]{2,1,0:T(8,128)S(1)}, u32[]{:S(2)}, u32[]{:S(2)}) collective-permute-start(f32[4,16,128]{2,1,0:T(8,128)S(1)} %get-tuple-element.90), channel_id=1, source_target_pairs={{8,192},{72,0},{136,64},{200,128},{9,193},{73,1},{137,65},{201,129... | collective-permute-start | bytes 98312 | tf_op jit(solution)/shard_map/ppermute | solution.py:238
  29.4 4.6 %collective-permute-start = (f32[4,16,128]{2,1,0:T(8,128)S(1)}, f32[4,16,128]{2,1,0:T(8,128)S(1)}, u32[]{:S(2)}, u32[]{:S(2)}) collective-permute-start(f32[4,16,128]{2,1,0:T(8,128)S(1)} %get-tuple-element.90), channel_id=1, source_target_pairs={{8,64},{72,128},{136,192},{200,0},{9,65},{73,129},{137,193},{201,1... | collective-permute-start | bytes 98312 | tf_op jit(solution)/shard_map/ppermute | solution.py:238
  34.1 36.3 %collective-permute-start.5 = (f32[4,16,128]{2,1,0:T(8,128)S(1)}, f32[4,16,128]{2,1,0:T(8,128)S(1)}, u32[]{:S(2)}, u32[]{:S(2)}) collective-permute-start(f32[4,16,128]{2,1,0:T(8,128)S(1)} %get-tuple-element.101), channel_id=1, source_target_pairs={{0,136},{64,200},{128,8},{192,72},{1,137},{65,201},{129,9},{193,73... | collective-permute-start | bytes 98312 | tf_op jit(solution)/shard_map/ppermute | solution.py:238
  35.4 35.4 %collective-permute-start.4 = (f32[4,16,128]{2,1,0:T(8,128)S(1)}, f32[4,16,128]{2,1,0:T(8,128)S(1)}, u32[]{:S(2)}, u32[]{:S(2)}) collective-permute-start(f32[4,16,128]{2,1,0:T(8,128)S(1)} %get-tuple-element.101), channel_id=1, source_target_pairs={{0,200},{64,8},{128,72},{192,136},{1,201},{65,9},{129,73},{193,137... | collective-permute-start | bytes 98312 | tf_op jit(solution)/shard_map/ppermute | solution.py:238
  36.7 34.1 %collective-permute-start.3 = (f32[4,16,128]{2,1,0:T(8,128)S(1)}, f32[4,16,128]{2,1,0:T(8,128)S(1)}, u32[]{:S(2)}, u32[]{:S(2)}) collective-permute-start(f32[4,16,128]{2,1,0:T(8,128)S(1)} %get-tuple-element.101), channel_id=1, source_target_pairs={{0,72},{64,136},{128,200},{192,8},{1,73},{65,137},{129,201},{193,9... | collective-permute-start | bytes 98312 | tf_op jit(solution)/shard_map/ppermute | solution.py:238

commit v9 on v8

--- a/solution.py
+++ b/solution.py
@@ -158,9 +158,9 @@
         query = high_ref[head], low_ref[head]
         output = second_ref[:, HEADS + head].reshape(rows) + product(query, halves(prefix_ref[head]), NN)
         inverse = lax.rsqrt(jnp.mean(output * output, axis=-1, keepdims=True) + 1e-06)
-        normed = output * inverse
         scaled = first_ref[:, HEADS + head].reshape(rows)
-        grad = inverse * (scaled - normed * jnp.mean(scaled * normed, axis=-1, keepdims=True))
+        shared = jnp.mean(scaled * output, axis=-1, keepdims=True)
+        grad = inverse * (scaled - output * (inverse * inverse * shared))
         chip_ref[head] = product((high_t_ref[head], low_t_ref[head]), halves(grad), NN)
         grad0_ref[head] = grad[:HD]
         grad1_ref[head] = grad[HD:]

time: 83.6 us -> 83.6 us (level)
  no operation moved by 1% of the time
where the time goes in v9:
time: 83.6 us; the launch traced here: 83.2 us
  blocking collectives  69.5 us (83%)
  starting transfers between devices  7.75 us (9%)
  Pallas kernels  4.52 us (5%)
    all_gather x1, blocking collectives, body(): thirds = lax.all_gather(third, 'c')  30.8 us
    all_to_all x2, blocking collectives, within(): lax.all_to_all(pieces.reshape(flat), SEQ, 0, 0, axis_index_groups=groups)  18.4 us
    all_gather x1, blocking collectives, body(): firsts = lax.all_gather(first, 'c')  16 us
    ppermute x6, starting transfers between devices, to_blocks(): return [lax.ppermute(total, ('zb', 'c'), pairs) for step, pairs in ends]  7.75 us
    pallas_call x7, Pallas kernels, call(): pl.pallas_call(kernel, out_shape=[jax.ShapeDtypeStruct(shape, dtype) for...  4.52 us
    all_gather x1, blocking collectives, body(): seconds = lax.all_gather(second, 'c')  2.37 us
    all_gather x1, blocking collectives, body(): lasts = lax.all_gather(last, 'c')  1.98 us
  transfers between devices with their start and end apart: 6, of which 1 were waited for; matrix products, arithmetic and copies ran while one was open for 0% of the time, Pallas kernels for 3%

profile of v9, /device:TPU:1, one launch (start us, length us, event | category | flops | bytes accessed | tf_op | source)
XLA Modules:
  0.0 83.2 jit_solution(6708701818727859987)
XLA Ops:
  0.6 1.2 %shard_map.76 = (bf16[128,256]{1,0:T(8,128)(2,1)S(1)}, bf16[128,256]{1,0:T(8,128)(2,1)S(1)}, bf16[128,256]{1,0:T(8,128)(2,1)S(1)}, f32[4,128,128]{2,1,0:T(8,128)S(1)}) custom-call(s32[1]{0:T(128)} %bitcast.9.at_ref, bf16[128,256]{1,0:T(8,128)(2,1)} %k_in.1, bf16[128,256]{1,0:T(8,128)(2,1)} %v_in.1, bf16[128,256]{1,0:T(8,128)(2,1)} %q_in.1, ...), custom_call_target="tpu_custom_call" | custom-call | tf_op jit(solution)/shard_map/pallas_call | solution.py:205
  1.8 16.0 %all-gather = f32[8,128,128]{2,1,0:T(8,128)S(1)} all-gather(f32[4,128,128]{2,1,0:T(8,128)S(1)} %get-tuple-element.86), channel_id=2, replica_groups=mesh['x'=4,'zb'=4,'zp'=4,'c'=2,'h'=8] {'c'}, dimensions={0}, use_global_device_ids=true | all-gather | bytes 786432 | tf_op jit(solution)/shard_map/all_gather | solution.py:257
  17.8 9.0 %conditional.3 = (f32[4,16,128]{2,1,0:T(8,128)S(1)}, f32[2,128,128]{2,1,0:T(8,128)S(1)}) conditional(s32[]{:T(128)} %convert_element_type.7, () %tuple.32, f32[2,4,128,128]{3,2,1,0:T(8,128)S(1)} %bitcast.26), branch_computations={%region_0.0_spmd, %region_1.0_spmd} | conditional | flops 32768 | bytes 655376 | solution.py:263
  17.8 8.9 %all_to_all.16 = f32[16,16,128]{2,1,0:T(8,128)S(1)} all-to-all(f32[16,16,128]{2,1,0:T(8,128)S(1)} %bitcast.33), channel_id=1, replica_groups={{16,0,32,48,272,256,288,304,528,512,544,560,784,768,800,816},{24,8,40,5..., dimensions={0} | all-to-all | bytes 262144 | tf_op jit(solution)/shard_map/cond/branch_1_fun/all_to_all | solution.py:234
  26.8 1.3 %collective-permute-start.2 = (f32[4,16,128]{2,1,0:T(8,128)S(1)}, f32[4,16,128]{2,1,0:T(8,128)S(1)}, u32[]{:S(2)}, u32[]{:S(2)}) collective-permute-start(f32[4,16,128]{2,1,0:T(8,128)S(1)} %get-tuple-element.90), channel_id=1, source_target_pairs={{8,128},{72,192},{136,0},{200,64},{9,129},{73,193},{137,1},{201,65... | collective-permute-start | bytes 98312 | tf_op jit(solution)/shard_map/ppermute | solution.py:238
  28.1 1.3 %collective-permute-start.1 = (f32[4,16,128]{2,1,0:T(8,128)S(1)}, f32[4,16,128]{2,1,0:T(8,128)S(1)}, u32[]{:S(2)}, u32[]{:S(2)}) collective-permute-start(f32[4,16,128]{2,1,0:T(8,128)S(1)} %get-tuple-element.90), channel_id=1, source_target_pairs={{8,192},{72,0},{136,64},{200,128},{9,193},{73,1},{137,65},{201,129... | collective-permute-start | bytes 98312 | tf_op jit(solution)/shard_map/ppermute | solution.py:238
  29.4 1.3 %collective-permute-start = (f32[4,16,128]{2,1,0:T(8,128)S(1)}, f32[4,16,128]{2,1,0:T(8,128)S(1)}, u32[]{:S(2)}, u32[]{:S(2)}) collective-permute-start(f32[4,16,128]{2,1,0:T(8,128)S(1)} %get-tuple-element.90), channel_id=1, source_target_pairs={{8,64},{72,128},{136,192},{200,0},{9,65},{73,129},{137,193},{201,1... | collective-permute-start | bytes 98312 | tf_op jit(solution)/shard_map/ppermute | solution.py:238
  30.7 0.7 shard_map.77
  31.4 2.4 %all-gather.1 = f32[12,128,128]{2,1,0:T(8,128)S(1)} all-gather(f32[6,128,128]{2,1,0:T(8,128)S(1)} %get-tuple-element.89), channel_id=3, replica_groups=mesh['x'=4,'zb'=4,'zp'=4,'c'=2,'h'=8] {'c'}, dimensions={0}, use_global_device_ids=true | all-gather | bytes 1179648 | tf_op jit(solution)/shard_map/all_gather | solution.py:266
  33.8 0.1 shard_map.78
  33.9 0.0 collective-permute-done.2
  33.9 0.0 collective-permute-done.1
  34.0 0.0 collective-permute-done
  34.0 0.1 conditional.4
  34.1 1.3 %collective-permute-start.5 = (f32[4,16,128]{2,1,0:T(8,128)S(1)}, f32[4,16,128]{2,1,0:T(8,128)S(1)}, u32[]{:S(2)}, u32[]{:S(2)}) collective-permute-start(f32[4,16,128]{2,1,0:T(8,128)S(1)} %get-tuple-element.101), channel_id=1, source_target_pairs={{0,136},{64,200},{128,8},{192,72},{1,137},{65,201},{129,9},{193,73... | collective-permute-start | bytes 98312 | tf_op jit(solution)/shard_map/ppermute | solution.py:238
  35.4 1.3 %collective-permute-start.4 = (f32[4,16,128]{2,1,0:T(8,128)S(1)}, f32[4,16,128]{2,1,0:T(8,128)S(1)}, u32[]{:S(2)}, u32[]{:S(2)}) collective-permute-start(f32[4,16,128]{2,1,0:T(8,128)S(1)} %get-tuple-element.101), channel_id=1, source_target_pairs={{0,200},{64,8},{128,72},{192,136},{1,201},{65,9},{129,73},{193,137... | collective-permute-start | bytes 98312 | tf_op jit(solution)/shard_map/ppermute | solution.py:238
  36.7 1.3 %collective-permute-start.3 = (f32[4,16,128]{2,1,0:T(8,128)S(1)}, f32[4,16,128]{2,1,0:T(8,128)S(1)}, u32[]{:S(2)}, u32[]{:S(2)}) collective-permute-start(f32[4,16,128]{2,1,0:T(8,128)S(1)} %get-tuple-element.101), channel_id=1, source_target_pairs={{0,72},{64,136},{128,200},{192,8},{1,73},{65,137},{129,201},{193,9... | collective-permute-start | bytes 98312 | tf_op jit(solution)/shard_map/ppermute | solution.py:238
  38.0 30.8 %all-gather.2 = f32[12,128,128]{2,1,0:T(8,128)S(1)} all-gather(f32[6,128,128]{2,1,0:T(8,128)S(1)} %get-tuple-element.96), channel_id=4, replica_groups=mesh['x'=4,'zb'=4,'zp'=4,'c'=2,'h'=8] {'c'}, dimensions={0}, use_global_device_ids=true | all-gather | bytes 1179648 | tf_op jit(solution)/shard_map/all_gather | solution.py:278
  68.8 1.5 %shard_map.79 = (f32[128,256]{1,0:T(8,128)}, f32[128,256]{1,0:T(8,128)S(1)}, f32[128,256]{1,0:T(8,128)S(1)}, f32[2,128,128]{2,1,0:T(8,128)S(1)}) custom-call(s32[1]{0:T(128)} %bitcast.9.at_ref, bf16[128,256]{1,0:T(8,128)(2,1)S(1)} %get-tuple-element.83.q_ref.refs_0_, bf16[128,256]{1,0:T(8,128)(2,1)S(1)} %get-tuple-element.84.k_ref.refs_1_, ...), custom_call_target="tpu_custom_call" | custom-call | tf_op jit(solution)/shard_map/pallas_call | solution.py:205
  70.2 0.0 collective-permute-done.5
  70.2 0.5 collective-permute-done.4
  70.7 0.0 collective-permute-done.3
  70.7 9.5 %conditional.5 = (f32[2,128,128]{2,1,0:T(8,128)S(1)}) conditional(s32[]{:T(128)} %convert_element_type.7, () %tuple.35, (s32[1]{0:T(128)}, f32[2,6,128,128]{3,2,1,0:T(8,128)S(1)}, f32[4,16,128]{2,1,0:T(8,128)S(1)}, f32[4,16,128]{2,1,0:T(8,128)S(1)}, f32[4,16,128]{2,1,0:T(8,128)S(1)}) %tuple.46), branch_computations={%region_4.0_spmd, %region_5.0_spmd} | conditional | bytes 262152 | solution.py:285
  70.7 9.5 %all_to_all.19 = f32[16,16,128]{2,1,0:T(8,128)S(1)} all-to-all(f32[16,16,128]{2,1,0:T(8,128)S(1)} %bitcast.20), channel_id=1, replica_groups={{16,0,32,48,272,256,288,304,528,512,544,560,784,768,800,816},{24,8,40,5..., dimensions={0} | all-to-all | bytes 262144 | tf_op jit(solution)/shard_map/cond/branch_1_fun/all_to_all | solution.py:234
  80.2 2.0 %all-gather.3 = f32[4,128,128]{2,1,0:T(8,128)S(1)} all-gather(f32[2,128,128]{2,1,0:T(8,128)S(1)} %get-tuple-element.114), channel_id=5, replica_groups=mesh['x'=4,'zb'=4,'zp'=4,'c'=2,'h'=8] {'c'}, dimensions={0}, use_global_device_ids=true | all-gather | bytes 393216 | tf_op jit(solution)/shard_map/all_gather | solution.py:286
  82.2 1.0 %shard_map.80 = (f32[128,256]{1,0:T(8,128)}, f32[128,256]{1,0:T(8,128)}) custom-call(s32[1]{0:T(128)} %bitcast.9.at_ref, bf16[128,256]{1,0:T(8,128)(2,1)S(1)} %get-tuple-element.84.k_ref.refs_1_, bf16[128,256]{1,0:T(8,128)(2,1)S(1)} %get-tuple-element.85.v_ref.refs_2_, f32[128,256]{1,0:T(8,128)S(1)} %get-tuple-element.98.near_dk_ref, ...), custom_call_target="tpu_custom_call" | custom-call | tf_op jit(solution)/shard_map/pallas_call | solution.py:205
  (6 shorter events, 0.1 us)
Async XLA Ops:
  26.8 7.2 %collective-permute-start.2 = (f32[4,16,128]{2,1,0:T(8,128)S(1)}, f32[4,16,128]{2,1,0:T(8,128)S(1)}, u32[]{:S(2)}, u32[]{:S(2)}) collective-permute-start(f32[4,16,128]{2,1,0:T(8,128)S(1)} %get-tuple-element.90), channel_id=1, source_target_pairs={{8,128},{72,192},{136,0},{200,64},{9,129},{73,193},{137,1},{201,65... | collective-permute-start | bytes 98312 | tf_op jit(solution)/shard_map/ppermute | solution.py:238
  28.1 5.9 %collective-permute-start.1 = (f32[4,16,128]{2,1,0:T(8,128)S(1)}, f32[4,16,128]{2,1,0:T(8,128)S(1)}, u32[]{:S(2)}, u32[]{:S(2)}) collective-permute-start(f32[4,16,128]{2,1,0:T(8,128)S(1)} %get-tuple-element.90), channel_id=1, source_target_pairs={{8,192},{72,0},{136,64},{200,128},{9,193},{73,1},{137,65},{201,129... | collective-permute-start | bytes 98312 | tf_op jit(solution)/shard_map/ppermute | solution.py:238
  29.4 4.6 %collective-permute-start = (f32[4,16,128]{2,1,0:T(8,128)S(1)}, f32[4,16,128]{2,1,0:T(8,128)S(1)}, u32[]{:S(2)}, u32[]{:S(2)}) collective-permute-start(f32[4,16,128]{2,1,0:T(8,128)S(1)} %get-tuple-element.90), channel_id=1, source_target_pairs={{8,64},{72,128},{136,192},{200,0},{9,65},{73,129},{137,193},{201,1... | collective-permute-start | bytes 98312 | tf_op jit(solution)/shard_map/ppermute | solution.py:238
  34.1 36.2 %collective-permute-start.5 = (f32[4,16,128]{2,1,0:T(8,128)S(1)}, f32[4,16,128]{2,1,0:T(8,128)S(1)}, u32[]{:S(2)}, u32[]{:S(2)}) collective-permute-start(f32[4,16,128]{2,1,0:T(8,128)S(1)} %get-tuple-element.101), channel_id=1, source_target_pairs={{0,136},{64,200},{128,8},{192,72},{1,137},{65,201},{129,9},{193,73... | collective-permute-start | bytes 98312 | tf_op jit(solution)/shard_map/ppermute | solution.py:238
  35.4 35.3 %collective-permute-start.4 = (f32[4,16,128]{2,1,0:T(8,128)S(1)}, f32[4,16,128]{2,1,0:T(8,128)S(1)}, u32[]{:S(2)}, u32[]{:S(2)}) collective-permute-start(f32[4,16,128]{2,1,0:T(8,128)S(1)} %get-tuple-element.101), channel_id=1, source_target_pairs={{0,200},{64,8},{128,72},{192,136},{1,201},{65,9},{129,73},{193,137... | collective-permute-start | bytes 98312 | tf_op jit(solution)/shard_map/ppermute | solution.py:238
  36.7 34.0 %collective-permute-start.3 = (f32[4,16,128]{2,1,0:T(8,128)S(1)}, f32[4,16,128]{2,1,0:T(8,128)S(1)}, u32[]{:S(2)}, u32[]{:S(2)}) collective-permute-start(f32[4,16,128]{2,1,0:T(8,128)S(1)} %get-tuple-element.101), channel_id=1, source_target_pairs={{0,72},{64,136},{128,200},{192,8},{1,73},{65,137},{129,201},{193,9... | collective-permute-start | bytes 98312 | tf_op jit(solution)/shard_map/ppermute | solution.py:238
